TPU v7x, 32 devices: a whole 2x2x4 slice. The times are simulated.
32 devices in a mesh: dp: 8 (over z, x), mp: 4 (over y, core).
Axes of the slice: x: 2, y: 2, z: 4, core: 2. Of those that a mesh axis runs over, the one named last changes fastest.
Arguments:
- dense_values: float32 [4096, 13], P('dp'), may hold values from 0 to 14, as said below
- field_ids: int32 [26, 4, 4096], P(None, None, 'dp'), may hold values from 0 to 65535
- lengths: int32 [26, 4096], P(None, 'dp'), may hold values from 1 to 4, as said below
- labels: int32 [4096], P('dp'), may hold values 0 or 1
- num_embed: float32 [13, 16], replicated, may hold values from -6 to 6
- embed_table: float32 [16, 65536], P(None, 'dp'), may hold values from -6 to 6
- gate_weight: bfloat16 [2, 624, 624], P(None, 'mp'), may hold values from -0.25 to 0.25
- gate_bias: float32 [2, 624], P(None, 'mp'), may hold values from -3 to 3
- narrow_first: bfloat16 [400, 624], P('mp'), may hold values from -0.25 to 0.25
- narrow_rest: bfloat16 [2, 400, 400], P(None, 'mp'), may hold values from -0.3125 to 0.3125
- narrow_gain: float32 [3, 400], P(None, 'mp'), may hold values from 0.1 to 1.9
- narrow_shift: float32 [3, 400], P(None, 'mp'), may hold values from -3 to 3
- broad_first: bfloat16 [800, 624], P('mp'), may hold values from -0.25 to 0.25
- broad_rest: bfloat16 [800, 800], P('mp'), may hold values from -0.21875 to 0.21875
- broad_gain: float32 [2, 800], P(None, 'mp'), may hold values from 0.1 to 1.9
- broad_shift: float32 [2, 800], P(None, 'mp'), may hold values from -3 to 3
- joining_left: float32 [400], replicated, may hold values from -0.3125 to 0.3125
- joining_right: float32 [800], replicated, may hold values from -0.21875 to 0.21875
- joining_pair: float32 [50, 8, 16], replicated, may hold values from -0.15625 to 0.15625
- joining_bias: float32 [1], replicated, may hold values from -3 to 3
Outputs:
- logits: float32 [4096], P('dp')
- num_embed_grad: float32 [13, 16], replicated
- embed_table_grad: float32 [16, 65536], P(None, 'dp')
- gate_weight_grad: float32 [2, 624, 624], P(None, 'mp')
- gate_bias_grad: float32 [2, 624], P(None, 'mp')
- narrow_first_grad: float32 [400, 624], P('mp')
- narrow_rest_grad: float32 [2, 400, 400], P(None, 'mp')
- narrow_gain_grad: float32 [3, 400], P(None, 'mp')
- narrow_shift_grad: float32 [3, 400], P(None, 'mp')
- broad_first_grad: float32 [800, 624], P('mp')
- broad_rest_grad: float32 [800, 800], P('mp')
- broad_gain_grad: float32 [2, 800], P(None, 'mp')
- broad_shift_grad: float32 [2, 800], P(None, 'mp')
- joining_left_grad: float32 [400], replicated
- joining_right_grad: float32 [800], replicated
- joining_pair_grad: float32 [50, 8, 16], replicated
- joining_bias_grad: float32 [1], replicated
Inputs may be any that keep to these rules, and one draw needn't show every extreme that they name: `lengths`: slots at or past a bag's length hold padding ids that count for nothing. `dense_values`: numeric features are positive.
All inputs are finite; a program needn't handle non-finite values. No bound on the sum of `labels` on one device may be relied on, other than what follows from the above.
Results may differ from a plain program's by a relative error of at most 0.015.
The roundings to bfloat16 on the way count: a program that leaves them out, or rounds other values in their place, can miss the bound.
Values may be sent and summed in bfloat16 or wider, within the bound.
A program may use at most 320 MiB of HBM per device.

v0:
```python
import jax
import jax.numpy as jnp
from jax import lax
from jax.sharding import PartitionSpec as P


def layer_forward(inputs, weight, gain_row, shift_row, batch_size):
    hidden = lax.dot_general(
        inputs, weight, (((1,), (1,)), ((), ())), preferred_element_type=jnp.float32
    )
    total_sum, square_sum = lax.psum(
        (jnp.sum(hidden, axis=0), jnp.sum(hidden * hidden, axis=0)), "dp"
    )
    batch_mean = total_sum / batch_size
    batch_var = square_sum / batch_size - batch_mean * batch_mean
    inverse = lax.rsqrt(batch_var + 1e-05)
    normed = (hidden - batch_mean) * inverse
    shaped = gain_row * normed + shift_row
    active = jax.nn.silu(shaped).astype(jnp.bfloat16)
    return (lax.all_gather(active, "mp", axis=1, tiled=True), (normed, shaped, inverse))


def layer_backward(grad_out, inputs, weight, gain_row, saved, batch_size):
    normed, shaped, inverse = saved
    sigma = jax.nn.sigmoid(shaped)
    grad_shaped = grad_out * sigma * (1.0 + shaped * (1.0 - sigma))
    shift_grad, gain_grad = lax.psum(
        (jnp.sum(grad_shaped, axis=0), jnp.sum(grad_shaped * normed, axis=0)), "dp"
    )
    grad_hidden = (
        gain_row
        * inverse
        * (grad_shaped - shift_grad / batch_size - normed * gain_grad / batch_size)
    ).astype(jnp.bfloat16)
    weight_grad = lax.dot_general(
        grad_hidden, inputs, (((0,), (0,)), ((), ())), preferred_element_type=jnp.float32
    )
    weight_grad = lax.psum(weight_grad, "dp")
    partial_input = jnp.dot(grad_hidden, weight, preferred_element_type=jnp.float32)
    grad_input = lax.psum_scatter(partial_input, "mp", scatter_dimension=1, tiled=True)
    return (grad_input, weight_grad, gain_grad, shift_grad)


def run_stream(start_input, weights, gain_rows, shifts, batch_size):
    inputs_list = [start_input]
    saved_list = []
    for position in range(len(weights)):
        output, saved = layer_forward(
            inputs_list[-1], weights[position], gain_rows[position], shifts[position], batch_size
        )
        inputs_list.append(output)
        saved_list.append(saved)
    return (inputs_list, saved_list)


def back_stream(grad_out, inputs_list, saved_list, weights, gain_rows, batch_size):
    weight_grads = []
    gain_grads = []
    shift_grads = []
    for position in reversed(range(len(weights))):
        grad_out, weight_grad, gain_grad, shift_grad = layer_backward(
            grad_out,
            inputs_list[position],
            weights[position],
            gain_rows[position],
            saved_list[position],
            batch_size,
        )
        weight_grads.insert(0, weight_grad)
        gain_grads.insert(0, gain_grad)
        shift_grads.insert(0, shift_grad)
    return (grad_out, weight_grads, jnp.stack(gain_grads), jnp.stack(shift_grads))


def shards(
    dense_values,
    field_ids,
    lengths,
    labels,
    num_embed,
    embed_table,
    gate_weight,
    gate_bias,
    narrow_first,
    narrow_rest,
    narrow_gain,
    narrow_shift,
    broad_first,
    broad_rest,
    broad_gain,
    broad_shift,
    joining_left,
    joining_right,
    joining_pair,
    joining_bias,
):
    highest = lax.Precision.HIGHEST
    tok_rows = dense_values.shape[0]
    batch_size = float(tok_rows * lax.axis_size("dp"))
    cat_fields = field_ids.shape[0]
    bag_size = field_ids.shape[1]
    own_rows = embed_table.shape[1]
    width = embed_table.shape[0]
    numeric_cols = dense_values.shape[1] * width
    positions = lax.broadcasted_iota(jnp.int32, field_ids.shape, 1)
    live_mask = positions < lengths[:, None, :]
    whole_table = lax.all_gather(embed_table, "dp", axis=1, tiled=True)
    row_index = jnp.where(live_mask, field_ids, 0)
    running = jnp.zeros((width, cat_fields, tok_rows), jnp.float32)
    for position in range(bag_size):
        picked = whole_table[:, row_index[:, position, :]]
        running = running + jnp.where(live_mask[None, :, position, :], picked, 0.0)
    pooled = jnp.transpose(running, (2, 1, 0)).reshape(tok_rows, cat_fields * width)
    numeric = (dense_values[:, :, None] * num_embed[None, :, :]).reshape(tok_rows, numeric_cols)
    features = jnp.concatenate([numeric, pooled], axis=1).astype(jnp.bfloat16)
    local_cols = gate_weight.shape[1]
    start_col = lax.axis_index("mp") * local_cols
    feature_cols = lax.dynamic_slice_in_dim(features, start_col, local_cols, 1).astype(jnp.float32)
    gate_input = (
        jnp.einsum("bd,khd->kbh", features, gate_weight, preferred_element_type=jnp.float32)
        + gate_bias[:, None, :]
    )
    gate_value = 2.0 * jax.nn.sigmoid(gate_input)
    fields_part = (feature_cols[None, :, :] * gate_value).astype(jnp.bfloat16)
    fields = lax.all_gather(fields_part, "mp", axis=2, tiled=True)
    narrow_weights = [narrow_first, narrow_rest[0], narrow_rest[1]]
    broad_weights = [broad_first, broad_rest]
    narrow_inputs, narrow_saved = run_stream(
        fields[0], narrow_weights, narrow_gain, narrow_shift, batch_size
    )
    broad_inputs, broad_saved = run_stream(
        fields[1], broad_weights, broad_gain, broad_shift, batch_size
    )
    head_count = joining_pair.shape[0]
    first_flat = narrow_inputs[-1].astype(jnp.float32)
    second_flat = broad_inputs[-1].astype(jnp.float32)
    first_heads = first_flat.reshape(tok_rows, head_count, -1)
    second_heads = second_flat.reshape(tok_rows, head_count, -1)
    turned = jnp.einsum("bhi,hij->bhj", first_heads, joining_pair, precision=highest)
    linear_part = jnp.dot(first_flat, joining_left, precision=highest) + jnp.dot(
        second_flat, joining_right, precision=highest
    )
    logits = linear_part + jnp.sum(turned * second_heads, axis=(1, 2)) + joining_bias[0]
    grad_logit = jax.nn.sigmoid(logits) - labels.astype(jnp.float32)
    joining_left_grad = jnp.sum(first_flat * grad_logit[:, None], axis=0)
    joining_right_grad = jnp.sum(second_flat * grad_logit[:, None], axis=0)
    joining_pair_grad = jnp.einsum(
        "bhi,bhj->hij", first_heads * grad_logit[:, None, None], second_heads, precision=highest
    )
    joining_bias_grad = jnp.sum(grad_logit).reshape(1)
    back_turned = jnp.einsum("hij,bhj->bhi", joining_pair, second_heads, precision=highest).reshape(
        tok_rows, -1
    )
    grad_first = grad_logit[:, None] * (joining_left[None, :] + back_turned)
    grad_second = grad_logit[:, None] * (joining_right[None, :] + turned.reshape(tok_rows, -1))
    narrow_cols = narrow_first.shape[0]
    broad_cols = broad_first.shape[0]
    grad_first = lax.dynamic_slice_in_dim(
        grad_first, lax.axis_index("mp") * narrow_cols, narrow_cols, 1
    )
    grad_second = lax.dynamic_slice_in_dim(
        grad_second, lax.axis_index("mp") * broad_cols, broad_cols, 1
    )
    grad_fields_first, narrow_wgrads, narrow_gain_grad, narrow_shift_grad = back_stream(
        grad_first, narrow_inputs, narrow_saved, narrow_weights, narrow_gain, batch_size
    )
    grad_fields_second, broad_wgrads, broad_gain_grad, broad_shift_grad = back_stream(
        grad_second, broad_inputs, broad_saved, broad_weights, broad_gain, batch_size
    )
    grad_fields = jnp.stack([grad_fields_first, grad_fields_second])
    grad_gate = (
        grad_fields * feature_cols[None, :, :] * gate_value * (1.0 - 0.5 * gate_value)
    ).astype(jnp.bfloat16)
    gate_weight_grad = jnp.einsum(
        "bd,kbh->khd", features, grad_gate, preferred_element_type=jnp.float32
    )
    gate_bias_grad = jnp.sum(grad_gate.astype(jnp.float32), axis=1)
    partial_features = jnp.einsum(
        "kbh,khd->bd", grad_gate, gate_weight, preferred_element_type=jnp.float32
    )
    own_term = jnp.sum(grad_fields * gate_value, axis=0)
    own_slice = lax.dynamic_slice_in_dim(partial_features, start_col, local_cols, 1) + own_term
    partial_features = lax.dynamic_update_slice_in_dim(partial_features, own_slice, start_col, 1)
    grad_features = lax.psum(partial_features, "mp").astype(jnp.bfloat16)
    numeric_grad = grad_features[:, :numeric_cols].astype(jnp.float32).reshape(tok_rows, -1, width)
    num_embed_grad = jnp.sum(dense_values[:, :, None] * numeric_grad, axis=0)
    pooled_grad = grad_features[:, numeric_cols:]
    row_index = jnp.where(live_mask, field_ids, 0)
    values = pooled_grad.astype(jnp.float32).reshape(tok_rows, cat_fields, width)
    running = jnp.zeros((own_rows * lax.axis_size("dp"), width), jnp.float32)
    for position in range(bag_size):
        masked = jnp.where(live_mask[:, position, :].T[:, :, None], values, 0.0).reshape(-1, width)
        running = running + jax.ops.segment_sum(
            masked,
            row_index[:, position, :].T.reshape(-1),
            num_segments=own_rows * lax.axis_size("dp"),
        )
    embed_table_grad = lax.psum_scatter(
        running.T.astype(jnp.bfloat16), "dp", scatter_dimension=1, tiled=True
    ).astype(jnp.float32)
    (
        joining_left_grad,
        joining_right_grad,
        joining_pair_grad,
        joining_bias_grad,
        gate_weight_grad,
        gate_bias_grad,
        num_embed_grad,
    ) = lax.psum(
        (
            joining_left_grad,
            joining_right_grad,
            joining_pair_grad,
            joining_bias_grad,
            gate_weight_grad,
            gate_bias_grad,
            num_embed_grad,
        ),
        "dp",
    )
    narrow_first_grad = narrow_wgrads[0]
    narrow_rest_grad = jnp.stack([narrow_wgrads[1], narrow_wgrads[2]])
    broad_first_grad = broad_wgrads[0]
    broad_rest_grad = broad_wgrads[1]
    return (
        logits,
        num_embed_grad,
        embed_table_grad,
        gate_weight_grad,
        gate_bias_grad,
        narrow_first_grad,
        narrow_rest_grad,
        narrow_gain_grad,
        narrow_shift_grad,
        broad_first_grad,
        broad_rest_grad,
        broad_gain_grad,
        broad_shift_grad,
        joining_left_grad,
        joining_right_grad,
        joining_pair_grad,
        joining_bias_grad,
    )


def solution(mesh):
    placed = (
        P("dp", None),
        P(None, None, "dp"),
        P(None, "dp"),
        P("dp"),
        P(),
        P(None, "dp"),
        P(None, "mp", None),
        P(None, "mp"),
        P("mp", None),
        P(None, "mp", None),
        P(None, "mp"),
        P(None, "mp"),
        P("mp", None),
        P("mp", None),
        P(None, "mp"),
        P(None, "mp"),
        P(),
        P(),
        P(),
        P(),
    )
    return jax.shard_map(
        shards,
        mesh=mesh,
        in_specs=placed,
        out_specs=(
            P("dp"),
            P(),
            P(None, "dp"),
            P(None, "mp", None),
            P(None, "mp"),
            P("mp", None),
            P(None, "mp", None),
            P(None, "mp"),
            P(None, "mp"),
            P("mp", None),
            P("mp", None),
            P(None, "mp"),
            P(None, "mp"),
            P(),
            P(),
            P(),
            P(),
        ),
        check_vma=False,
    )
```

profile of v0, /device:TPU:0, one launch (start us, length us, event | category | flops | bytes accessed | tf_op | source)
XLA Modules:
  0.0 1911.6 jit_solution(6472268366988857508)
XLA Ops:
  11.7 639.9 %all-gather.6.cloned.1.call-done = f32[16,65536]{0,1:T(8,128)} async-done(((f32[16,8192]{0,1:T(8,128)}), f32[16,65536]{0,1:T(8,128)}) %all-gather.6.cloned.1.call-update) | async-done | bytes 4194320 | tf_op jit(solution)/shard_map/all_gather | solution.py:107
  651.7 54.9 %gather_fusion.3 = f32[13312,16]{1,0:T(8,128)} fusion(f32[16,65536]{0,1:T(8,128)} %all-gather.6.cloned.1.call-done, s32[13312]{0:T(1024)S(1)} %broadcast_clamp_fusion), kind=kCustom, calls=%fused_computation.3 | custom fusion | bytes 1757184 | tf_op jit(solution)/shard_map/gather | solution.py:111
  711.2 54.9 %gather_fusion.2 = f32[13312,16]{1,0:T(8,128)} fusion(f32[16,65536]{0,1:T(8,128)} %all-gather.6.cloned.1.call-done, s32[13312]{0:T(1024)S(1)} %broadcast_clamp_fusion.1), kind=kCustom, calls=%fused_computation.2 | custom fusion | bytes 1757184 | tf_op jit(solution)/shard_map/gather | solution.py:111
  770.8 54.9 %gather_fusion = f32[13312,16]{1,0:T(8,128)} fusion(f32[16,65536]{0,1:T(8,128)} %all-gather.6.cloned.1.call-done, s32[13312]{0:T(1024)S(1)} %broadcast_clamp_fusion.3), kind=kCustom, calls=%fused_computation | custom fusion | bytes 1757184 | tf_op jit(solution)/shard_map/gather | solution.py:111
  831.1 54.9 %gather_fusion.1 = f32[13312,16]{1,0:T(8,128)} fusion(f32[16,65536]{0,1:T(8,128)} %all-gather.6.cloned.1.call-done, s32[13312]{0:T(1024)S(1)} %broadcast_clamp_fusion.2), kind=kCustom, calls=%fused_computation.1 | custom fusion | bytes 1757184 | tf_op jit(solution)/shard_map/gather | solution.py:111
  907.4 7.9 all-gather.8.cloned.1.call-done
  921.7 21.4 %all-reduce.14 = (f32[100]{0:T(128)S(1)}, f32[100]{0:T(128)S(1)}) all-reduce(f32[100]{0:T(128)S(1)} %get-tuple-element.138, f32[100]{0:T(128)S(1)} %get-tuple-element.137), channel_id=1, replica_groups=mesh['dp'=8,'mp'=4] {'dp'}, use_global_device_ids=true, to_apply=%region_3.4 | all-reduce | flops 200 | bytes 1600 | tf_op jit(solution)/shard_map/psum | solution.py:11
  951.7 17.1 all-reduce.13
  976.3 9.1 all_gather.26
  987.8 19.2 %all-reduce.12 = (f32[100]{0:T(128)S(1)}, f32[100]{0:T(128)S(1)}, f32[200]{0:T(256)S(1)}, f32[200]{0:T(256)S(1)}) all-reduce(f32[100]{0:T(128)S(1)} %get-tuple-element.134, f32[100]{0:T(128)S(1)} %get-tuple-element.133, f32[200]{0:T(256)S(1)} %get-tuple-element.124, ...), channel_id=1, replica_groups=mesh['dp'=8,'mp'=4] {'dp'}, use_global_device_ids=true, to_apply=%region_11.12 | all-reduce | flops 600 | bytes 4800 | tf_op jit(solution)/shard_map/psum | solution.py:11
  1007.7 6.7 all-gather.2
  1016.4 8.9 all_gather.27
  1036.0 17.8 all-reduce.11
  1057.3 13.4 fusion
  1081.7 19.8 %all-reduce.10 = (f32[200]{0:T(256)}, f32[200]{0:T(256)}, f32[100]{0:T(128)}, f32[100]{0:T(128)}) all-reduce(f32[200]{0:T(256)} %get-tuple-element.122, f32[200]{0:T(256)} %get-tuple-element.121, f32[100]{0:T(128)} %get-tuple-element.130, f32[100]{0:T(128)} %get-tuple-element.129), channel_id=1, replica_groups=mesh['dp'=8,'mp'=4] {'dp'}, use_global_device_ids=true, to_apply=%region_39.40 | all-reduce | flops 600 | bytes 4800 | tf_op jit(solution)/shard_map/psum | solution.py:27
  1124.9 14.3 fusion.1
  1149.8 21.9 %all-reduce.9 = (f32[200]{0:T(256)S(1)}, f32[200]{0:T(256)S(1)}, f32[100]{0:T(128)}, f32[100]{0:T(128)}) all-reduce(f32[200]{0:T(256)S(1)} %get-tuple-element.120, f32[200]{0:T(256)S(1)} %get-tuple-element.119, f32[100]{0:T(128)S(1)} %get-tuple-element.128, f32[100]{0:T(128)S(1)} %get-tuple-element.127), channel_id=1, replica_groups=mesh['dp'=8,'mp'=4] {'dp'}, use_global_device_ids=true, to_apply=%region_44.45 | all-reduce | flops 600 | bytes 4800 | tf_op jit(solution)/shard_map/psum | solution.py:27
  1180.1 26.6 %fusion.84 = (f32[512,160]{0,1:T(8,128)}, f32[512,160]{0,1:T(8,128)}) fusion(f32[512,624]{0,1:T(8,128)S(1)} %fusion.98, f32[512,624]{0,1:T(8,128)} %fusion.73), kind=kCustom, calls=%all-reduce-scatter.4 | all-reduce-scatter fusion | flops 655361 | bytes 3211776
  1226.2 28.1 %all-reduce.21 = bf16[512,624]{0,1:T(8,128)(2,1)} all-reduce(f32[512,624]{0,1:T(8,128)S(1)} %dynamic_update_slice.3), channel_id=1, replica_groups=mesh['dp'=8,'mp'=4] {'mp'}, use_global_device_ids=true, to_apply=%region_47.48 | all-reduce | flops 319488 | bytes 1916928 | tf_op jit(solution)/shard_map/psum | solution.py:184
  1260.4 15.3 broadcast_select_fusion.3
  1275.8 320.5 %scatter_custom_fusion = f32[65536,16]{1,0:T(8,128)} fusion(s32[53248]{0:T(1024)} %bitcast.264, f32[13312,16]{1,0:T(8,128)} %get-tuple-element.188, f32[]{:T(128)} %constant.84, f32[13312,16]{1,0:T(8,128)} %get-tuple-element.189, f32[13312,16]{1,0:T(8,128)} %get-tuple-element.190, f32[13312,16]{1,0:T(8,128)} %get-tuple-element.187, f32[]{:T(128)} %constant.57.clone.1), kind=kCustom, calls=%fused_computation.5 | custom fusion | flops 3407872 | bytes 31458304 | tf_op jit(solution)/shard_map/add | solution.py:193
  1596.3 17.1 convert_bitcast_fusion
  1618.5 41.5 %all-reduce.8 = (f32[13,16]{1,0:T(8,128)}, f32[2,156]{1,0:T(2,128)}, f32[400]{0:T(512)}, f32[800]{0:T(1024)}, f32[50,8,16]{2,1,0:T(8,128)S(1)}, /*index=5*/f32[1]{0:T(128)}) all-reduce(f32[13,16]{1,0:T(8,128)S(1)} %reduce_sum.268, f32[2,156]{1,0:T(2,128)S(1)} %get-tuple-element.178, ...), channel_id=1, replica_groups=mesh['dp'=8,'mp'=4] {'dp'}, use_global_device_ids=true, to_apply=%region_49.50 | all-reduce | flops 8121 | bytes 64968 | tf_op jit(solution)/shard_map/psum | solution.py:209
  1665.6 232.1 %reduce-scatter.13.cloned.1.call-done = bf16[16,8192]{0,1:T(8,128)(2,1)} async-done(((bf16[16,65536]{0,1:T(8,128)(2,1)}), bf16[16,8192]{0,1:T(8,128)(2,1)}) %reduce-scatter.13.cloned.1.call-update) | async-done | bytes 262160 | tf_op jit(solution)/shard_map/reduce_scatter | solution.py:198
  (313 shorter events, 176.5 us)
Async XLA Ops:
  7.2 887.4 %copy-start = (bf16[2,156,624]{2,0,1:T(2,128)(2,1)S(1)}, bf16[2,156,624]{2,0,1:T(2,128)(2,1)}, u32[]{:S(2)}) copy-start(bf16[2,156,624]{2,0,1:T(2,128)(2,1)} %param.26) | copy-start | bytes 1168132
  7.2 644.4 %all-gather.6.cloned.1.call-start = ((), (), s32[]{:S(2)}) async-start(), calls=%async_computation.2 | async-start | bytes 37748736 | tf_op jit(solution)/shard_map/all_gather | solution.py:107
  11.1 904.2 %all-gather.8.cloned.1.call-start = ((), (), s32[]{:S(2)}) async-start(), calls=%async_computation.3 | async-start | bytes 1597440 | tf_op jit(solution)/shard_map/all_gather | solution.py:125
  11.5 883.1 %copy-start.8 = (bf16[512,208]{0,1:T(8,128)(2,1)}, bf16[512,208]{0,1:T(8,128)(2,1)S(1)}, u32[]{:S(2)}) copy-start(bf16[512,208]{0,1:T(8,128)(2,1)S(1)} %multiply_convert_fusion.1) | copy-start | bytes 638980
  11.6 879.9 %copy-start.17 = (pred[512,26]{0,1:T(8,128)(4,1)}, pred[512,26]{0,1:T(8,128)(4,1)S(1)}, u32[]{:S(2)}) copy-start(pred[512,26]{0,1:T(8,128)(4,1)S(1)} %get-tuple-element.207) | copy-start | bytes 39940
  11.6 879.9 %copy-start.19 = (pred[512,26]{0,1:T(8,128)(4,1)}, pred[512,26]{0,1:T(8,128)(4,1)S(1)}, u32[]{:S(2)}) copy-start(pred[512,26]{0,1:T(8,128)(4,1)S(1)} %get-tuple-element.206) | copy-start | bytes 39940
  11.6 879.9 %copy-start.21 = (pred[512,26]{0,1:T(8,128)(4,1)}, pred[512,26]{0,1:T(8,128)(4,1)S(1)}, u32[]{:S(2)}) copy-start(pred[512,26]{0,1:T(8,128)(4,1)S(1)} %get-tuple-element.205) | copy-start | bytes 39940
  11.6 879.9 %copy-start.22 = (pred[512,26]{0,1:T(8,128)(4,1)}, pred[512,26]{0,1:T(8,128)(4,1)S(1)}, u32[]{:S(2)}) copy-start(pred[512,26]{0,1:T(8,128)(4,1)S(1)} %get-tuple-element.204) | copy-start | bytes 39940
  897.1 251.2 %reduce-scatter.11.cloned.1.call-start = ((), (), s32[]{:S(2)}) async-start(), calls=%async_computation.4 | async-start | bytes 2048000 | tf_op jit(solution)/shard_map/reduce_scatter | solution.py:40
  907.3 108.9 %copy-start.35 = (f32[1,200]{1,0:T(1,128)}, f32[1,200]{1,0:T(1,128)S(1)}, u32[]{:S(2)}) copy-start(f32[1,200]{1,0:T(1,128)S(1)} %get-tuple-element.221) | copy-start | bytes 2404
  907.3 108.9 %copy-start.45 = (f32[1,200]{1,0:T(1,128)}, f32[1,200]{1,0:T(1,128)S(1)}, u32[]{:S(2)}) copy-start(f32[1,200]{1,0:T(1,128)S(1)} %get-tuple-element.223) | copy-start | bytes 2404
  907.4 100.2 %copy-start.54 = (f32[100]{0:T(128)}, f32[100]{0:T(128)S(1)}, u32[]{:S(2)}) copy-start(f32[100]{0:T(128)S(1)} %get-tuple-element.218) | copy-start | bytes 1204
  907.4 100.2 %copy-start.56 = (f32[100]{0:T(128)}, f32[100]{0:T(128)S(1)}, u32[]{:S(2)}) copy-start(f32[100]{0:T(128)S(1)} %get-tuple-element.242) | copy-start | bytes 1204
  943.1 83.7 %copy-start.43 = (f32[100]{0:T(128)}, f32[100]{0:T(128)S(1)}, u32[]{:S(2)}) copy-start(f32[100]{0:T(128)S(1)} %get-tuple-element.232) | copy-start | bytes 1204
  1029.8 81.7 %copy-start.20 = (pred[512,26]{0,1:T(8,128)(4,1)S(1)}, pred[512,26]{0,1:T(8,128)(4,1)}, u32[]{:S(2)}) copy-start(pred[512,26]{0,1:T(8,128)(4,1)} %copy-done.19) | copy-start | bytes 39940
  1029.8 82.4 %copy-start.18 = (pred[512,26]{0,1:T(8,128)(4,1)S(1)}, pred[512,26]{0,1:T(8,128)(4,1)}, u32[]{:S(2)}) copy-start(pred[512,26]{0,1:T(8,128)(4,1)} %copy-done.17) | copy-start | bytes 39940
  1071.5 4.7 collective-permute-start
  1106.9 553.9 %all-reduce.20.cloned.1.call-start = ((), (), s32[]{:S(2)}) async-start(), calls=%async_computation.6 | async-start | bytes 5447680 | tf_op jit(solution)/shard_map/psum | solution.py:209
  1139.2 6.5 collective-permute-start.1
  1207.4 8.8 collective-permute-start.2
  1212.0 5.4 collective-permute-start.3
  1275.7 622.0 %reduce-scatter.13.cloned.1.call-start = ((), (), s32[]{:S(2)}) async-start(), calls=%async_computation.5 | async-start | bytes 18874368 | tf_op jit(solution)/shard_map/reduce_scatter | solution.py:198
  1613.5 291.1 %copy-start.1 = (bf16[2,156,624]{2,0,1:T(2,128)(2,1)S(1)}, bf16[2,156,624]{2,0,1:T(2,128)(2,1)}, u32[]{:S(2)}) copy-start(bf16[2,156,624]{2,0,1:T(2,128)(2,1)} %param.26) | copy-start | bytes 1168132
  1660.8 242.9 %copy-start.13 = (f32[200,800]{1,0:T(8,128)S(1)}, f32[200,800]{1,0:T(8,128)}, u32[]{:S(2)}) copy-start(f32[200,800]{1,0:T(8,128)} %get-tuple-element.253) | copy-start | bytes 1920004
  (63 other events, 1301.5 us)
Sparse Core Ops, SparseCore 0:
  11.2 640.4 all-gather.5
  897.3 17.9 all-gather.7
  1107.0 28.2 reduce-scatter.10
  1275.8 117.3 all-reduce.19
  1613.7 283.9 reduce-scatter.12
where the time goes:
time: 1920 us; the launch traced here: 1910 us
  waiting for transfers between devices  880 us (46%)
  other arithmetic  387 us (20%)
  local copies, waits for them, and re-layouts  301 us (16%)
  blocking collectives  278 us (14%)
  matrix products  39 us (2%)
    all_gather x1, waiting for transfers between devices, shards(): whole_table = lax.all_gather(embed_table, 'dp', axis=1, tiled=True)  640 us
    add x1, other arithmetic, shards(): running + jax.ops.segment_sum(masked, row_index[:, position, :].T.reshape...  321 us
    gather x8, local copies, waits for them, and re-layouts, shards(): picked = whole_table[:, row_index[:, position, :]]  240 us
    reduce_scatter x1, waiting for transfers between devices, shards(): lax.psum_scatter(running.T.astype(jnp.bfloat16), 'dp', scatter_dimension=...  232 us
    psum x3, blocking collectives, layer_backward(): lax.psum((jnp.sum(grad_shaped, axis=0), jnp.sum(grad_shaped * normed, axi...  59.5 us
    psum x3, blocking collectives, layer_forward(): lax.psum((jnp.sum(hidden, axis=0), jnp.sum(hidden * hidden, axis=0)), 'dp')  57.6 us
    unnamed x3, blocking collectives  54.3 us
    psum x1, blocking collectives, shards(): lax.psum((joining_left_grad, joining_right_grad, joining_pair_grad, joini...  41.5 us
  transfers between devices with their start and end apart: 9, of which 3 were waited for; matrix products, arithmetic and copies ran while one was open for 21% of the time, Pallas kernels for 0%

commit v1 on v0

--- a/solution.py
+++ b/solution.py
@@ -1,7 +1,301 @@
+import functools
 import jax
 import jax.numpy as jnp
 from jax import lax
+from jax.experimental import pallas as pl
+from jax.experimental.pallas import tpu as pltpu
 from jax.sharding import PartitionSpec as P
+
+MESH = pl.DeviceIdType.MESH
+VM = pl.BlockSpec(memory_space=pltpu.VMEM)
+HI = 256
+CHUNK = 512
+
+
+def params(cid, mib=48):
+    if cid is None:
+        return pltpu.CompilerParams(vmem_limit_bytes=mib << 20)
+    return pltpu.CompilerParams(
+        collective_id=cid, has_side_effects=True, vmem_limit_bytes=mib << 20
+    )
+
+
+def greet(dp, mp):
+    me, mine = lax.axis_index("dp"), lax.axis_index("mp")
+    barrier = pltpu.get_barrier_semaphore()
+    for step in range(1, dp):
+        pl.semaphore_signal(
+            barrier, inc=1, device_id={"dp": lax.rem(me + step, dp)}, device_id_type=MESH
+        )
+    for step in range(1, mp):
+        pl.semaphore_signal(
+            barrier, inc=1, device_id={"mp": lax.rem(mine + step, mp)}, device_id_type=MESH
+        )
+    pl.semaphore_wait(barrier, dp - 1 + mp - 1)
+
+
+def remote(src, dst, send, recv, where):
+    return pltpu.make_async_remote_copy(
+        src_ref=src, dst_ref=dst, send_sem=send, recv_sem=recv,
+        device_id=where, device_id_type=MESH,
+    )
+
+
+def spread_dp(dp, pick, send, recv):
+    me = lax.axis_index("dp")
+    out = []
+    for step in range(1, dp):
+        to = lax.rem(me + step, dp)
+        copy = remote(pick(me), pick(me), send.at[step - 1], recv.at[step - 1], {"dp": to})
+        copy.start()
+        out.append(copy)
+    return out
+
+
+def compact_keys(key):
+    count = key.shape[0]
+    dead = (key < 0).astype(jnp.int32)
+    sub = lax.broadcasted_iota(jnp.int32, (8, 128), 0)
+    lane = lax.broadcasted_iota(jnp.int32, (8, 128), 1)
+    running = jnp.zeros((8, 128), jnp.int32)
+    before = []
+    for v in range(count):
+        before.append(running)
+        running = running + dead[v]
+    scan = running
+    for k in (1, 2, 4):
+        scan = scan + jnp.where(sub >= k, pltpu.roll(scan, k, 0), 0)
+    over_sub = scan - running
+    column = jnp.broadcast_to(jnp.sum(running, axis=0, keepdims=True), (8, 128))
+    scan = column
+    for k in (1, 2, 4, 8, 16, 32, 64):
+        scan = scan + jnp.where(lane >= k, pltpu.roll(scan, k, 1), 0)
+    base = over_sub + scan - column
+    shift = jnp.stack([jnp.where(dead[v] > 0, 0, before[v] + base) for v in range(count)])
+
+    def next_place(x):
+        n = x.shape[0]
+        flat = x.reshape(n * 8, 128)
+        y = jnp.stack([pltpu.roll(x[v], 7, 0) for v in range(n)])
+        z = jnp.stack([pltpu.roll(y[v], 127, 1) for v in range(n)])
+        return jnp.where(sub[None] < 7, y, z)
+
+    bit = 0
+    step = 1
+    while step < count:
+        moved_key = jnp.concatenate([key[step:], next_place(key[:step])], axis=0)
+        moved_shift = jnp.concatenate([shift[step:], next_place(shift[:step])], axis=0)
+        key, shift = settle(key, shift, moved_key, moved_shift, bit)
+        bit, step = bit + 1, step * 2
+    for j in (1, 2, 4):
+        def roll_sub(x):
+            y = jnp.stack([pltpu.roll(x[v], 8 - j, 0) for v in range(count)])
+            z = jnp.stack([pltpu.roll(y[v], 127, 1) for v in range(count)])
+            return jnp.where(sub[None] < 8 - j, y, z)
+        key, shift = settle(key, shift, roll_sub(key), roll_sub(shift), bit)
+        bit += 1
+    for j in (1, 2, 4, 8, 16, 32, 64):
+        def roll_lane(x):
+            return jnp.stack([pltpu.roll(x[v], 128 - j, 1) for v in range(count)])
+        key, shift = settle(key, shift, roll_lane(key), roll_lane(shift), bit)
+        bit += 1
+    return key
+
+
+def settle(key, shift, moved_key, moved_shift, bit):
+    take = (moved_shift & (1 << bit)) != 0
+    stay = (shift & (1 << bit)) == 0
+    key = jnp.where(take, moved_key, jnp.where(stay, key, -1))
+    shift = jnp.where(take, moved_shift, jnp.where(stay, shift, 0))
+    return key, shift
+
+
+def make_keys(ids, lens, scratch, own_rows, mp, bits):
+    cats, slots, rows = ids.shape
+    part = own_rows // mp
+    mine = lax.axis_index("mp")
+    scratch[...] = jnp.full_like(scratch, -1)
+    slot = lax.broadcasted_iota(jnp.int32, (slots, rows), 0)
+    event = lax.broadcasted_iota(jnp.int32, (slots, rows), 1)
+
+    def body(c, carry):
+        values = ids[c]
+        holder = values // own_rows
+        inner = values - holder * own_rows
+        owner = inner // part
+        place = holder * part + inner - owner * part
+        live = (slot < lens[pl.ds(c, 1), :]) & (owner == mine)
+        key = jnp.where(live, place * (1 << bits) + c * rows + event, -1)
+        for q in range(rows // 128):
+            scratch[pl.ds((c * (rows // 128) + q) * slots, slots), :] = key[:, q * 128 : (q + 1) * 128]
+        return carry
+
+    lax.fori_loop(0, cats, body, 0)
+
+
+def table_kernel(dp, mp, own_rows, bits, ids, lens, table, t2, keys, scratch, send, recv):
+    part = own_rows // mp
+    blocks = part // HI
+    tall = blocks * 16
+    me, mine = lax.axis_index("dp"), lax.axis_index("mp")
+    greet(dp, mp)
+    own = table[:, pl.ds(pl.multiple_of(mine * part, HI), part)].astype(jnp.bfloat16)
+    for b in range(blocks):
+        t2[pl.ds(pl.multiple_of(me * tall + b * 16, 16), 16), :] = own[:, b * HI : (b + 1) * HI]
+
+    def slot(i):
+        return t2.at[pl.ds(pl.multiple_of(i * tall, 16), tall), :]
+
+    copies = spread_dp(dp, slot, send, recv)
+    make_keys(ids, lens, scratch, own_rows, mp, bits)
+    count = scratch.shape[0] // 8
+    packed = compact_keys(scratch[...].reshape(count, 8, 128))
+    keys[...] = jnp.transpose(packed.reshape(count * 8, 128))
+    for copy in copies:
+        copy.wait()
+
+
+def lookup_kernel(cats, rows, bits, keys, t2, pooled, total):
+    lows = t2.shape[0] // 16
+    filled = jnp.max(keys[...], axis=1, keepdims=True) >= 0
+    chunks = jnp.sum(filled.astype(jnp.int32))
+    total[...] = jnp.zeros_like(total)
+    hi_iota = lax.broadcasted_iota(jnp.int32, (HI, CHUNK), 0)
+    event_iota = lax.broadcasted_iota(jnp.int32, (rows, CHUNK), 0)
+
+    def body(k, carry):
+        key = keys[pl.ds(k, 1), :]
+        place = lax.shift_right_arithmetic(key, bits)
+        bag = key & ((1 << bits) - 1)
+        cat = bag // rows
+        event = bag - cat * rows
+        low = lax.shift_right_arithmetic(place, 8)
+        high = place & (HI - 1)
+        pick = jnp.where(hi_iota == high, 1.0, 0.0).astype(jnp.bfloat16)
+        z = jnp.zeros((16, CHUNK), jnp.float32)
+        for b in range(0, lows, 16):
+            n = min(16, lows - b)
+            y = jnp.dot(t2[b * 16 : (b + n) * 16, :], pick, preferred_element_type=jnp.float32)
+            for j in range(n):
+                z = z + jnp.where(low == b + j, y[j * 16 : (j + 1) * 16], 0.0)
+        z = z.astype(jnp.bfloat16)
+        zero = jnp.zeros_like(z)
+        wide = jnp.concatenate([jnp.where(cat == c, z, zero) for c in range(cats)], axis=0)
+        place_of = jnp.where(event_iota == event, 1.0, 0.0).astype(jnp.bfloat16)
+        total[...] += lax.dot_general(
+            wide, place_of, (((1,), (1,)), ((), ())), preferred_element_type=jnp.float32
+        )
+        return carry
+
+    lax.fori_loop(0, chunks, body, 0)
+    pooled[...] = total[...].astype(pooled.dtype)
+
+
+def scatter_kernel(cats, rows, bits, keys, grad, out, total):
+    lows = total.shape[0] // 16
+    filled = jnp.max(keys[...], axis=1, keepdims=True) >= 0
+    chunks = jnp.sum(filled.astype(jnp.int32))
+    total[...] = jnp.zeros_like(total)
+    hi_iota = lax.broadcasted_iota(jnp.int32, (HI, CHUNK), 0)
+    event_iota = lax.broadcasted_iota(jnp.int32, (rows, CHUNK), 0)
+
+    def body(k, carry):
+        key = keys[pl.ds(k, 1), :]
+        place = lax.shift_right_arithmetic(key, bits)
+        bag = key & ((1 << bits) - 1)
+        cat = bag // rows
+        event = bag - cat * rows
+        low = lax.shift_right_arithmetic(place, 8)
+        high = place & (HI - 1)
+        place_of = jnp.where(event_iota == event, 1.0, 0.0).astype(jnp.bfloat16)
+        wide = jnp.dot(grad[...], place_of, preferred_element_type=jnp.float32)
+        g = jnp.zeros((16, CHUNK), jnp.float32)
+        for c in range(cats):
+            g = g + jnp.where(cat == c, wide[c * 16 : (c + 1) * 16], 0.0)
+        g = g.astype(jnp.bfloat16)
+        zero = jnp.zeros_like(g)
+        pick = jnp.where(hi_iota == high, 1.0, 0.0).astype(jnp.bfloat16)
+        for b in range(0, lows, 16):
+            n = min(16, lows - b)
+            tall = jnp.concatenate([jnp.where(low == b + j, g, zero) for j in range(n)], axis=0)
+            total[b * 16 : (b + n) * 16, :] += lax.dot_general(
+                tall, pick, (((1,), (1,)), ((), ())), preferred_element_type=jnp.float32
+            )
+        return carry
+
+    lax.fori_loop(0, chunks, body, 0)
+    out[...] = total[...].astype(out.dtype)
+
+
+def relay_own(mp, slot, send, recv):
+    mine = lax.axis_index("mp")
+    core = lax.rem(mine, 2)
+    other = mine + 1 - 2 * core
+    chips = mp // 2
+    out = []
+    for k in range(1, chips):
+        to = lax.rem(mine + 2 * k, mp)
+        copy = remote(slot(mine), slot(mine), send.at[2 * k], recv.at[2 * k], {"mp": to})
+        copy.start()
+        out.append(copy)
+    copy = remote(slot(mine), slot(mine), send.at[1], recv.at[1], {"mp": other})
+    copy.start()
+    out.append(copy)
+    return out
+
+
+def relay_rest(mp, slot, send, recv, started):
+    mine = lax.axis_index("mp")
+    core = lax.rem(mine, 2)
+    other = mine + 1 - 2 * core
+    chips = mp // 2
+    passed = []
+    for k in range(1, chips):
+        source = lax.rem(mine + mp - 2 * k, mp)
+        remote(slot(source), slot(source), send.at[2 * k], recv.at[2 * k], {"mp": other}).wait_recv()
+        copy = remote(slot(source), slot(source), send.at[2 * k + 1], recv.at[2 * k + 1], {"mp": other})
+        copy.start()
+        passed.append(copy)
+    remote(slot(other), slot(other), send.at[1], recv.at[1], {"mp": other}).wait_recv()
+    for k in range(1, chips):
+        far = lax.rem(other + mp - 2 * k, mp)
+        remote(slot(far), slot(far), send.at[2 * k + 1], recv.at[2 * k + 1], {"mp": other}).wait_recv()
+    for copy in started + passed:
+        copy.wait_send()
+
+
+def rows_kernel(dp, mp, grads, out, landed, shares, send, recv, send2, recv2):
+    tall = grads.shape[0] // dp
+    me, mine = lax.axis_index("dp"), lax.axis_index("mp")
+    greet(dp, mp)
+    copies = []
+    for step in range(1, dp):
+        to = lax.rem(me + step, dp)
+        copy = remote(
+            grads.at[pl.ds(pl.multiple_of(to * tall, 16), tall), :],
+            landed.at[step - 1], send.at[step - 1], recv.at[step - 1], {"dp": to},
+        )
+        copy.start()
+        copies.append(copy)
+    total = grads[pl.ds(pl.multiple_of(me * tall, 16), tall), :].astype(jnp.float32)
+    for step in range(1, dp):
+        copies[step - 1].wait_recv()
+        total = total + landed[step - 1].astype(jnp.float32)
+    shares[mine] = total.astype(jnp.bfloat16)
+
+    def slot(i):
+        return shares.at[i]
+
+    started = relay_own(mp, slot, send2, recv2)
+    relay_rest(mp, slot, send2, recv2, started)
+    blocks = tall // 16
+    for m in range(mp):
+        for b in range(blocks):
+            out[:, (m * blocks + b) * HI : (m * blocks + b + 1) * HI] = shares[
+                m, b * 16 : (b + 1) * 16, :
+            ].astype(jnp.float32)
+    for copy in copies:
+        copy.wait_send()
 
 
 def layer_forward(inputs, weight, gain_row, shift_row, batch_size):
@@ -102,15 +396,38 @@
     own_rows = embed_table.shape[1]
     width = embed_table.shape[0]
     numeric_cols = dense_values.shape[1] * width
-    positions = lax.broadcasted_iota(jnp.int32, field_ids.shape, 1)
-    live_mask = positions < lengths[:, None, :]
-    whole_table = lax.all_gather(embed_table, "dp", axis=1, tiled=True)
-    row_index = jnp.where(live_mask, field_ids, 0)
-    running = jnp.zeros((width, cat_fields, tok_rows), jnp.float32)
-    for position in range(bag_size):
-        picked = whole_table[:, row_index[:, position, :]]
-        running = running + jnp.where(live_mask[None, :, position, :], picked, 0.0)
-    pooled = jnp.transpose(running, (2, 1, 0)).reshape(tok_rows, cat_fields * width)
+    dp, mp = lax.axis_size("dp"), lax.axis_size("mp")
+    bits = (cat_fields * tok_rows - 1).bit_length()
+    part = own_rows // mp
+    tall = part // HI * 16
+    lookups = cat_fields * bag_size * tok_rows
+    vregs = 1 << (-(-lookups // 1024) - 1).bit_length()
+    t2, keys = pl.pallas_call(
+        functools.partial(table_kernel, dp, mp, own_rows, bits),
+        out_shape=(
+            jax.ShapeDtypeStruct((dp * tall, HI), jnp.bfloat16),
+            jax.ShapeDtypeStruct((128, vregs * 8), jnp.int32),
+        ),
+        in_specs=[VM] * 3,
+        out_specs=(VM, VM),
+        scratch_shapes=[
+            pltpu.VMEM((vregs * 8, 128), jnp.int32),
+            pltpu.SemaphoreType.DMA((dp - 1,)),
+            pltpu.SemaphoreType.DMA((dp - 1,)),
+        ],
+        compiler_params=params(0),
+        name="table",
+    )(field_ids, lengths, embed_table)
+    pooled_t = pl.pallas_call(
+        functools.partial(lookup_kernel, cat_fields, tok_rows, bits),
+        out_shape=jax.ShapeDtypeStruct((cat_fields * 16, tok_rows), jnp.float32),
+        in_specs=[VM] * 2,
+        out_specs=VM,
+        scratch_shapes=[pltpu.VMEM((cat_fields * 16, tok_rows), jnp.float32)],
+        compiler_params=params(None),
+        name="lookup",
+    )(keys, t2)
+    pooled = lax.psum(pooled_t, "mp").T
     numeric = (dense_values[:, :, None] * num_embed[None, :, :]).reshape(tok_rows, numeric_cols)
     features = jnp.concatenate([numeric, pooled], axis=1).astype(jnp.bfloat16)
     local_cols = gate_weight.shape[1]
@@ -185,19 +502,31 @@
     numeric_grad = grad_features[:, :numeric_cols].astype(jnp.float32).reshape(tok_rows, -1, width)
     num_embed_grad = jnp.sum(dense_values[:, :, None] * numeric_grad, axis=0)
     pooled_grad = grad_features[:, numeric_cols:]
-    row_index = jnp.where(live_mask, field_ids, 0)
-    values = pooled_grad.astype(jnp.float32).reshape(tok_rows, cat_fields, width)
-    running = jnp.zeros((own_rows * lax.axis_size("dp"), width), jnp.float32)
-    for position in range(bag_size):
-        masked = jnp.where(live_mask[:, position, :].T[:, :, None], values, 0.0).reshape(-1, width)
-        running = running + jax.ops.segment_sum(
-            masked,
-            row_index[:, position, :].T.reshape(-1),
-            num_segments=own_rows * lax.axis_size("dp"),
-        )
-    embed_table_grad = lax.psum_scatter(
-        running.T.astype(jnp.bfloat16), "dp", scatter_dimension=1, tiled=True
-    ).astype(jnp.float32)
+    row_sums = pl.pallas_call(
+        functools.partial(scatter_kernel, cat_fields, tok_rows, bits),
+        out_shape=jax.ShapeDtypeStruct((dp * tall, HI), jnp.bfloat16),
+        in_specs=[VM] * 2,
+        out_specs=VM,
+        scratch_shapes=[pltpu.VMEM((dp * tall, HI), jnp.float32)],
+        compiler_params=params(None),
+        name="scatter",
+    )(keys, pooled_grad.T)
+    embed_table_grad = pl.pallas_call(
+        functools.partial(rows_kernel, dp, mp),
+        out_shape=jax.ShapeDtypeStruct((width, own_rows), jnp.float32),
+        in_specs=[VM],
+        out_specs=VM,
+        scratch_shapes=[
+            pltpu.VMEM((dp - 1, tall, HI), jnp.bfloat16),
+            pltpu.VMEM((mp, tall, HI), jnp.bfloat16),
+            pltpu.SemaphoreType.DMA((dp - 1,)),
+            pltpu.SemaphoreType.DMA((dp - 1,)),
+            pltpu.SemaphoreType.DMA((mp,)),
+            pltpu.SemaphoreType.DMA((mp,)),
+        ],
+        compiler_params=params(1),
+        name="rows",
+    )(row_sums)
     (
         joining_left_grad,
         joining_right_grad,

time: 1920 us -> 501 us (0.26)
  waiting for transfers between devices: 880 us -> 35.6 us
  other arithmetic: 387 us -> 22.2 us
  local copies, waits for them, and re-layouts: 301 us -> 32.6 us
  Pallas kernels: 0 us -> 53.1 us
  blocking collectives: 278 us -> 304 us
    all_gather x1 -> x0, waiting for transfers between devices: 640 us -> none  [shards(): whole_table = lax.all_gather(embed_table, 'dp', axis=1, tiled=True)]
    add x1 -> x0, other arithmetic: 321 us -> none  [shards(): running + jax.ops.segment_sum(masked, row_index[:, position, :].T.reshape...]
    gather x8 -> x0, local copies, waits for them, and re-layouts: 240 us -> none  [shards(): picked = whole_table[:, row_index[:, position, :]]]
    reduce_scatter x1 -> x0, waiting for transfers between devices: 232 us -> none  [shards(): lax.psum_scatter(running.T.astype(jnp.bfloat16), 'dp', scatter_dimension=...]
    pallas_call x0 -> x4, Pallas kernels: none -> 53.1 us  [the longest x1 20.8 us: shards(): pl.pallas_call(functools.partial(rows_kernel, dp, mp), out_shape=jax.Shap...]
    psum x0 -> x1, blocking collectives: none -> 21.6 us  [shards(): pooled = lax.psum(pooled_t, 'mp').T]
    psum x1, waiting for transfers between devices: 0.01 us -> 19.3 us  [shards(): lax.psum((joining_left_grad, joining_right_grad, joining_pair_grad, joini...]
  transfers between devices with their start and end apart: 9 -> 7, of which waited for: 3 -> 4; matrix products, arithmetic and copies ran while one was open for 21% -> 8% of each run, Pallas kernels for 0% -> 6%
where the time goes in v1:
time: 501 us
  blocking collectives  304 us (61%)
  Pallas kernels  53.1 us (11%)
  waiting for transfers between devices  35.6 us (7%)
  local copies, waits for them, and re-layouts  32.6 us (7%)
  matrix products  27.8 us (6%)
  other arithmetic  22.2 us (4%)
  between operations  16.5 us (3%)
  starting transfers between devices  8.84 us (2%)
    psum x3, blocking collectives, layer_forward(): lax.psum((jnp.sum(hidden, axis=0), jnp.sum(hidden * hidden, axis=0)), 'dp')  57.8 us
    psum x3, blocking collectives, layer_backward(): lax.psum((jnp.sum(grad_shaped, axis=0), jnp.sum(grad_shaped * normed, axi...  57.6 us
    unnamed x3, blocking collectives  55.3 us
    psum x1, blocking collectives, shards(): lax.psum((joining_left_grad, joining_right_grad, joining_pair_grad, joini...  45.9 us
    all_gather x5, blocking collectives, layer_forward(): lax.all_gather(active, 'mp', axis=1, tiled=True)  37.2 us
    psum x1, blocking collectives, shards(): grad_features = lax.psum(partial_features, 'mp').astype(jnp.bfloat16)  28.8 us
    unnamed x237, local copies, waits for them, and re-layouts  24 us
    psum x1, blocking collectives, shards(): pooled = lax.psum(pooled_t, 'mp').T  21.6 us
  transfers between devices with their start and end apart: 7, of which 4 were waited for; matrix products, arithmetic and copies ran while one was open for 8% of the time, Pallas kernels for 6%

profile of v1, /device:TPU:0, one launch (start us, length us, event | category | flops | bytes accessed | tf_op | source)
XLA Modules:
  0.0 500.7 jit_solution(2493173897065582162)
XLA Ops:
  10.1 15.2 %table.2 = (bf16[1024,256]{1,0:T(8,128)(2,1)S(1)}, s32[128,512]{1,0:T(8,128)S(1)}) custom-call(s32[26,4,512]{2,1,0:T(4,128)S(1)} %copy-done.2, s32[26,512]{1,0:T(8,128)S(1)} %copy-done.3, f32[16,8192]{1,0:T(8,128)S(1)} %copy-done.1), custom_call_target="tpu_custom_call" | custom-call | tf_op jit(solution)/shard_map/table/pallas_call | solution.py:405
  25.4 8.5 %lookup.1 = f32[416,512]{1,0:T(8,128)S(1)} custom-call(s32[128,512]{1,0:T(8,128)S(1)} %get-tuple-element.19.keys, bf16[1024,256]{1,0:T(8,128)(2,1)S(1)} %get-tuple-element.20.t2), custom_call_target="tpu_custom_call" | custom-call | tf_op jit(solution)/shard_map/lookup/pallas_call | solution.py:421
  33.9 21.6 %all-reduce.22 = bf16[416,512]{1,0:T(8,128)(2,1)S(1)} all-reduce(f32[416,512]{1,0:T(8,128)S(1)} %lookup.1), channel_id=1, replica_groups=mesh['dp'=8,'mp'=4] {'mp'}, use_global_device_ids=true, to_apply=%region_0.0 | all-reduce | flops 212992 | bytes 1277952 | tf_op jit(solution)/shard_map/psum | solution.py:430
  65.4 15.2 %all-gather.5.cloned.1.call-done = bf16[2,512,624]{1,0,2:T(2,128)(2,1)} async-done(((bf16[2,512,156]{1,0,2:T(2,128)(2,1)}), bf16[2,512,624]{1,0,2:T(2,128)(2,1)}) %all-gather.5.cloned.1.call-update) | async-done | bytes 1277968 | tf_op jit(solution)/shard_map/all_gather | solution.py:442
  86.0 21.4 %all-reduce.14 = (f32[100]{0:T(128)S(1)}, f32[100]{0:T(128)S(1)}) all-reduce(f32[100]{0:T(128)S(1)} %get-tuple-element.108, f32[100]{0:T(128)S(1)} %get-tuple-element.107), channel_id=1, replica_groups=mesh['dp'=8,'mp'=4] {'dp'}, use_global_device_ids=true, to_apply=%region_4.0 | all-reduce | flops 200 | bytes 1600 | tf_op jit(solution)/shard_map/psum | solution.py:305
  108.1 6.2 %all-gather = bf16[4,100,512]{2,1,0:T(8,128)(2,1)S(1)} all-gather(bf16[1,100,512]{2,1,0:T(8,128)(2,1)S(1)} %fusion.42), channel_id=1, replica_groups=mesh['dp'=8,'mp'=4] {'mp'}, dimensions={0}, use_global_device_ids=true | all-gather | bytes 512000 | tf_op jit(solution)/shard_map/all_gather | solution.py:314
  116.2 17.1 %all-reduce.13 = (f32[200]{0:T(256)S(1)}, f32[200]{0:T(256)S(1)}, f32[100]{0:T(128)S(1)}, f32[100]{0:T(128)S(1)}) all-reduce(f32[200]{0:T(256)S(1)} %get-tuple-element.96, f32[200]{0:T(256)S(1)} %get-tuple-element.95, f32[100]{0:T(128)S(1)} %get-tuple-element.106, f32[100]{0:T(128)S(1)} %get-tuple-element.105), channel_id=1, replica_groups=mesh['dp'=8,'mp'=4] {'dp'}, use_global_device_ids=true, to_apply=%region_16.17 | all-reduce | flops 600 | bytes 4800 | tf_op jit(solution)/shard_map/psum | solution.py:305
  133.6 6.2 %all-gather.1 = bf16[4,100,512]{2,1,0:T(8,128)(2,1)S(1)} all-gather(bf16[1,100,512]{2,1,0:T(8,128)(2,1)S(1)} %fusion.43), channel_id=1, replica_groups=mesh['dp'=8,'mp'=4] {'mp'}, dimensions={0}, use_global_device_ids=true | all-gather | bytes 512000 | tf_op jit(solution)/shard_map/all_gather | solution.py:314
  140.7 9.3 %all_gather.22 = bf16[512,800]{0,1:T(8,128)(2,1)} all-gather(bf16[512,200]{0,1:T(8,128)(2,1)S(1)} %multiply_convert_fusion.5), channel_id=1, replica_groups=mesh['dp'=8,'mp'=4] {'mp'}, dimensions={1}, use_global_device_ids=true | all-gather | bytes 1024000 | tf_op jit(solution)/shard_map/all_gather | solution.py:314
  152.2 19.3 %all-reduce.12 = (f32[200]{0:T(256)S(1)}, f32[200]{0:T(256)S(1)}, f32[100]{0:T(128)S(1)}, f32[100]{0:T(128)S(1)}) all-reduce(f32[200]{0:T(256)S(1)} %get-tuple-element.94, f32[200]{0:T(256)S(1)} %get-tuple-element.93, f32[100]{0:T(128)S(1)} %get-tuple-element.104, f32[100]{0:T(128)S(1)} %get-tuple-element.103), channel_id=1, replica_groups=mesh['dp'=8,'mp'=4] {'dp'}, use_global_device_ids=true, to_apply=%region_20.21 | all-reduce | flops 600 | bytes 4800 | tf_op jit(solution)/shard_map/psum | solution.py:305
  172.9 8.2 %all_gather.23 = bf16[512,800]{0,1:T(8,128)(2,1)S(1)} all-gather(bf16[512,200]{0,1:T(8,128)(2,1)S(1)} %multiply_convert_fusion.4), channel_id=1, replica_groups=mesh['dp'=8,'mp'=4] {'mp'}, dimensions={1}, use_global_device_ids=true | all-gather | bytes 1024000 | tf_op jit(solution)/shard_map/all_gather | solution.py:314
  182.2 7.2 %all-gather.2 = bf16[4,100,512]{2,1,0:T(8,128)(2,1)} all-gather(bf16[1,100,512]{2,1,0:T(8,128)(2,1)S(1)} %fusion.44), channel_id=1, replica_groups=mesh['dp'=8,'mp'=4] {'mp'}, dimensions={0}, use_global_device_ids=true | all-gather | bytes 512000 | tf_op jit(solution)/shard_map/all_gather | solution.py:314
  197.7 17.8 %all-reduce.11 = (f32[100]{0:T(128)}, f32[100]{0:T(128)}) all-reduce(f32[100]{0:T(128)} %get-tuple-element.102, f32[100]{0:T(128)} %get-tuple-element.101), channel_id=1, replica_groups=mesh['dp'=8,'mp'=4] {'dp'}, use_global_device_ids=true, to_apply=%region_25.26 | all-reduce | flops 200 | bytes 1600 | tf_op jit(solution)/shard_map/psum | solution.py:321
  219.1 13.8 %fusion = f32[512,104]{0,1:T(8,128)} fusion(f32[512,400]{0,1:T(8,128)} %fusion.45), kind=kCustom, calls=%all-reduce-scatter | all-reduce-scatter fusion | flops 212993 | bytes 1032704
  243.8 19.8 %all-reduce.10 = (f32[200]{0:T(256)}, f32[200]{0:T(256)}, f32[100]{0:T(128)}, f32[100]{0:T(128)}) all-reduce(f32[200]{0:T(256)} %get-tuple-element.92, f32[200]{0:T(256)} %get-tuple-element.91, f32[100]{0:T(128)} %get-tuple-element.100, f32[100]{0:T(128)} %get-tuple-element.99), channel_id=1, replica_groups=mesh['dp'=8,'mp'=4] {'dp'}, use_global_device_ids=true, to_apply=%region_40.41 | all-reduce | flops 600 | bytes 4800 | tf_op jit(solution)/shard_map/psum | solution.py:321
  273.2 14.8 %fusion.1 = f32[512,104]{0,1:T(8,128)S(1)} fusion(f32[512,400]{0,1:T(8,128)S(1)} %fusion.49), kind=kCustom, calls=%all-reduce-scatter.1 | all-reduce-scatter fusion | flops 212993 | bytes 1032704
  296.7 20.0 %all-reduce.9 = (f32[200]{0:T(256)S(1)}, f32[200]{0:T(256)S(1)}, f32[100]{0:T(128)S(1)}, f32[100]{0:T(128)S(1)}) all-reduce(f32[200]{0:T(256)S(1)} %get-tuple-element.90, f32[200]{0:T(256)S(1)} %get-tuple-element.89, f32[100]{0:T(128)S(1)} %get-tuple-element.98, f32[100]{0:T(128)S(1)} %get-tuple-element.97), channel_id=1, replica_groups=mesh['dp'=8,'mp'=4] {'dp'}, use_global_device_ids=true, to_apply=%region_45.46 | all-reduce | flops 600 | bytes 4800 | tf_op jit(solution)/shard_map/psum | solution.py:321
  320.1 26.7 %fusion.71 = (f32[512,160]{0,1:T(8,128)}, f32[512,160]{0,1:T(8,128)}) fusion(f32[512,624]{0,1:T(8,128)S(1)} %fusion.85, f32[512,624]{0,1:T(8,128)S(1)} %fusion.60), kind=kCustom, calls=%all-reduce-scatter.4 | all-reduce-scatter fusion | flops 655361 | bytes 3211776
  351.4 4.1 collective-permute-start.3
  363.0 28.8 %all-reduce.23 = bf16[512,624]{0,1:T(8,128)(2,1)S(1)} all-reduce(f32[512,624]{0,1:T(8,128)S(1)} %dynamic_update_slice.3), channel_id=1, replica_groups=mesh['dp'=8,'mp'=4] {'mp'}, use_global_device_ids=true, to_apply=%region_48.49 | all-reduce | flops 319488 | bytes 1916928 | tf_op jit(solution)/shard_map/psum | solution.py:501
  391.8 8.5 %scatter.1.grads = bf16[1024,256]{1,0:T(8,128)(2,1)S(1)} custom-call(s32[128,512]{1,0:T(8,128)S(1)} %get-tuple-element.19.keys, bf16[416,512]{1,0:T(8,128)(2,1)S(1)} %slice_bitcast_fusion.grad), custom_call_target="tpu_custom_call" | custom-call | tf_op jit(solution)/shard_map/scatter/pallas_call | solution.py:505
  400.3 20.8 %rows.1 = f32[16,8192]{1,0:T(8,128)S(1)} custom-call(bf16[1024,256]{1,0:T(8,128)(2,1)S(1)} %scatter.1.grads), custom_call_target="tpu_custom_call" | custom-call | tf_op jit(solution)/shard_map/rows/pallas_call | solution.py:514
  421.4 45.9 %all-reduce.8 = (f32[13,16]{1,0:T(8,128)}, f32[2,156]{1,0:T(2,128)}, f32[400]{0:T(512)}, f32[800]{0:T(1024)}, f32[50,8,16]{2,1,0:T(8,128)S(1)}, /*index=5*/f32[1]{0:T(128)}) all-reduce(f32[13,16]{1,0:T(8,128)S(1)} %reduce_sum.268, f32[2,156]{1,0:T(2,128)S(1)} %get-tuple-element.148, ...), channel_id=1, replica_groups=mesh['dp'=8,'mp'=4] {'dp'}, use_global_device_ids=true, to_apply=%region_50.51 | all-reduce | flops 8121 | bytes 64968 | tf_op jit(solution)/shard_map/psum | solution.py:538
  468.1 19.3 %all-reduce.21.cloned.1.call-done = (f32[2,156,624]{2,1,0:T(8,128)}, f32[100,624]{1,0:T(8,128)}, f32[1,100,400]{1,2,0:T(8,128)}, f32[1,100,400]{1,2,0:T(8,128)}, f32[200,624]{1,0:T(8,128)}, /*index=5*/f32[200,800]{1,0:T(8,128)}) async-done(((f32[2,156,624]{2,1,0:T(8,128)}, f32[100,624]{1,0:T(8,128)}, f32[1,100,400]{1,2,0:T(8,128)}, f32[1,100,400]{1,2,0:T(8,128)}, f32[200,624]{1,0:T(8,128)}, ...) | async-done | bytes 2487568 | tf_op jit(solution)/shard_map/psum | solution.py:538
  (325 shorter events, 88.3 us)
Async XLA Ops:
  7.2 49.5 %copy-start = (bf16[2,156,624]{2,0,1:T(2,128)(2,1)S(1)}, bf16[2,156,624]{2,0,1:T(2,128)(2,1)}, u32[]{:S(2)}) copy-start(bf16[2,156,624]{2,0,1:T(2,128)(2,1)} %param.26) | copy-start | bytes 1168132
  7.2 73.4 %all-gather.5.cloned.1.call-start = ((), (), s32[]{:S(2)}) async-start(), calls=%async_computation.1 | async-start | bytes 1597440 | tf_op jit(solution)/shard_map/all_gather | solution.py:442
  25.4 30.2 %copy-start.38 = (f32[512,13]{0,1:T(8,128)S(1)}, f32[512,13]{0,1:T(8,128)}, u32[]{:S(2)}) copy-start(f32[512,13]{0,1:T(8,128)} %param.20) | copy-start | bytes 79876
  59.3 235.9 %reduce-scatter.10.cloned.1.call-start = ((), (), s32[]{:S(2)}) async-start(), calls=%async_computation.2 | async-start | bytes 2048000 | tf_op jit(solution)/shard_map/reduce_scatter | solution.py:334
  59.9 54.6 %copy-start.25 = (bf16[1,100,400]{1,2,0:T(8,128)(2,1)}, bf16[1,100,400]{1,2,0:T(8,128)(2,1)S(1)}, u32[]{:S(2)}) copy-start(bf16[1,100,400]{1,2,0:T(8,128)(2,1)S(1)} %copy.76) | copy-start | bytes 240004
  60.1 90.0 %copy-start.27 = (bf16[1,100,400]{1,2,0:T(8,128)(2,1)}, bf16[1,100,400]{1,2,0:T(8,128)(2,1)S(1)}, u32[]{:S(2)}) copy-start(bf16[1,100,400]{1,2,0:T(8,128)(2,1)S(1)} %copy.77) | copy-start | bytes 240004
  64.8 75.7 %copy-start.45 = (f32[1,200]{1,0:T(1,128)}, f32[1,200]{1,0:T(1,128)S(1)}, u32[]{:S(2)}) copy-start(f32[1,200]{1,0:T(1,128)S(1)} %get-tuple-element.176) | copy-start | bytes 2404
  64.8 107.3 %copy-start.48 = (f32[1,200]{1,0:T(1,128)}, f32[1,200]{1,0:T(1,128)S(1)}, u32[]{:S(2)}) copy-start(f32[1,200]{1,0:T(1,128)S(1)} %get-tuple-element.175) | copy-start | bytes 2404
  64.8 75.7 %copy-start.64 = (f32[1,200]{1,0:T(1,128)}, f32[1,200]{1,0:T(1,128)S(1)}, u32[]{:S(2)}) copy-start(f32[1,200]{1,0:T(1,128)S(1)} %get-tuple-element.178) | copy-start | bytes 2404
  64.8 107.3 %copy-start.66 = (f32[1,200]{1,0:T(1,128)}, f32[1,200]{1,0:T(1,128)S(1)}, u32[]{:S(2)}) copy-start(f32[1,200]{1,0:T(1,128)S(1)} %get-tuple-element.177) | copy-start | bytes 2404
  65.4 42.1 %copy-start.75 = (f32[100]{0:T(128)}, f32[100]{0:T(128)S(1)}, u32[]{:S(2)}) copy-start(f32[100]{0:T(128)S(1)} %get-tuple-element.173) | copy-start | bytes 1204
  65.4 42.1 %copy-start.77 = (f32[100]{0:T(128)}, f32[100]{0:T(128)S(1)}, u32[]{:S(2)}) copy-start(f32[100]{0:T(128)S(1)} %get-tuple-element.195) | copy-start | bytes 1204
  65.4 68.0 %copy-start.79 = (f32[100]{0:T(128)}, f32[100]{0:T(128)S(1)}, u32[]{:S(2)}) copy-start(f32[100]{0:T(128)S(1)} %get-tuple-element.174) | copy-start | bytes 1204
  65.4 68.0 %copy-start.80 = (f32[100]{0:T(128)}, f32[100]{0:T(128)S(1)}, u32[]{:S(2)}) copy-start(f32[100]{0:T(128)S(1)} %get-tuple-element.194) | copy-start | bytes 1204
  65.4 116.3 %copy-start.81 = (f32[100]{0:T(128)}, f32[100]{0:T(128)S(1)}, u32[]{:S(2)}) copy-start(f32[100]{0:T(128)S(1)} %get-tuple-element.172) | copy-start | bytes 1204
  150.5 30.7 %copy-start.86 = (f32[3,100]{1,0:T(4,128)S(1)}, f32[3,100]{1,0:T(4,128)}, u32[]{:S(2)}) copy-start(f32[3,100]{1,0:T(4,128)} %param.30) | copy-start | bytes 3604
  150.5 30.6 %copy-start.94 = (f32[100]{0:T(128)S(1)}, f32[100]{0:T(128)}, u32[]{:S(2)}) copy-start(f32[100]{0:T(128)} %copy-done.93) | copy-start | bytes 1204
  150.5 30.6 %copy-start.96 = (f32[100]{0:T(128)S(1)}, f32[100]{0:T(128)}, u32[]{:S(2)}) copy-start(f32[100]{0:T(128)} %copy-done.95) | copy-start | bytes 1204
  150.5 31.2 %copy-start.83 = (f32[100]{0:T(128)S(1)}, f32[100]{0:T(128)}, u32[]{:S(2)}) copy-start(f32[100]{0:T(128)} %get-tuple-element.196) | copy-start | bytes 1204
  233.6 4.7 collective-permute-start
  268.0 219.4 %all-reduce.21.cloned.1.call-start = ((), (), s32[]{:S(2)}) async-start(), calls=%async_computation.3 | async-start | bytes 5447680 | tf_op jit(solution)/shard_map/psum | solution.py:538
  288.1 5.1 %collective-permute-start.1 = (f32[512,12]{0,1:T(8,128)S(1)}, f32[512,12]{0,1:T(8,128)S(1)}, u32[]{:S(2)}, u32[]{:S(2)}) collective-permute-start(f32[512,12]{0,1:T(8,128)S(1)} %slice.74), channel_id=1, source_target_pairs={{0,1},{1,2},{2,3},{4,5},{5,6},{6,7},{8,9},{9,10},{10,11},{12,13},{... | collective-permute-start | bytes 73736
  347.6 7.9 %collective-permute-start.2 = (f32[512,12]{0,1:T(8,128)S(1)}, f32[512,12]{0,1:T(8,128)S(1)}, u32[]{:S(2)}, u32[]{:S(2)}) collective-permute-start(f32[512,12]{0,1:T(8,128)S(1)} %slice.75), channel_id=1, source_target_pairs={{0,1},{1,2},{2,3},{4,5},{5,6},{6,7},{8,9},{9,10},{10,11},{12,13},{... | collective-permute-start | bytes 73736
  351.4 4.8 collective-permute-start.3
  (90 other events, 630.1 us)
Sparse Core Ops, SparseCore 0:
  59.5 21.0 all-gather.4
  268.1 27.0 reduce-scatter.9
  359.1 128.2 all-reduce.20

commit v2 on v1

v2 whole, which is shorter than its diff:
```python
import functools
import jax
import jax.numpy as jnp
from jax import lax
from jax.experimental import pallas as pl
from jax.experimental.pallas import tpu as pltpu
from jax.sharding import PartitionSpec as P

MESH = pl.DeviceIdType.MESH
VM = pl.BlockSpec(memory_space=pltpu.VMEM)
HI = 256
CHUNK = 512


def params(cid, mib=48):
    if cid is None:
        return pltpu.CompilerParams(vmem_limit_bytes=mib << 20)
    return pltpu.CompilerParams(
        collective_id=cid, has_side_effects=True, vmem_limit_bytes=mib << 20
    )


def greet(dp, mp):
    me, mine = lax.axis_index("dp"), lax.axis_index("mp")
    barrier = pltpu.get_barrier_semaphore()
    for step in range(1, dp):
        pl.semaphore_signal(
            barrier, inc=1, device_id={"dp": lax.rem(me + step, dp)}, device_id_type=MESH
        )
    for step in range(1, mp):
        pl.semaphore_signal(
            barrier, inc=1, device_id={"mp": lax.rem(mine + step, mp)}, device_id_type=MESH
        )
    pl.semaphore_wait(barrier, dp - 1 + mp - 1)


def remote(src, dst, send, recv, where):
    return pltpu.make_async_remote_copy(
        src_ref=src, dst_ref=dst, send_sem=send, recv_sem=recv,
        device_id=where, device_id_type=MESH,
    )


def spread_dp(dp, pick, send, recv):
    me = lax.axis_index("dp")
    out = []
    for step in range(1, dp):
        to = lax.rem(me + step, dp)
        copy = remote(pick(me), pick(me), send.at[step - 1], recv.at[step - 1], {"dp": to})
        copy.start()
        out.append(copy)
    return out


def compact_keys(key):
    count = key.shape[0]
    dead = (key < 0).astype(jnp.int32)
    sub = lax.broadcasted_iota(jnp.int32, (8, 128), 0)
    lane = lax.broadcasted_iota(jnp.int32, (8, 128), 1)
    running = jnp.zeros((8, 128), jnp.int32)
    before = []
    for v in range(count):
        before.append(running)
        running = running + dead[v]
    scan = running
    for k in (1, 2, 4):
        scan = scan + jnp.where(sub >= k, pltpu.roll(scan, k, 0), 0)
    over_sub = scan - running
    column = jnp.broadcast_to(jnp.sum(running, axis=0, keepdims=True), (8, 128))
    scan = column
    for k in (1, 2, 4, 8, 16, 32, 64):
        scan = scan + jnp.where(lane >= k, pltpu.roll(scan, k, 1), 0)
    base = over_sub + scan - column
    shift = jnp.stack([jnp.where(dead[v] > 0, 0, before[v] + base) for v in range(count)])

    def next_place(x):
        n = x.shape[0]
        flat = x.reshape(n * 8, 128)
        y = jnp.stack([pltpu.roll(x[v], 7, 0) for v in range(n)])
        z = jnp.stack([pltpu.roll(y[v], 127, 1) for v in range(n)])
        return jnp.where(sub[None] < 7, y, z)

    bit = 0
    step = 1
    while step < count:
        moved_key = jnp.concatenate([key[step:], next_place(key[:step])], axis=0)
        moved_shift = jnp.concatenate([shift[step:], next_place(shift[:step])], axis=0)
        key, shift = settle(key, shift, moved_key, moved_shift, bit)
        bit, step = bit + 1, step * 2
    for j in (1, 2, 4):
        def roll_sub(x):
            y = jnp.stack([pltpu.roll(x[v], 8 - j, 0) for v in range(count)])
            z = jnp.stack([pltpu.roll(y[v], 127, 1) for v in range(count)])
            return jnp.where(sub[None] < 8 - j, y, z)
        key, shift = settle(key, shift, roll_sub(key), roll_sub(shift), bit)
        bit += 1
    for j in (1, 2, 4, 8, 16, 32, 64):
        def roll_lane(x):
            return jnp.stack([pltpu.roll(x[v], 128 - j, 1) for v in range(count)])
        key, shift = settle(key, shift, roll_lane(key), roll_lane(shift), bit)
        bit += 1
    return key


def settle(key, shift, moved_key, moved_shift, bit):
    take = (moved_shift & (1 << bit)) != 0
    stay = (shift & (1 << bit)) == 0
    key = jnp.where(take, moved_key, jnp.where(stay, key, -1))
    shift = jnp.where(take, moved_shift, jnp.where(stay, shift, 0))
    return key, shift


def make_keys(ids, lens, scratch, own_rows, mp, bits):
    cats, slots, rows = ids.shape
    part = own_rows // mp
    mine = lax.axis_index("mp")
    scratch[...] = jnp.full_like(scratch, -1)
    slot = lax.broadcasted_iota(jnp.int32, (slots, rows), 0)
    event = lax.broadcasted_iota(jnp.int32, (slots, rows), 1)

    def body(c, carry):
        values = ids[c]
        holder = values // own_rows
        inner = values - holder * own_rows
        owner = inner // part
        place = holder * part + inner - owner * part
        live = (slot < lens[pl.ds(c, 1), :]) & (owner == mine)
        key = jnp.where(live, place * (1 << bits) + c * rows + event, -1)
        for q in range(rows // 128):
            scratch[pl.ds((c * (rows // 128) + q) * slots, slots), :] = key[:, q * 128 : (q + 1) * 128]
        return carry

    lax.fori_loop(0, cats, body, 0)


def lookup_kernel(cats, rows, bits, keys, t2, pooled, total):
    lows = t2.shape[0] // 16
    filled = jnp.max(keys[...], axis=1, keepdims=True) >= 0
    chunks = jnp.sum(filled.astype(jnp.int32))
    total[...] = jnp.zeros_like(total)
    hi_iota = lax.broadcasted_iota(jnp.int32, (HI, CHUNK), 0)
    event_iota = lax.broadcasted_iota(jnp.int32, (rows, CHUNK), 0)

    def body(k, carry):
        key = keys[pl.ds(k, 1), :]
        place = lax.shift_right_arithmetic(key, bits)
        bag = key & ((1 << bits) - 1)
        cat = bag // rows
        event = bag - cat * rows
        low = lax.shift_right_arithmetic(place, 8)
        high = place & (HI - 1)
        pick = jnp.where(hi_iota == high, 1.0, 0.0).astype(jnp.bfloat16)
        z = jnp.zeros((16, CHUNK), jnp.float32)
        for b in range(0, lows, 16):
            n = min(16, lows - b)
            y = jnp.dot(t2[b * 16 : (b + n) * 16, :], pick, preferred_element_type=jnp.float32)
            for j in range(n):
                z = z + jnp.where(low == b + j, y[j * 16 : (j + 1) * 16], 0.0)
        z = z.astype(jnp.bfloat16)
        zero = jnp.zeros_like(z)
        wide = jnp.concatenate([jnp.where(cat == c, z, zero) for c in range(cats)], axis=0)
        place_of = jnp.where(event_iota == event, 1.0, 0.0).astype(jnp.bfloat16)
        total[...] += lax.dot_general(
            wide, place_of, (((1,), (1,)), ((), ())), preferred_element_type=jnp.float32
        )
        return carry

    lax.fori_loop(0, chunks, body, 0)
    pooled[...] = total[...].astype(pooled.dtype)


def scatter_kernel(cats, rows, bits, keys, grad, out, total):
    lows = total.shape[0] // 16
    filled = jnp.max(keys[...], axis=1, keepdims=True) >= 0
    chunks = jnp.sum(filled.astype(jnp.int32))
    total[...] = jnp.zeros_like(total)
    hi_iota = lax.broadcasted_iota(jnp.int32, (HI, CHUNK), 0)
    event_iota = lax.broadcasted_iota(jnp.int32, (rows, CHUNK), 0)

    def body(k, carry):
        key = keys[pl.ds(k, 1), :]
        place = lax.shift_right_arithmetic(key, bits)
        bag = key & ((1 << bits) - 1)
        cat = bag // rows
        event = bag - cat * rows
        low = lax.shift_right_arithmetic(place, 8)
        high = place & (HI - 1)
        place_of = jnp.where(event_iota == event, 1.0, 0.0).astype(jnp.bfloat16)
        wide = jnp.dot(grad[...], place_of, preferred_element_type=jnp.float32)
        g = jnp.zeros((16, CHUNK), jnp.float32)
        for c in range(cats):
            g = g + jnp.where(cat == c, wide[c * 16 : (c + 1) * 16], 0.0)
        g = g.astype(jnp.bfloat16)
        zero = jnp.zeros_like(g)
        pick = jnp.where(hi_iota == high, 1.0, 0.0).astype(jnp.bfloat16)
        for b in range(0, lows, 16):
            n = min(16, lows - b)
            tall = jnp.concatenate([jnp.where(low == b + j, g, zero) for j in range(n)], axis=0)
            total[b * 16 : (b + n) * 16, :] += lax.dot_general(
                tall, pick, (((1,), (1,)), ((), ())), preferred_element_type=jnp.float32
            )
        return carry

    lax.fori_loop(0, chunks, body, 0)
    out[...] = total[...].astype(out.dtype)


def relay_own(mp, slot, send, recv):
    mine = lax.axis_index("mp")
    core = lax.rem(mine, 2)
    other = mine + 1 - 2 * core
    chips = mp // 2
    out = []
    for k in range(1, chips):
        to = lax.rem(mine + 2 * k, mp)
        copy = remote(slot(mine), slot(mine), send.at[2 * k], recv.at[2 * k], {"mp": to})
        copy.start()
        out.append(copy)
    copy = remote(slot(mine), slot(mine), send.at[1], recv.at[1], {"mp": other})
    copy.start()
    out.append(copy)
    return out


def relay_rest(mp, slot, send, recv, started):
    mine = lax.axis_index("mp")
    core = lax.rem(mine, 2)
    other = mine + 1 - 2 * core
    chips = mp // 2
    passed = []
    for k in range(1, chips):
        source = lax.rem(mine + mp - 2 * k, mp)
        remote(slot(source), slot(source), send.at[2 * k], recv.at[2 * k], {"mp": other}).wait_recv()
        copy = remote(slot(source), slot(source), send.at[2 * k + 1], recv.at[2 * k + 1], {"mp": other})
        copy.start()
        passed.append(copy)
    remote(slot(other), slot(other), send.at[1], recv.at[1], {"mp": other}).wait_recv()
    for k in range(1, chips):
        far = lax.rem(other + mp - 2 * k, mp)
        remote(slot(far), slot(far), send.at[2 * k + 1], recv.at[2 * k + 1], {"mp": other}).wait_recv()
    for copy in started + passed:
        copy.wait_send()


def nn(a, b):
    return jnp.dot(a, b, preferred_element_type=jnp.float32)


def nt(a, b):
    return lax.dot_general(a, b, (((1,), (1,)), ((), ())), preferred_element_type=jnp.float32)


def tn(a, b):
    return lax.dot_general(a, b, (((0,), (0,)), ((), ())), preferred_element_type=jnp.float32)


def sigmoid(x):
    return 0.5 * jnp.tanh(0.5 * x) + 0.5


def low(x):
    return x.astype(jnp.bfloat16)


def column_sum(x):
    return jnp.sum(x, axis=0, keepdims=True)


def widen_dense(dense, width):
    fields = dense.shape[1]
    row = lax.broadcasted_iota(jnp.int32, (fields, fields * width), 0)
    col = lax.broadcasted_iota(jnp.int32, (fields, fields * width), 1)
    ones = jnp.where(col // width == row, 1.0, 0.0)
    return jnp.dot(dense, ones, precision=lax.Precision.HIGHEST, preferred_element_type=jnp.float32)


def first_kernel(
    dp, mp, own_rows, bits,
    ids, lens, table, dense, num_row, gate_w, gate_b, n_first, n_gain, n_shift, b_first, b_gain, b_shift,
    t2, keys, numeric, gates, n1, b1, vec,
    scratch, gate_slots, n_slots, b_slots, v_slots, send, recv, send2, recv2,
):
    part = own_rows // mp
    blocks = part // HI
    tall = blocks * 16
    me, mine = lax.axis_index("dp"), lax.axis_index("mp")
    greet(dp, mp)
    own = table[:, pl.ds(pl.multiple_of(mine * part, HI), part)].astype(jnp.bfloat16)
    for b in range(blocks):
        t2[pl.ds(pl.multiple_of(me * tall + b * 16, 16), 16), :] = own[:, b * HI : (b + 1) * HI]

    def slot(i):
        return t2.at[pl.ds(pl.multiple_of(i * tall, 16), tall), :]

    copies = spread_dp(dp, slot, send, recv)
    gate_slots[mine] = gate_w[...]
    n_slots[mine] = n_first[...]
    b_slots[mine] = b_first[...]
    row = 0
    for ref in (gate_b, n_gain, n_shift, b_gain, b_shift):
        v_slots[mine, row : row + ref.shape[0], : ref.shape[1]] = ref[...]
        row += ref.shape[0]
    groups = []
    for i, ref in enumerate((gate_slots, n_slots, b_slots, v_slots)):
        started = relay_own(mp, lambda k, ref=ref: ref.at[k], send2.at[i], recv2.at[i])
        groups.append((ref, i, started))
    numeric[...] = low(widen_dense(dense[...], 16) * num_row[...])
    make_keys(ids, lens, scratch, own_rows, mp, bits)
    count = scratch.shape[0] // 8
    packed = compact_keys(scratch[...].reshape(count, 8, 128))
    keys[...] = jnp.transpose(packed.reshape(count * 8, 128))
    for ref, i, started in groups:
        relay_rest(mp, lambda k, ref=ref: ref.at[k], send2.at[i], recv2.at[i], started)
    cols, small, large = gate_w.shape[1], n_first.shape[0], b_first.shape[0]
    for m in range(mp):
        for k in range(2):
            gates[k, m * cols : (m + 1) * cols, :] = gate_slots[m, k]
        n1[m * small : (m + 1) * small, :] = n_slots[m]
        b1[m * large : (m + 1) * large, :] = b_slots[m]
    row = 0
    for ref in (gate_b, n_gain, n_shift, b_gain, b_shift):
        r, w = ref.shape
        vec[row : row + r, : mp * w] = jnp.concatenate(
            [v_slots[m, row : row + r, :w] for m in range(mp)], axis=1
        )
        row += r
    for copy in copies:
        copy.wait()


def own_columns(x, mine, width, mp):
    out = jnp.zeros((x.shape[0], width), x.dtype)
    for m in range(mp):
        out = jnp.where(mine == m, x[:, m * width : (m + 1) * width], out)
    return out


def dense_kernel(
    dp, mp, hx, batch,
    partial, numeric, gates, n1, b1, n_rest, b_rest, vec, left, right, pair, bias, labels, dense,
    logits, grads_t, p_out, q_out, small, n_gain_g, n_shift_g, b_gain_g, b_shift_g, left_g, right_g, bias_g,
    half_a, half_c, pooled, feat, gate, fields, own_term, grad_gate, n_slots, b_slots, n23, b2,
    yn, dn, yb, db, un, ub, gyn, gyb, pair_hi, pair_lo, pair_g, sums,
    fsend, frecv, wsend, wrecv, ssend, srecv,
):
    me, mine = lax.axis_index("dp"), lax.axis_index("mp")
    core = lax.rem(mine, 2)
    chip = mine // 2
    chips = mp // 2
    other = mine + 1 - 2 * core
    rows = feat.shape[0]
    block = 128
    steps = rows // block
    h1, h2 = n1.shape[0], b1.shape[0]
    s1, s2 = h1 // mp, h2 // mp
    wide = feat.shape[1]
    num = numeric.shape[1]
    gcols = wide // mp
    half = partial.shape[0] // 2
    greet(dp, mp)

    def rowset(i):
        return pl.ds(pl.multiple_of(i * block, block), block)

    def part(c):
        return pl.ds(pl.multiple_of(c * half, 16), half)

    copy_a = remote(partial.at[part(1 - core), :], half_a, fsend.at[0], frecv.at[0], {"mp": other})
    copy_a.start()
    n_slots[mine] = n_rest[...]
    b_slots[mine] = b_rest[...]
    copy_a.wait_recv()
    half_c[chip] = low(partial[part(core), :] + half_a[...])
    copies = []
    for k in range(1, chips):
        copy = remote(
            half_c.at[chip], half_c.at[chip], fsend.at[k], frecv.at[k],
            {"mp": lax.rem(mine + 2 * k, mp)},
        )
        copy.start()
        copies.append(copy)
    for i in range(0, h1, 80):
        row = lax.broadcasted_iota(jnp.int32, (80, h2), 0) + i
        col = lax.broadcasted_iota(jnp.int32, (80, h2), 1)
        pieces = jnp.concatenate([pair[i : i + 80, :]] * (h2 // 16), axis=1)
        spread = jnp.where(row // hx == col // 16, pieces, 0.0)
        high = low(spread)
        pair_hi[i : i + 80, :] = high
        pair_lo[i : i + 80, :] = low(spread - high.astype(jnp.float32))
    for copy in copies:
        copy.wait_recv()
    total = half_c[0].astype(jnp.float32)
    for k in range(1, chips):
        total = total + half_c[k].astype(jnp.float32)
    pooled[part(core), :] = low(total)
    copy_b = remote(
        pooled.at[part(core), :], pooled.at[part(core), :], fsend.at[chips], frecv.at[chips], {"mp": other}
    )
    copy_b.start()
    n_started = relay_own(mp, lambda k: n_slots.at[k], wsend.at[0], wrecv.at[0])
    b_started = relay_own(mp, lambda k: b_slots.at[k], wsend.at[1], wrecv.at[1])
    feat[:, :num] = numeric[...]
    copy_b.wait_recv()
    feat[:, num:] = low(jnp.transpose(pooled[...].astype(jnp.float32)))

    def push(slot):
        out = []
        for step in range(1, dp):
            copy = remote(
                sums.at[slot, me], sums.at[slot, me], ssend.at[slot, step - 1], srecv.at[slot, step - 1],
                {"dp": lax.rem(me + step, dp)},
            )
            copy.start()
            out.append(copy)
        return out

    def pull(slot, copies):
        for copy in copies:
            copy.wait_recv()
        total = sums[slot, 0]
        for d in range(1, dp):
            total = total + sums[slot, d]
        return total

    def put(slot, row, value):
        sums[slot, me, row : row + 1, : value.shape[1]] = value

    def norm(total, row, width):
        mean = total[row : row + 1, :width] / batch
        var = total[row + 1 : row + 2, :width] / batch - mean * mean
        return mean, lax.rsqrt(var + 1e-05)

    def activate(y_ref, d_ref, u_ref, layer, at, mean, rstd, gain, shift):
        normed = (y_ref[layer, at, :] - mean) * rstd
        z = gain * normed + shift
        s = sigmoid(z)
        u = z * s
        y_ref[layer, at, :] = normed
        d_ref[layer, at, :] = s + u * (1.0 - s)
        u = low(u)
        u_ref[layer, at, :] = u
        return u

    def gain_n(layer):
        return vec[2 + layer : 3 + layer, :h1], vec[5 + layer : 6 + layer, :h1]

    def gain_b(layer):
        return vec[8 + layer : 9 + layer, :h2], vec[10 + layer : 11 + layer, :h2]

    zero1 = jnp.zeros((1, h1), jnp.float32)
    zero2 = jnp.zeros((1, h2), jnp.float32)

    def forward_one(i, carry):
        a, b, c, d = carry
        at = rowset(i)
        x = feat[at, :]
        wide_x = x.astype(jnp.float32)
        for k in range(2):
            value = 2.0 * sigmoid(nt(x, gates[k]) + vec[k : k + 1, :wide])
            gate[k, at, :] = value
            fields[k, at, :] = low(wide_x * value)
        y = nt(fields[0, at, :], n1[...])
        yn[0, at, :] = y
        v = nt(fields[1, at, :], b1[...])
        yb[0, at, :] = v
        return a + column_sum(y), b + column_sum(y * y), c + column_sum(v), d + column_sum(v * v)

    stats = lax.fori_loop(0, steps, forward_one, (zero1, zero1, zero2, zero2))
    for r in range(4):
        put(0, r, stats[r])
    sent = [push(0)]
    relay_rest(mp, lambda k: n_slots.at[k], wsend.at[0], wrecv.at[0], n_started)
    relay_rest(mp, lambda k: b_slots.at[k], wsend.at[1], wrecv.at[1], b_started)
    for m in range(mp):
        for k in range(2):
            n23[k, m * s1 : (m + 1) * s1, :] = n_slots[m, k]
        b2[m * s2 : (m + 1) * s2, :] = b_slots[m]
    total = pull(0, sent[0])
    mean_n, rstd_n = norm(total, 0, h1)
    mean_b, rstd_b = norm(total, 2, h2)
    rstd_n1, rstd_b1 = rstd_n, rstd_b

    def forward_two(i, carry):
        a, b, c, d = carry
        at = rowset(i)
        u = activate(yn, dn, un, 0, at, mean_n, rstd_n, *gain_n(0))
        y = nt(u, n23[0])
        yn[1, at, :] = y
        u = activate(yb, db, ub, 0, at, mean_b, rstd_b, *gain_b(0))
        v = nt(u, b2[...])
        yb[1, at, :] = v
        return a + column_sum(y), b + column_sum(y * y), c + column_sum(v), d + column_sum(v * v)

    stats = lax.fori_loop(0, steps, forward_two, (zero1, zero1, zero2, zero2))
    for r in range(4):
        put(1, r, stats[r])
    sent.append(push(1))
    total = pull(1, sent[1])
    mean_n2, rstd_n2 = norm(total, 0, h1)
    mean_b2, rstd_b2 = norm(total, 2, h2)

    def forward_three(i, carry):
        a, b = carry
        at = rowset(i)
        u = activate(yn, dn, un, 1, at, mean_n2, rstd_n2, *gain_n(1))
        y = nt(u, n23[1])
        yn[2, at, :] = y
        return a + column_sum(y), b + column_sum(y * y)

    stats = lax.fori_loop(0, steps, forward_three, (zero1, zero1))
    for r in range(2):
        put(2, r, stats[r])
    sent.append(push(2))

    def broad_out(i, carry):
        activate(yb, db, ub, 1, rowset(i), mean_b2, rstd_b2, *gain_b(1))
        return carry

    lax.fori_loop(0, steps, broad_out, 0)
    pair_g[...] = jnp.zeros_like(pair_g)
    label = jnp.transpose(jnp.broadcast_to(labels[...].astype(jnp.float32), (8, rows)))[:, 0:1]
    own_term[:, 0:1] = label
    total = pull(2, sent[2])
    mean_n3, rstd_n3 = norm(total, 0, h1)

    def join(i, carry):
        l_sum, r_sum, g_sum, a, b, c, d = carry
        at = rowset(i)
        first = activate(yn, dn, un, 2, at, mean_n3, rstd_n3, *gain_n(2))
        second = ub[1, at, :]
        turned = nn(first, pair_hi[...]) + nn(first, pair_lo[...])
        first32, second32 = first.astype(jnp.float32), second.astype(jnp.float32)
        to_second = right[...] + turned
        logit = (
            jnp.sum(first32 * left[...], axis=1, keepdims=True)
            + jnp.sum(second32 * to_second, axis=1, keepdims=True)
            + bias[...]
        )
        g = sigmoid(logit) - own_term[at, 0:1]
        own_term[at, 1:2] = logit
        back = nt(second, pair_hi[...]) + nt(second, pair_lo[...])
        weighted = g * first32
        l_sum = l_sum + column_sum(weighted)
        r_sum = r_sum + column_sum(g * second32)
        g_sum = g_sum + column_sum(g)
        pair_g[...] += tn(second, low(weighted))
        gz = g * (left[...] + back) * dn[2, at, :]
        dn[2, at, :] = gz
        a = a + column_sum(gz)
        b = b + column_sum(gz * yn[2, at, :])
        gz = g * to_second * db[1, at, :]
        db[1, at, :] = gz
        c = c + column_sum(gz)
        d = d + column_sum(gz * yb[1, at, :])
        return l_sum, r_sum, g_sum, a, b, c, d

    l_sum, r_sum, g_sum, a, b, c, d = lax.fori_loop(
        0, steps, join, (zero1, zero2, jnp.zeros((1, 1), jnp.float32), zero1, zero1, zero2, zero2)
    )
    for r, value in enumerate((a, b, c, d)):
        put(3, r, value)
    sent.append(push(3))
    for r, value in enumerate((l_sum, r_sum, g_sum)):
        put(6, r, value)
    join_sent = push(6)
    logits[...] = jnp.transpose(own_term[:, 0:128])[1:2, :]

    def own_part(x, width):
        full = x.shape[1]
        pad = -(-width // 128) * 128
        row = lax.broadcasted_iota(jnp.int32, (full, pad), 0)
        col = lax.broadcasted_iota(jnp.int32, (full, pad), 1)
        choose = jnp.where((row == col + mine * width) & (col < width), 1.0, 0.0).astype(jnp.bfloat16)
        return low(nn(x, choose))

    def weight_grad(grad_y, inputs, width):
        return low(tn(own_part(grad_y, width), inputs)[:width, :])

    def up16(x):
        return -(-x // 16) * 16

    g_rows, n_rows, b_rows = up16(gcols), up16(s1), up16(s2)
    p_out[...] = jnp.zeros_like(p_out)
    q_out[...] = jnp.zeros_like(q_out)
    folded = jnp.zeros((16, h1), jnp.float32)
    col = lax.broadcasted_iota(jnp.int32, (16, h1), 1)
    for h in range(h2 // 16):
        folded = folded + jnp.where(col // hx == h, pair_g[h * 16 : (h + 1) * 16, :], 0.0)
    q_out[n_rows + b_rows : n_rows + b_rows + 16, :h1] = low(folded)

    total = pull(3, sent[3])

    def grad_y(gz, normed, rstd, gain, total_rows):
        return low(gain * rstd * (gz - total_rows[0:1] / batch - normed * (total_rows[1:2] / batch)))

    t_n3, t_b2 = total[0:2, :h1], total[2:4, :h2]

    def back_one(i, carry):
        a, b, c, d = carry
        at = rowset(i)
        g = grad_y(dn[2, at, :], yn[2, at, :], rstd_n3, gain_n(2)[0], t_n3)
        gyn[2, at, :] = g
        gz = nn(g, n23[1]) * dn[1, at, :]
        dn[1, at, :] = gz
        a, b = a + column_sum(gz), b + column_sum(gz * yn[1, at, :])
        g = grad_y(db[1, at, :], yb[1, at, :], rstd_b2, gain_b(1)[0], t_b2)
        gyb[1, at, :] = g
        gz = nn(g, b2[...]) * db[0, at, :]
        db[0, at, :] = gz
        c, d = c + column_sum(gz), d + column_sum(gz * yb[0, at, :])
        return a, b, c, d

    stats = lax.fori_loop(0, steps, back_one, (zero1, zero1, zero2, zero2))
    for r in range(4):
        put(4, r, stats[r])
    sent.append(push(4))
    q_out[:s1, h1 : 2 * h1] = weight_grad(gyn[2], un[1], s1)
    q_out[n_rows : n_rows + s2, :] = weight_grad(gyb[1], ub[0], s2)
    total = pull(4, sent[4])
    t_n2, t_b1 = total[0:2, :h1], total[2:4, :h2]

    def back_two(i, carry):
        a, b = carry
        at = rowset(i)
        g = grad_y(dn[1, at, :], yn[1, at, :], rstd_n2, gain_n(1)[0], t_n2)
        gyn[1, at, :] = g
        gz = nn(g, n23[0]) * dn[0, at, :]
        dn[0, at, :] = gz
        return a + column_sum(gz), b + column_sum(gz * yn[0, at, :])

    stats = lax.fori_loop(0, steps, back_two, (zero1, zero1))
    for r in range(2):
        put(5, r, stats[r])
    sent.append(push(5))

    def gate_back(k, at, grad):
        x = feat[at, :].astype(jnp.float32)
        value = gate[k, at, :]
        g = low(grad * x * value * (1.0 - 0.5 * value))
        grad_gate[k, at, :] = g
        return grad * value, g

    def back_broad(i, carry):
        at = rowset(i)
        g = grad_y(db[0, at, :], yb[0, at, :], rstd_b1, gain_b(0)[0], t_b1)
        gyb[0, at, :] = g
        term, _ = gate_back(1, at, nn(g, b1[...]))
        own_term[at, :] = term
        return carry

    lax.fori_loop(0, steps, back_broad, 0)
    q_out[:s1, :h1] = weight_grad(gyn[1], un[0], s1)
    p_out[2 * g_rows + n_rows : 2 * g_rows + n_rows + s2, :] = weight_grad(gyb[0], fields[1], s2)
    p_out[g_rows : g_rows + gcols, :] = weight_grad(grad_gate[1], feat[...], gcols)
    total = pull(5, sent[5])
    t_n1 = total[0:2, :h1]

    def back_narrow(i, carry):
        ga, gb, ne = carry
        at = rowset(i)
        g = grad_y(dn[0, at, :], yn[0, at, :], rstd_n1, gain_n(0)[0], t_n1)
        gyn[0, at, :] = g
        term, g0 = gate_back(0, at, nn(g, n1[...]))
        g1 = grad_gate[1, at, :]
        whole = nn(g0, gates[0]) + nn(g1, gates[1]) + term + own_term[at, :]
        whole = low(whole).astype(jnp.float32)
        own_term[at, :] = whole
        ne = ne + column_sum(whole[:, :num] * widen_dense(dense[at, :], 16))
        return ga + column_sum(g0.astype(jnp.float32)), gb + column_sum(g1.astype(jnp.float32)), ne

    zero_g = jnp.zeros((1, wide), jnp.float32)
    ga, gb, ne = lax.fori_loop(
        0, steps, back_narrow, (zero_g, zero_g, jnp.zeros((1, num), jnp.float32))
    )
    grads_t[...] = low(jnp.transpose(own_term[:, num:]))
    p_out[:gcols, :] = weight_grad(grad_gate[0], feat[...], gcols)
    p_out[2 * g_rows : 2 * g_rows + s1, :] = weight_grad(gyn[0], fields[0], s1)
    small[...] = jnp.zeros_like(small)
    small[0:1, :gcols] = own_columns(ga, mine, gcols, mp)
    small[1:2, :gcols] = own_columns(gb, mine, gcols, mp)
    small[2:3, :num] = ne
    for layer, t in enumerate((t_n1, t_n2, t_n3)):
        n_shift_g[layer : layer + 1, :] = own_columns(t[0:1], mine, s1, mp)
        n_gain_g[layer : layer + 1, :] = own_columns(t[1:2], mine, s1, mp)
    for layer, t in enumerate((t_b1, t_b2)):
        b_shift_g[layer : layer + 1, :] = own_columns(t[0:1], mine, s2, mp)
        b_gain_g[layer : layer + 1, :] = own_columns(t[1:2], mine, s2, mp)
    total = pull(6, join_sent)
    left_g[...] = total[0:1, :h1]
    right_g[...] = total[1:2, :h2]
    bias_g[...] = total[2:3, 0:1]
    copy_a.wait_send()
    copy_b.wait_send()
    for copy in copies:
        copy.wait_send()
    for group in sent + [join_sent]:
        for copy in group:
            copy.wait_send()


def reduce_kernel(
    dp, mp,
    grads, p_in, q_in, small,
    table_g, gate_g, n_first_g, n_rest_g, b_first_g, b_rest_g, pair_g, small_out,
    landed, shares, s_slots, p_work, q_work, p_land, q_land, p_full, q_full,
    send, recv, send2, recv2, send3, recv3, psend, precv,
):
    tall = grads.shape[0] // dp
    me, mine = lax.axis_index("dp"), lax.axis_index("mp")
    greet(dp, mp)
    levels = dp.bit_length() - 1
    orders = (list(range(levels)), list(range(1, levels)) + [0])
    p_work[...] = p_in[...]
    q_work[...] = q_in[...]
    s_slots[me] = small[...]
    works = (p_work, q_work)
    lands = (p_land, q_land)
    fulls = (p_full, q_full)
    starts = [0, 0]
    sizes = [p_work.shape[0], q_work.shape[0]]
    waits = []

    def flip(bit):
        return me + (1 << bit) - 2 * (1 << bit) * lax.rem(me // (1 << bit), 2)

    def halve(w, level):
        bit = orders[w][level]
        size = sizes[w] // 2
        up = lax.rem(me // (1 << bit), 2)
        keep = starts[w] + up * size
        give = starts[w] + (1 - up) * size
        offset = works[w].shape[0] - 2 * size
        where = pl.ds(offset, size)
        copy = remote(
            works[w].at[pl.ds(pl.multiple_of(give, 16), size), :], lands[w].at[where, :],
            psend.at[w, level], precv.at[w, level], {"dp": flip(bit)},
        )
        copy.start()
        starts[w], sizes[w] = keep, size
        return copy, where

    def add(w, copy, where):
        copy.wait_recv()
        at = pl.ds(pl.multiple_of(starts[w], 16), sizes[w])
        works[w][at, :] = low(
            works[w][at, :].astype(jnp.float32) + lands[w][where, :].astype(jnp.float32)
        )
        waits.append(copy)

    def double(w, level):
        bit = orders[w][level]
        at = fulls[w].at[pl.ds(pl.multiple_of(starts[w], 16), sizes[w]), :]
        copy = remote(at, at, psend.at[w, levels + level], precv.at[w, levels + level], {"dp": flip(bit)})
        copy.start()
        up = lax.rem(me // (1 << bit), 2)
        starts[w] = starts[w] - up * sizes[w]
        sizes[w] = sizes[w] * 2
        return copy

    pend = [halve(w, 0) for w in (0, 1)]
    copies = []
    for step in range(1, dp):
        to = lax.rem(me + step, dp)
        copy = remote(
            grads.at[pl.ds(pl.multiple_of(to * tall, 16), tall), :],
            landed.at[step - 1], send.at[step - 1], recv.at[step - 1], {"dp": to},
        )
        copy.start()
        copies.append(copy)
    small_copies = spread_dp(dp, lambda k: s_slots.at[k], send3, recv3)
    for level in range(1, levels):
        for w in (0, 1):
            add(w, *pend[w])
            pend[w] = halve(w, level)
    total = grads[pl.ds(pl.multiple_of(me * tall, 16), tall), :].astype(jnp.float32)
    for step in range(1, dp):
        copies[step - 1].wait_recv()
        total = total + landed[step - 1].astype(jnp.float32)
    shares[mine] = total.astype(jnp.bfloat16)

    def slot(i):
        return shares.at[i]

    started = relay_own(mp, slot, send2, recv2)
    back = []
    for w in (0, 1):
        add(w, *pend[w])
        at = pl.ds(pl.multiple_of(starts[w], 16), sizes[w])
        fulls[w][at, :] = works[w][at, :]
        back.append(double(w, levels - 1))
    relay_rest(mp, slot, send2, recv2, started)
    blocks = tall // 16
    for m in range(mp):
        for b in range(blocks):
            table_g[:, (m * blocks + b) * HI : (m * blocks + b + 1) * HI] = shares[
                m, b * 16 : (b + 1) * 16, :
            ].astype(jnp.float32)
    for level in range(levels - 2, -1, -1):
        for w in (0, 1):
            back[w].wait_recv()
            waits.append(back[w])
            back[w] = double(w, level)
    for copy in small_copies:
        copy.wait_recv()
    value = s_slots[0]
    for d in range(1, dp):
        value = value + s_slots[d]
    small_out[...] = value
    for w in (0, 1):
        back[w].wait_recv()
        waits.append(back[w])
    def up16(x):
        return -(-x // 16) * 16

    gcols, s1, s2, h1 = gate_g.shape[1], n_first_g.shape[0], b_first_g.shape[0], n_rest_g.shape[2]
    g_rows, n_rows, b_rows = up16(gcols), up16(s1), up16(s2)

    def full(work, row, count, col, width):
        return work[row : row + count, col : col + width].astype(jnp.float32)

    wide = n_first_g.shape[1]
    gate_g[0] = full(p_full, 0, gcols, 0, wide)
    gate_g[1] = full(p_full, g_rows, gcols, 0, wide)
    n_first_g[...] = full(p_full, 2 * g_rows, s1, 0, wide)
    b_first_g[...] = full(p_full, 2 * g_rows + n_rows, s2, 0, wide)
    n_rest_g[0] = full(q_full, 0, s1, 0, h1)
    n_rest_g[1] = full(q_full, 0, s1, h1, h1)
    b_rest_g[...] = full(q_full, n_rows, s2, 0, 2 * h1)
    pair_g[...] = jnp.transpose(full(q_full, n_rows + b_rows, 16, 0, 512))[:h1, :]
    for copy in copies + small_copies + waits:
        copy.wait_send()


def f32(*shape):
    return jax.ShapeDtypeStruct(shape, jnp.float32)


def b16(*shape):
    return jax.ShapeDtypeStruct(shape, jnp.bfloat16)


def held(*shape):
    return pltpu.VMEM(shape, jnp.float32)


def held16(*shape):
    return pltpu.VMEM(shape, jnp.bfloat16)


def dma(*shape):
    return pltpu.SemaphoreType.DMA(shape)


def shards(
    dense_values,
    field_ids,
    lengths,
    labels,
    num_embed,
    embed_table,
    gate_weight,
    gate_bias,
    narrow_first,
    narrow_rest,
    narrow_gain,
    narrow_shift,
    broad_first,
    broad_rest,
    broad_gain,
    broad_shift,
    joining_left,
    joining_right,
    joining_pair,
    joining_bias,
):
    dp, mp = lax.axis_size("dp"), lax.axis_size("mp")
    chips = mp // 2
    rows = dense_values.shape[0]
    cats, slots = field_ids.shape[:2]
    width, own_rows = embed_table.shape
    num = dense_values.shape[1] * width
    wide = gate_weight.shape[2]
    gcols = gate_weight.shape[1]
    s1, s2 = narrow_first.shape[0], broad_first.shape[0]
    h1, h2 = s1 * mp, s2 * mp
    hx = joining_pair.shape[1]
    bits = (cats * rows - 1).bit_length()
    tall = own_rows // mp // HI * 16
    vregs = 1 << (-(-(cats * slots * rows) // 1024) - 1).bit_length()
    t2, keys, numeric, gates, n1, b1, vec = pl.pallas_call(
        functools.partial(first_kernel, dp, mp, own_rows, bits),
        out_shape=(
            b16(dp * tall, HI),
            jax.ShapeDtypeStruct((128, vregs * 8), jnp.int32),
            b16(rows, num),
            b16(2, wide, wide),
            b16(h1, wide),
            b16(h2, wide),
            f32(16, 896),
        ),
        in_specs=[VM] * 13,
        out_specs=(VM,) * 7,
        scratch_shapes=[
            pltpu.VMEM((vregs * 8, 128), jnp.int32),
            held16(mp, 2, gcols, wide),
            held16(mp, s1, wide),
            held16(mp, s2, wide),
            held(mp, 16, 256),
            dma(dp - 1),
            dma(dp - 1),
            dma(4, mp),
            dma(4, mp),
        ],
        compiler_params=params(0),
        name="first",
    )(
        field_ids, lengths, embed_table, dense_values, num_embed.reshape(1, num), gate_weight, gate_bias,
        narrow_first, narrow_gain, narrow_shift, broad_first, broad_gain, broad_shift,
    )
    partial = pl.pallas_call(
        functools.partial(lookup_kernel, cats, rows, bits),
        out_shape=f32(cats * 16, rows),
        in_specs=[VM] * 2,
        out_specs=VM,
        scratch_shapes=[held(cats * 16, rows)],
        compiler_params=params(None),
        name="lookup",
    )(keys, t2)

    def up(x, n):
        return -(-x // n) * n

    p_rows = up(2 * up(gcols, 16) + up(s1, 16) + up(s2, 16), 16 * dp)
    q_rows = up(up(s1, 16) + up(s2, 16) + 16, 16 * dp)
    (
        logits, grads_t, p_part, q_part, small,
        n_gain_g, n_shift_g, b_gain_g, b_shift_g, left_g, right_g, bias_g,
    ) = pl.pallas_call(
        functools.partial(dense_kernel, dp, mp, hx, float(rows * dp)),
        out_shape=(
            f32(1, rows),
            b16(cats * 16, rows),
            b16(p_rows, wide),
            b16(q_rows, h2),
            f32(8, 256),
            f32(3, s1),
            f32(3, s1),
            f32(2, s2),
            f32(2, s2),
            f32(1, h1),
            f32(1, h2),
            f32(1, 1),
        ),
        in_specs=[VM] * 14,
        out_specs=(VM,) * 12,
        scratch_shapes=[
            held(cats * 8, rows),
            held16(chips, cats * 8, rows),
            held16(cats * 16, rows),
            held16(rows, wide),
            held(2, rows, wide),
            held16(2, rows, wide),
            held(rows, wide),
            held16(2, rows, wide),
            held16(mp, 2, s1, h1),
            held16(mp, s2, h2),
            held16(2, h1, h1),
            held16(h2, h2),
            held(3, rows, h1),
            held(3, rows, h1),
            held(2, rows, h2),
            held(2, rows, h2),
            held16(3, rows, h1),
            held16(2, rows, h2),
            held16(3, rows, h1),
            held16(2, rows, h2),
            held16(h1, h2),
            held16(h1, h2),
            held(h2, h1),
            held(7, dp, 4, 896),
            dma(chips + 1),
            dma(chips + 1),
            dma(2, mp),
            dma(2, mp),
            dma(7, dp - 1),
            dma(7, dp - 1),
        ],
        compiler_params=params(1, 60),
        name="dense",
    )(
        partial, numeric, gates, n1, b1, narrow_rest, broad_rest, vec,
        joining_left.reshape(1, h1), joining_right.reshape(1, h2), joining_pair.reshape(h1, width),
        joining_bias.reshape(1, 1), labels.reshape(1, rows), dense_values,
    )
    row_sums = pl.pallas_call(
        functools.partial(scatter_kernel, cats, rows, bits),
        out_shape=b16(dp * tall, HI),
        in_specs=[VM] * 2,
        out_specs=VM,
        scratch_shapes=[held(dp * tall, HI)],
        compiler_params=params(None),
        name="scatter",
    )(keys, grads_t)
    (
        embed_table_grad, gate_weight_grad, narrow_first_grad, narrow_rest_grad,
        broad_first_grad, broad_rest_grad, pair_g, small,
    ) = pl.pallas_call(
        functools.partial(reduce_kernel, dp, mp),
        out_shape=(
            f32(width, own_rows),
            f32(2, gcols, wide),
            f32(s1, wide),
            f32(2, s1, h1),
            f32(s2, wide),
            f32(s2, h2),
            f32(h1, width),
            f32(8, 256),
        ),
        in_specs=[VM] * 4,
        out_specs=(VM,) * 8,
        scratch_shapes=[
            held16(dp - 1, tall, HI),
            held16(mp, tall, HI),
            held(dp, 8, 256),
            held16(p_rows, wide),
            held16(q_rows, h2),
            held16(p_rows, wide),
            held16(q_rows, h2),
            held16(p_rows, wide),
            held16(q_rows, h2),
            dma(dp - 1),
            dma(dp - 1),
            dma(mp),
            dma(mp),
            dma(dp - 1),
            dma(dp - 1),
            dma(2, 2 * (dp.bit_length() - 1)),
            dma(2, 2 * (dp.bit_length() - 1)),
        ],
        compiler_params=params(2),
        name="reduce",
    )(row_sums, p_part, q_part, small)
    return (
        logits.reshape(rows),
        small[2, :num].reshape(-1, width),
        embed_table_grad,
        gate_weight_grad,
        small[:2, :gcols],
        narrow_first_grad,
        narrow_rest_grad,
        n_gain_g,
        n_shift_g,
        broad_first_grad,
        broad_rest_grad,
        b_gain_g,
        b_shift_g,
        left_g.reshape(h1),
        right_g.reshape(h2),
        pair_g.reshape(joining_pair.shape),
        bias_g.reshape(1),
    )


def solution(mesh):
    placed = (
        P("dp", None),
        P(None, None, "dp"),
        P(None, "dp"),
        P("dp"),
        P(),
        P(None, "dp"),
        P(None, "mp", None),
        P(None, "mp"),
        P("mp", None),
        P(None, "mp", None),
        P(None, "mp"),
        P(None, "mp"),
        P("mp", None),
        P("mp", None),
        P(None, "mp"),
        P(None, "mp"),
        P(),
        P(),
        P(),
        P(),
    )
    return jax.shard_map(
        shards,
        mesh=mesh,
        in_specs=placed,
        out_specs=(
            P("dp"),
            P(),
            P(None, "dp"),
            P(None, "mp", None),
            P(None, "mp"),
            P("mp", None),
            P(None, "mp", None),
            P(None, "mp"),
            P(None, "mp"),
            P("mp", None),
            P("mp", None),
            P(None, "mp"),
            P(None, "mp"),
            P(),
            P(),
            P(),
            P(),
        ),
        check_vma=False,
    )
```

time: 501 us -> 216 us (0.43)
  blocking collectives: 304 us -> 0 us
  Pallas kernels: 53.1 us -> 178 us
  waiting for transfers between devices: 35.6 us -> 0 us
  matrix products: 27.8 us -> 0 us
  other arithmetic: 22.2 us -> 1.35 us
  between operations: 16.5 us -> 3.5 us
  starting transfers between devices: 8.84 us -> 0 us
    psum x9 -> x0, blocking collectives: 212 us -> none  [the longest x3 57.8 us: layer_forward(): lax.psum((jnp.sum(hidden, axis=0), jnp.sum(hidden * hidden, axis=0)), 'dp')]
    pallas_call x4 -> x5, Pallas kernels: 53.1 us -> 178 us  [the longest x1 70.6 us: shards(): pl.pallas_call(functools.partial(dense_kernel, dp, mp, hx, float(rows * d...]
    unnamed x3 -> x0, blocking collectives: 55.3 us -> none
    all_gather x5 -> x0, blocking collectives: 37.2 us -> none  [layer_forward(): lax.all_gather(active, 'mp', axis=1, tiled=True)]
    dot_general x23 -> x0, matrix products: 27.8 us -> none  [the longest x5 9.22 us: layer_backward(): lax.dot_general(grad_hidden, inputs, (((0,), (0,)), ((), ())), preferred_...]
    psum x1 -> x0, waiting for transfers between devices: 19.3 us -> none  [shards(): lax.psum((joining_left_grad, joining_right_grad, joining_pair_grad, joini...]
    all_gather x1 -> x0, waiting for transfers between devices: 15.2 us -> none  [shards(): fields = lax.all_gather(fields_part, 'mp', axis=2, tiled=True)]
    reduce_sum x10 -> x0, other arithmetic: 11.8 us -> none  [the longest x5 9.24 us: layer_backward(): jnp.sum(grad_shaped, axis=0)]
  transfers between devices with their start and end apart: 7 -> 0, of which waited for: 4 -> 0; matrix products, arithmetic and copies ran while one was open for 8% -> 0% of each run, Pallas kernels for 6% -> 0%
where the time goes in v2:
time: 216 us; the launch traced here: 214 us
  Pallas kernels  178 us (82%)
  local copies, waits for them, and re-layouts  30.7 us (14%)
  between operations  3.5 us (2%)
    pallas_call x1, Pallas kernels, shards(): pl.pallas_call(functools.partial(dense_kernel, dp, mp, hx, float(rows * d...  70.6 us
    pallas_call x1, Pallas kernels, shards(): pl.pallas_call(functools.partial(reduce_kernel, dp, mp), out_shape=(f32(w...  56.8 us
    pallas_call x1, Pallas kernels, shards(): pl.pallas_call(functools.partial(first_kernel, dp, mp, own_rows, bits), o...  28.3 us
    unnamed x79, local copies, waits for them, and re-layouts  27.4 us
    pallas_call x1, Pallas kernels, shards(): pl.pallas_call(functools.partial(lookup_kernel, cats, rows, bits), out_sh...  11.2 us
    pallas_call x1, Pallas kernels, shards(): pl.pallas_call(functools.partial(scatter_kernel, cats, rows, bits), out_s...  11.2 us

profile of v2, /device:TPU:0, one launch (start us, length us, event | category | flops | bytes accessed | tf_op | source)
XLA Modules:
  0.0 213.7 jit_solution(14581724631874379832)
XLA Ops:
  1.5 0.8 reshape.67.num_row
  2.3 1.3 reshape.69.right
  3.6 1.7 copy.39
  5.3 1.6 copy.40.n_rest
  6.9 0.9 copy.37.dense
  7.8 1.1 copy.38.gate_w
  9.0 28.3 %first.1 = (bf16[1024,256]{1,0:T(8,128)(2,1)S(1)}, s32[128,512]{1,0:T(8,128)S(1)}, bf16[512,208]{1,0:T(8,128)(2,1)S(1)}, bf16[2,624,624]{2,1,0:T(8,128)(2,1)S(1)...) custom-call(s32[26,4,512]{2,1,0:T(4,128)S(1)} %copy-done.14, ...), custom_call_target="tpu_custom_call" | custom-call | tf_op jit(solution)/shard_map/first/pallas_call | solution.py:890
  37.4 1.2 copy-done.2
  38.6 1.0 copy-done.3
  39.6 0.8 copy-done.7
  41.7 11.2 %lookup.1.partial = f32[416,512]{1,0:T(8,128)S(1)} custom-call(s32[128,512]{1,0:T(8,128)S(1)} %get-tuple-element.44.keys, bf16[1024,256]{1,0:T(8,128)(2,1)S(1)} %get-tuple-element.45.t2), custom_call_target="tpu_custom_call" | custom-call | tf_op jit(solution)/shard_map/lookup/pallas_call | solution.py:920
  52.9 0.9 copy-done
  53.8 70.6 %dense.3 = (f32[1,512]{1,0:T(1,128)}, bf16[416,512]{1,0:T(8,128)(2,1)}, bf16[640,624]{1,0:T(8,128)(2,1)}, bf16[384,800]{1,0:T(8,128)(2,1)}, f32[8,256]{1,0:T(8,1...) custom-call(f32[416,512]{1,0:T(8,128)} %copy-done, ...), custom_call_target="tpu_custom_call" | custom-call | tf_op jit(solution)/shard_map/dense/pallas_call | solution.py:938
  124.4 1.4 reduce.2
  125.8 1.0 copy-done.9
  126.8 11.2 %scatter.1.grads = bf16[1024,256]{1,0:T(8,128)(2,1)S(1)} custom-call(s32[128,512]{1,0:T(8,128)S(1)} %get-tuple-element.44.keys, bf16[416,512]{1,0:T(8,128)(2,1)S(1)} %copy-done.9), custom_call_target="tpu_custom_call" | custom-call | tf_op jit(solution)/shard_map/scatter/pallas_call | solution.py:995
  138.0 1.1 copy-done.5
  139.8 56.8 %reduce.6 = (f32[16,8192]{1,0:T(8,128)S(1)}, f32[2,156,624]{2,1,0:T(8,128)S(1)}, f32[100,624]{1,0:T(8,128)S(1)}, f32[2,100,400]{2,1,0:T(8,128)S(1)}, f32[200,624...) custom-call(bf16[1024,256]{1,0:T(8,128)(2,1)S(1)} %scatter.1.grads, ...), custom_call_target="tpu_custom_call" | custom-call | tf_op jit(solution)/shard_map/reduce/pallas_call | solution.py:1007
  200.0 1.7 copy.44
  201.7 2.1 copy.43
  203.8 1.5 copy.42
  205.9 0.8 copy.58
  208.5 0.8 copy.62
  209.3 0.9 copy.63
  (66 shorter events, 9.7 us)
Async XLA Ops:
  0.7 8.3 %copy-start.24 = (f32[2,200]{1,0:T(2,128)S(1)}, f32[2,200]{1,0:T(2,128)}, u32[]{:S(2)}) copy-start(f32[2,200]{1,0:T(2,128)} %b_shift.1) | copy-start | bytes 4804
  0.7 8.3 %copy-start.23 = (f32[2,200]{1,0:T(2,128)S(1)}, f32[2,200]{1,0:T(2,128)}, u32[]{:S(2)}) copy-start(f32[2,200]{1,0:T(2,128)} %b_gain.1) | copy-start | bytes 4804
  0.7 8.3 %copy-start.13 = (bf16[200,624]{1,0:T(8,128)(2,1)S(1)}, bf16[200,624]{1,0:T(8,128)(2,1)}, u32[]{:S(2)}) copy-start(bf16[200,624]{1,0:T(8,128)(2,1)} %b_first.1) | copy-start | bytes 748804
  0.7 8.3 %copy-start.22 = (f32[3,100]{1,0:T(4,128)S(1)}, f32[3,100]{1,0:T(4,128)}, u32[]{:S(2)}) copy-start(f32[3,100]{1,0:T(4,128)} %n_shift.1) | copy-start | bytes 3604
  0.7 8.3 %copy-start.21 = (f32[3,100]{1,0:T(4,128)S(1)}, f32[3,100]{1,0:T(4,128)}, u32[]{:S(2)}) copy-start(f32[3,100]{1,0:T(4,128)} %n_gain.1) | copy-start | bytes 3604
  0.7 8.3 %copy-start.16 = (bf16[100,624]{1,0:T(8,128)(2,1)S(1)}, bf16[100,624]{1,0:T(8,128)(2,1)}, u32[]{:S(2)}) copy-start(bf16[100,624]{1,0:T(8,128)(2,1)} %n_first.1) | copy-start | bytes 374404
  0.7 8.3 %copy-start.20 = (f32[2,156]{1,0:T(2,128)S(1)}, f32[2,156]{1,0:T(2,128)}, u32[]{:S(2)}) copy-start(f32[2,156]{1,0:T(2,128)} %gate_b.1) | copy-start | bytes 3748
  0.7 8.3 %copy-start.6 = (f32[16,8192]{1,0:T(8,128)S(1)}, f32[16,8192]{1,0:T(8,128)}, u32[]{:S(2)}) copy-start(f32[16,8192]{1,0:T(8,128)} %table.1) | copy-start | bytes 1572868
  0.7 8.3 %copy-start.17 = (s32[26,512]{1,0:T(8,128)S(1)}, s32[26,512]{1,0:T(8,128)}, u32[]{:S(2)}) copy-start(s32[26,512]{1,0:T(8,128)} %lens.1) | copy-start | bytes 159748
  0.7 8.3 %copy-start.14 = (s32[26,4,512]{2,1,0:T(4,128)S(1)}, s32[26,4,512]{2,1,0:T(4,128)}, u32[]{:S(2)}) copy-start(s32[26,4,512]{2,1,0:T(4,128)} %ids.1) | copy-start | bytes 638980
  7.8 45.1 %copy-start.1 = (f32[512,13]{1,0:T(8,128)}, f32[512,13]{1,0:T(8,128)S(1)}, u32[]{:S(2)}) copy-start(f32[512,13]{1,0:T(8,128)S(1)} %copy.37.dense) | copy-start | bytes 79876
  37.4 1.2 copy-start.2
  38.6 1.0 copy-start.3
  52.9 0.9 copy-start
  124.4 13.5 %copy-start.4 = (bf16[640,624]{1,0:T(8,128)(2,1)S(1)}, bf16[640,624]{1,0:T(8,128)(2,1)}, u32[]{:S(2)}) copy-start(bf16[640,624]{1,0:T(8,128)(2,1)} %get-tuple-element.53.p_in) | copy-start | bytes 2396164
  125.8 1.0 copy-start.9
  138.0 1.1 copy-start.5
  198.7 6.6 %copy-start.30 = (f32[1,512]{1,0:T(1,128)S(1)}, f32[1,512]{1,0:T(1,128)}, u32[]{:S(2)}) copy-start(f32[1,512]{1,0:T(1,128)} %get-tuple-element.51) | copy-start | bytes 6148
  201.6 5.0 %copy-start.11 = (f32[100,624]{1,0:T(8,128)S(1)}, f32[100,624]{1,0:T(8,128)}, u32[]{:S(2)}) copy-start(f32[100,624]{1,0:T(8,128)} %copy-done.10) | copy-start | bytes 748804
  203.8 3.6 %copy-start.29 = (f32[3,100]{1,0:T(4,128)S(1)}, f32[3,100]{1,0:T(4,128)}, u32[]{:S(2)}) copy-start(f32[3,100]{1,0:T(4,128)} %get-tuple-element.112) | copy-start | bytes 3604
  203.8 4.2 %copy-start.28 = (f32[3,100]{1,0:T(4,128)S(1)}, f32[3,100]{1,0:T(4,128)}, u32[]{:S(2)}) copy-start(f32[3,100]{1,0:T(4,128)} %get-tuple-element.113) | copy-start | bytes 3604
  206.7 3.5 %copy-start.27 = (f32[2,200]{1,0:T(2,128)S(1)}, f32[2,200]{1,0:T(2,128)}, u32[]{:S(2)}) copy-start(f32[2,200]{1,0:T(2,128)} %get-tuple-element.116) | copy-start | bytes 4804
  206.7 4.1 %copy-start.26 = (f32[2,200]{1,0:T(2,128)S(1)}, f32[2,200]{1,0:T(2,128)}, u32[]{:S(2)}) copy-start(f32[2,200]{1,0:T(2,128)} %get-tuple-element.117) | copy-start | bytes 4804
  206.7 4.7 %copy-start.25 = (f32[1,400]{1,0:T(1,128)S(1)}, f32[1,400]{1,0:T(1,128)}, u32[]{:S(2)}) copy-start(f32[1,400]{1,0:T(1,128)} %get-tuple-element.67) | copy-start | bytes 4804
  (7 other events, 4.9 us)

commit v3 on v2

--- a/solution.py
+++ b/solution.py
@@ -8,6 +8,7 @@
 
 MESH = pl.DeviceIdType.MESH
 VM = pl.BlockSpec(memory_space=pltpu.VMEM)
+ANY = pl.BlockSpec(memory_space=pltpu.HBM)
 HI = 256
 CHUNK = 512
 
@@ -20,7 +21,7 @@
     )
 
 
-def greet(dp, mp):
+def hail(dp, mp):
     me, mine = lax.axis_index("dp"), lax.axis_index("mp")
     barrier = pltpu.get_barrier_semaphore()
     for step in range(1, dp):
@@ -31,7 +32,10 @@
         pl.semaphore_signal(
             barrier, inc=1, device_id={"mp": lax.rem(mine + step, mp)}, device_id_type=MESH
         )
-    pl.semaphore_wait(barrier, dp - 1 + mp - 1)
+
+
+def all_in(dp, mp):
+    pl.semaphore_wait(pltpu.get_barrier_semaphore(), dp - 1 + mp - 1)
 
 
 def remote(src, dst, send, recv, where):
@@ -266,57 +270,85 @@
     return jnp.sum(x, axis=0, keepdims=True)
 
 
-def widen_dense(dense, width):
-    fields = dense.shape[1]
+def widen_dense(dense_t, width):
+    fields = dense_t.shape[0]
     row = lax.broadcasted_iota(jnp.int32, (fields, fields * width), 0)
     col = lax.broadcasted_iota(jnp.int32, (fields, fields * width), 1)
     ones = jnp.where(col // width == row, 1.0, 0.0)
-    return jnp.dot(dense, ones, precision=lax.Precision.HIGHEST, preferred_element_type=jnp.float32)
-
-
-def first_kernel(
-    dp, mp, own_rows, bits,
-    ids, lens, table, dense, num_row, gate_w, gate_b, n_first, n_gain, n_shift, b_first, b_gain, b_shift,
-    t2, keys, numeric, gates, n1, b1, vec,
-    scratch, gate_slots, n_slots, b_slots, v_slots, send, recv, send2, recv2,
-):
+    return lax.dot_general(
+        dense_t, ones, (((0,), (0,)), ((), ())),
+        precision=lax.Precision.HIGHEST, preferred_element_type=jnp.float32,
+    )
+
+
+def bring(sources, places, sem):
+    copies = []
+    for i, (source, place) in enumerate(zip(sources, places)):
+        copy = pltpu.make_async_copy(source, place, sem.at[i])
+        copy.start()
+        copies.append(copy)
+    return copies
+
+
+def first_kernel(dp, mp, own_rows, bits, *refs):
+    count = 13
+    sources, refs = refs[:count], refs[count:]
+    t2, keys, numeric, gates, n1, vec, n_own = refs[:7]
+    places, refs = refs[7 : 7 + count], refs[7 + count :]
+    scratch, gate_slots, n_slots, v_slots, send, recv, send2, recv2, sem = refs
+    brought = bring(sources, places, sem)
+    (
+        table, gate_w, n_first, gate_b, n_gain, n_shift, b_gain, b_shift,
+        ids, lens, dense_t, num_embed, n_rest,
+    ) = places
     part = own_rows // mp
     blocks = part // HI
     tall = blocks * 16
     me, mine = lax.axis_index("dp"), lax.axis_index("mp")
-    greet(dp, mp)
+    hail(dp, mp)
+    for copy in brought[:8]:
+        copy.wait()
     own = table[:, pl.ds(pl.multiple_of(mine * part, HI), part)].astype(jnp.bfloat16)
     for b in range(blocks):
         t2[pl.ds(pl.multiple_of(me * tall + b * 16, 16), 16), :] = own[:, b * HI : (b + 1) * HI]
-
-    def slot(i):
-        return t2.at[pl.ds(pl.multiple_of(i * tall, 16), tall), :]
-
-    copies = spread_dp(dp, slot, send, recv)
-    gate_slots[mine] = gate_w[...]
+    for k in range(2):
+        gate_slots[mine, k] = gate_w[:, k, :]
     n_slots[mine] = n_first[...]
-    b_slots[mine] = b_first[...]
     row = 0
     for ref in (gate_b, n_gain, n_shift, b_gain, b_shift):
         v_slots[mine, row : row + ref.shape[0], : ref.shape[1]] = ref[...]
         row += ref.shape[0]
+    all_in(dp, mp)
+
+    def slot(i):
+        return t2.at[pl.ds(pl.multiple_of(i * tall, 16), tall), :]
+
     groups = []
-    for i, ref in enumerate((gate_slots, n_slots, b_slots, v_slots)):
+    for i, ref in enumerate((gate_slots, n_slots, v_slots)):
         started = relay_own(mp, lambda k, ref=ref: ref.at[k], send2.at[i], recv2.at[i])
         groups.append((ref, i, started))
-    numeric[...] = low(widen_dense(dense[...], 16) * num_row[...])
+    copies = spread_dp(dp, slot, send, recv)
+    for copy in brought[8:]:
+        copy.wait()
+    for k in range(2):
+        n_own[k] = n_rest[:, k, :]
+    fields, width = num_embed.shape
+    tiled = jnp.concatenate([num_embed[...]] * fields, axis=1)
+    row = lax.broadcasted_iota(jnp.int32, tiled.shape, 0)
+    col = lax.broadcasted_iota(jnp.int32, tiled.shape, 1)
+    num_row = column_sum(jnp.where(col // width == row, tiled, 0.0))
+    numeric[...] = low(widen_dense(dense_t[...], width) * num_row)
     make_keys(ids, lens, scratch, own_rows, mp, bits)
     count = scratch.shape[0] // 8
     packed = compact_keys(scratch[...].reshape(count, 8, 128))
     keys[...] = jnp.transpose(packed.reshape(count * 8, 128))
     for ref, i, started in groups:
         relay_rest(mp, lambda k, ref=ref: ref.at[k], send2.at[i], recv2.at[i], started)
-    cols, small, large = gate_w.shape[1], n_first.shape[0], b_first.shape[0]
+    cols, small = gate_slots.shape[2], n_first.shape[0]
     for m in range(mp):
         for k in range(2):
             gates[k, m * cols : (m + 1) * cols, :] = gate_slots[m, k]
         n1[m * small : (m + 1) * small, :] = n_slots[m]
-        b1[m * large : (m + 1) * large, :] = b_slots[m]
     row = 0
     for ref in (gate_b, n_gain, n_shift, b_gain, b_shift):
         r, w = ref.shape
@@ -335,14 +367,39 @@
     return out
 
 
+def up16(x):
+    return -(-x // 16) * 16
+
+
+def own_part(x, mine, width):
+    full = x.shape[1]
+    pad = -(-width // 128) * 128
+    row = lax.broadcasted_iota(jnp.int32, (full, pad), 0)
+    col = lax.broadcasted_iota(jnp.int32, (full, pad), 1)
+    choose = jnp.where((row == col + mine * width) & (col < width), 1.0, 0.0).astype(jnp.bfloat16)
+    return low(nn(x, choose))
+
+
+def weight_grad(grad_y, inputs, mine, width):
+    return low(tn(own_part(grad_y, mine, width), inputs)[:width, :])
+
+
 def dense_kernel(
     dp, mp, hx, batch,
-    partial, numeric, gates, n1, b1, n_rest, b_rest, vec, left, right, pair, bias, labels, dense,
-    logits, grads_t, p_out, q_out, small, n_gain_g, n_shift_g, b_gain_g, b_shift_g, left_g, right_g, bias_g,
-    half_a, half_c, pooled, feat, gate, fields, own_term, grad_gate, n_slots, b_slots, n23, b2,
-    yn, dn, yb, db, un, ub, gyn, gyb, pair_hi, pair_lo, pair_g, sums,
+    partial, numeric, gates, n1, n_rest, vec,
+    b_first_hbm, b_rest_hbm, left_hbm, right_hbm, pair_hbm, bias_hbm, labels_hbm, dense_hbm,
+    logits, grads_t, feat, fields, grad_gate, gyn1, gyb1, q_out, small,
+    n_gain_g, n_shift_g, b_gain_g, b_shift_g, left_g, right_g, bias_g,
+    half_a, half_c, pooled, gate, own_term, b1_slots, n_slots, b_slots, b1, n23, b2,
+    yn, dn, yb, db, un, ub, gyn, gyb, pair_hi, pair_lo, pair_g, to_first, sums,
     fsend, frecv, wsend, wrecv, ssend, srecv,
+    b_first, b_rest, left, right, pair_t, bias, labels, dense_t, sem,
 ):
+    brought = bring(
+        (b_first_hbm, b_rest_hbm, left_hbm, right_hbm, pair_hbm, bias_hbm, labels_hbm, dense_hbm),
+        (b_first, b_rest, left, right, pair_t, bias, labels, dense_t),
+        sem,
+    )
     me, mine = lax.axis_index("dp"), lax.axis_index("mp")
     core = lax.rem(mine, 2)
     chip = mine // 2
@@ -357,7 +414,9 @@
     num = numeric.shape[1]
     gcols = wide // mp
     half = partial.shape[0] // 2
-    greet(dp, mp)
+    hail(dp, mp)
+    n_slots[mine] = n_rest[...]
+    all_in(dp, mp)
 
     def rowset(i):
         return pl.ds(pl.multiple_of(i * block, block), block)
@@ -367,7 +426,9 @@
 
     copy_a = remote(partial.at[part(1 - core), :], half_a, fsend.at[0], frecv.at[0], {"mp": other})
     copy_a.start()
-    n_slots[mine] = n_rest[...]
+    for copy in brought:
+        copy.wait()
+    b1_slots[mine] = b_first[...]
     b_slots[mine] = b_rest[...]
     copy_a.wait_recv()
     half_c[chip] = low(partial[part(core), :] + half_a[...])
@@ -379,10 +440,20 @@
         )
         copy.start()
         copies.append(copy)
+    heads = pair_t.shape[2]
+    by_head = jnp.transpose(pair_t[...].reshape(hx * 16, heads))
+    row = lax.broadcasted_iota(jnp.int32, (h1, heads), 0)
+    col = lax.broadcasted_iota(jnp.int32, (h1, heads), 1)
+    repeat = jnp.where(row // hx == col, 1.0, 0.0)
+    tall = jnp.dot(repeat, by_head, precision=lax.Precision.HIGHEST, preferred_element_type=jnp.float32)
+    row = lax.broadcasted_iota(jnp.int32, (h1, 16), 0)
+    pick = jnp.zeros((h1, 16), jnp.float32)
+    for i in range(hx):
+        pick = jnp.where(row % hx == i, tall[:, i * 16 : (i + 1) * 16], pick)
     for i in range(0, h1, 80):
         row = lax.broadcasted_iota(jnp.int32, (80, h2), 0) + i
         col = lax.broadcasted_iota(jnp.int32, (80, h2), 1)
-        pieces = jnp.concatenate([pair[i : i + 80, :]] * (h2 // 16), axis=1)
+        pieces = jnp.concatenate([pick[i : i + 80, :]] * heads, axis=1)
         spread = jnp.where(row // hx == col // 16, pieces, 0.0)
         high = low(spread)
         pair_hi[i : i + 80, :] = high
@@ -397,37 +468,48 @@
         pooled.at[part(core), :], pooled.at[part(core), :], fsend.at[chips], frecv.at[chips], {"mp": other}
     )
     copy_b.start()
-    n_started = relay_own(mp, lambda k: n_slots.at[k], wsend.at[0], wrecv.at[0])
-    b_started = relay_own(mp, lambda k: b_slots.at[k], wsend.at[1], wrecv.at[1])
+    weights = (b1_slots, n_slots, b_slots)
+    moving = [
+        relay_own(mp, lambda k, ref=ref: ref.at[k], wsend.at[i], wrecv.at[i])
+        for i, ref in enumerate(weights)
+    ]
+
+    def arrive(i):
+        relay_rest(mp, lambda k: weights[i].at[k], wsend.at[i], wrecv.at[i], moving[i])
+
     feat[:, :num] = numeric[...]
     copy_b.wait_recv()
     feat[:, num:] = low(jnp.transpose(pooled[...].astype(jnp.float32)))
-
-    def push(slot):
+    started = []
+
+    def push(slot, *values):
+        width = -(-values[0].shape[1] // 128) * 128
+        for r, value in enumerate(values):
+            sums[slot, me, r : r + 1, : value.shape[1]] = value
         out = []
         for step in range(1, dp):
+            at = sums.at[slot, me, :, pl.ds(0, width)]
             copy = remote(
-                sums.at[slot, me], sums.at[slot, me], ssend.at[slot, step - 1], srecv.at[slot, step - 1],
-                {"dp": lax.rem(me + step, dp)},
+                at, at, ssend.at[slot, step - 1], srecv.at[slot, step - 1], {"dp": lax.rem(me + step, dp)}
             )
             copy.start()
             out.append(copy)
-        return out
-
-    def pull(slot, copies):
-        for copy in copies:
+        started.append(out)
+        return slot, width, out
+
+    def pull(sent):
+        slot, width, out = sent
+        for copy in out:
             copy.wait_recv()
-        total = sums[slot, 0]
+        total = sums[slot, 0, :, :width]
         for d in range(1, dp):
-            total = total + sums[slot, d]
+            total = total + sums[slot, d, :, :width]
         return total
 
-    def put(slot, row, value):
-        sums[slot, me, row : row + 1, : value.shape[1]] = value
-
-    def norm(total, row, width):
-        mean = total[row : row + 1, :width] / batch
-        var = total[row + 1 : row + 2, :width] / batch - mean * mean
+    def norm(sent, width):
+        total = pull(sent)
+        mean = total[0:1, :width] / batch
+        var = total[1:2, :width] / batch - mean * mean
         return mean, lax.rsqrt(var + 1e-05)
 
     def activate(y_ref, d_ref, u_ref, layer, at, mean, rstd, gain, shift):
@@ -450,9 +532,10 @@
     zero1 = jnp.zeros((1, h1), jnp.float32)
     zero2 = jnp.zeros((1, h2), jnp.float32)
 
-    def forward_one(i, carry):
-        a, b, c, d = carry
-        at = rowset(i)
+    def loop(body, *start):
+        return lax.fori_loop(0, steps, lambda i, carry: body(rowset(i), *carry), tuple(start))
+
+    def gates_and_first(at, a, b):
         x = feat[at, :]
         wide_x = x.astype(jnp.float32)
         for k in range(2):
@@ -461,177 +544,142 @@
             fields[k, at, :] = low(wide_x * value)
         y = nt(fields[0, at, :], n1[...])
         yn[0, at, :] = y
-        v = nt(fields[1, at, :], b1[...])
-        yb[0, at, :] = v
-        return a + column_sum(y), b + column_sum(y * y), c + column_sum(v), d + column_sum(v * v)
-
-    stats = lax.fori_loop(0, steps, forward_one, (zero1, zero1, zero2, zero2))
-    for r in range(4):
-        put(0, r, stats[r])
-    sent = [push(0)]
-    relay_rest(mp, lambda k: n_slots.at[k], wsend.at[0], wrecv.at[0], n_started)
-    relay_rest(mp, lambda k: b_slots.at[k], wsend.at[1], wrecv.at[1], b_started)
+        return a + column_sum(y), b + column_sum(y * y)
+
+    sent_n = push(0, *loop(gates_and_first, zero1, zero1))
+    arrive(0)
+    for m in range(mp):
+        b1[m * s2 : (m + 1) * s2, :] = b1_slots[m]
+
+    def broad_first(at, a, b):
+        y = nt(fields[1, at, :], b1[...])
+        yb[0, at, :] = y
+        return a + column_sum(y), b + column_sum(y * y)
+
+    sent_b = push(1, *loop(broad_first, zero2, zero2))
+    arrive(1)
     for m in range(mp):
         for k in range(2):
             n23[k, m * s1 : (m + 1) * s1, :] = n_slots[m, k]
+    mean_n1, rstd_n1 = norm(sent_n, h1)
+
+    def narrow_second(at, a, b):
+        y = nt(activate(yn, dn, un, 0, at, mean_n1, rstd_n1, *gain_n(0)), n23[0])
+        yn[1, at, :] = y
+        return a + column_sum(y), b + column_sum(y * y)
+
+    sent_n = push(2, *loop(narrow_second, zero1, zero1))
+    arrive(2)
+    for m in range(mp):
         b2[m * s2 : (m + 1) * s2, :] = b_slots[m]
-    total = pull(0, sent[0])
-    mean_n, rstd_n = norm(total, 0, h1)
-    mean_b, rstd_b = norm(total, 2, h2)
-    rstd_n1, rstd_b1 = rstd_n, rstd_b
-
-    def forward_two(i, carry):
-        a, b, c, d = carry
-        at = rowset(i)
-        u = activate(yn, dn, un, 0, at, mean_n, rstd_n, *gain_n(0))
-        y = nt(u, n23[0])
-        yn[1, at, :] = y
-        u = activate(yb, db, ub, 0, at, mean_b, rstd_b, *gain_b(0))
-        v = nt(u, b2[...])
-        yb[1, at, :] = v
-        return a + column_sum(y), b + column_sum(y * y), c + column_sum(v), d + column_sum(v * v)
-
-    stats = lax.fori_loop(0, steps, forward_two, (zero1, zero1, zero2, zero2))
-    for r in range(4):
-        put(1, r, stats[r])
-    sent.append(push(1))
-    total = pull(1, sent[1])
-    mean_n2, rstd_n2 = norm(total, 0, h1)
-    mean_b2, rstd_b2 = norm(total, 2, h2)
-
-    def forward_three(i, carry):
-        a, b = carry
-        at = rowset(i)
-        u = activate(yn, dn, un, 1, at, mean_n2, rstd_n2, *gain_n(1))
-        y = nt(u, n23[1])
+    mean_b1, rstd_b1 = norm(sent_b, h2)
+
+    def broad_second(at, a, b):
+        y = nt(activate(yb, db, ub, 0, at, mean_b1, rstd_b1, *gain_b(0)), b2[...])
+        yb[1, at, :] = y
+        return a + column_sum(y), b + column_sum(y * y)
+
+    sent_b = push(3, *loop(broad_second, zero2, zero2))
+    mean_n2, rstd_n2 = norm(sent_n, h1)
+
+    def narrow_third(at, a, b):
+        y = nt(activate(yn, dn, un, 1, at, mean_n2, rstd_n2, *gain_n(1)), n23[1])
         yn[2, at, :] = y
         return a + column_sum(y), b + column_sum(y * y)
 
-    stats = lax.fori_loop(0, steps, forward_three, (zero1, zero1))
-    for r in range(2):
-        put(2, r, stats[r])
-    sent.append(push(2))
-
-    def broad_out(i, carry):
-        activate(yb, db, ub, 1, rowset(i), mean_b2, rstd_b2, *gain_b(1))
-        return carry
-
-    lax.fori_loop(0, steps, broad_out, 0)
-    pair_g[...] = jnp.zeros_like(pair_g)
+    sent_n = push(4, *loop(narrow_third, zero1, zero1))
     label = jnp.transpose(jnp.broadcast_to(labels[...].astype(jnp.float32), (8, rows)))[:, 0:1]
     own_term[:, 0:1] = label
-    total = pull(2, sent[2])
-    mean_n3, rstd_n3 = norm(total, 0, h1)
-
-    def join(i, carry):
-        l_sum, r_sum, g_sum, a, b, c, d = carry
-        at = rowset(i)
-        first = activate(yn, dn, un, 2, at, mean_n3, rstd_n3, *gain_n(2))
-        second = ub[1, at, :]
-        turned = nn(first, pair_hi[...]) + nn(first, pair_lo[...])
-        first32, second32 = first.astype(jnp.float32), second.astype(jnp.float32)
-        to_second = right[...] + turned
+    pair_g[...] = jnp.zeros_like(pair_g)
+    mean_b2, rstd_b2 = norm(sent_b, h2)
+
+    def broad_out(at):
+        second = activate(yb, db, ub, 1, at, mean_b2, rstd_b2, *gain_b(1))
+        to_first[at, :] = left[...] + (nt(second, pair_hi[...]) + nt(second, pair_lo[...]))
+        return ()
+
+    loop(broad_out)
+    mean_n3, rstd_n3 = norm(sent_n, h1)
+    to_right = right[...].reshape(1, h2)
+
+    def join_narrow(at, l_sum, g_sum, a, b):
+        first = activate(yn, dn, un, 2, at, mean_n3, rstd_n3, *gain_n(2)).astype(jnp.float32)
+        second = ub[1, at, :].astype(jnp.float32)
         logit = (
-            jnp.sum(first32 * left[...], axis=1, keepdims=True)
-            + jnp.sum(second32 * to_second, axis=1, keepdims=True)
+            jnp.sum(first * to_first[at, :], axis=1, keepdims=True)
+            + jnp.sum(second * to_right, axis=1, keepdims=True)
             + bias[...]
         )
         g = sigmoid(logit) - own_term[at, 0:1]
         own_term[at, 1:2] = logit
-        back = nt(second, pair_hi[...]) + nt(second, pair_lo[...])
-        weighted = g * first32
-        l_sum = l_sum + column_sum(weighted)
-        r_sum = r_sum + column_sum(g * second32)
-        g_sum = g_sum + column_sum(g)
-        pair_g[...] += tn(second, low(weighted))
-        gz = g * (left[...] + back) * dn[2, at, :]
+        own_term[at, 2:3] = g
+        gz = g * to_first[at, :] * dn[2, at, :]
         dn[2, at, :] = gz
-        a = a + column_sum(gz)
-        b = b + column_sum(gz * yn[2, at, :])
-        gz = g * to_second * db[1, at, :]
+        return (
+            l_sum + column_sum(g * first), g_sum + column_sum(g),
+            a + column_sum(gz), b + column_sum(gz * yn[2, at, :]),
+        )
+
+    l_sum, g_sum, a, b = loop(join_narrow, zero1, jnp.zeros((1, 1), jnp.float32), zero1, zero1)
+    sent_n = push(5, a, b)
+
+    def join_broad(at, r_sum, a, b):
+        first = un[2, at, :]
+        second = ub[1, at, :]
+        g = own_term[at, 2:3]
+        turned = nn(first, pair_hi[...]) + nn(first, pair_lo[...])
+        pair_g[...] += tn(second, low(g * first.astype(jnp.float32)))
+        gz = g * (to_right + turned) * db[1, at, :]
         db[1, at, :] = gz
-        c = c + column_sum(gz)
-        d = d + column_sum(gz * yb[1, at, :])
-        return l_sum, r_sum, g_sum, a, b, c, d
-
-    l_sum, r_sum, g_sum, a, b, c, d = lax.fori_loop(
-        0, steps, join, (zero1, zero2, jnp.zeros((1, 1), jnp.float32), zero1, zero1, zero2, zero2)
-    )
-    for r, value in enumerate((a, b, c, d)):
-        put(3, r, value)
-    sent.append(push(3))
-    for r, value in enumerate((l_sum, r_sum, g_sum)):
-        put(6, r, value)
-    join_sent = push(6)
+        return (
+            r_sum + column_sum(g * second.astype(jnp.float32)),
+            a + column_sum(gz), b + column_sum(gz * yb[1, at, :]),
+        )
+
+    r_sum, a, b = loop(join_broad, zero2, zero2, zero2)
+    sent_b = push(6, a, b)
+    sums[10, me, 1:2, 512:513] = g_sum
+    sent_join = push(10, r_sum, l_sum)
     logits[...] = jnp.transpose(own_term[:, 0:128])[1:2, :]
-
-    def own_part(x, width):
-        full = x.shape[1]
-        pad = -(-width // 128) * 128
-        row = lax.broadcasted_iota(jnp.int32, (full, pad), 0)
-        col = lax.broadcasted_iota(jnp.int32, (full, pad), 1)
-        choose = jnp.where((row == col + mine * width) & (col < width), 1.0, 0.0).astype(jnp.bfloat16)
-        return low(nn(x, choose))
-
-    def weight_grad(grad_y, inputs, width):
-        return low(tn(own_part(grad_y, width), inputs)[:width, :])
-
-    def up16(x):
-        return -(-x // 16) * 16
-
-    g_rows, n_rows, b_rows = up16(gcols), up16(s1), up16(s2)
-    p_out[...] = jnp.zeros_like(p_out)
-    q_out[...] = jnp.zeros_like(q_out)
-    folded = jnp.zeros((16, h1), jnp.float32)
-    col = lax.broadcasted_iota(jnp.int32, (16, h1), 1)
-    for h in range(h2 // 16):
-        folded = folded + jnp.where(col // hx == h, pair_g[h * 16 : (h + 1) * 16, :], 0.0)
-    q_out[n_rows + b_rows : n_rows + b_rows + 16, :h1] = low(folded)
-
-    total = pull(3, sent[3])
-
-    def grad_y(gz, normed, rstd, gain, total_rows):
-        return low(gain * rstd * (gz - total_rows[0:1] / batch - normed * (total_rows[1:2] / batch)))
-
-    t_n3, t_b2 = total[0:2, :h1], total[2:4, :h2]
-
-    def back_one(i, carry):
-        a, b, c, d = carry
-        at = rowset(i)
+    n_rows, b_rows = up16(s1), up16(s2)
+
+    def grad_y(gz, normed, rstd, gain, total):
+        return low(gain * rstd * (gz - total[0:1] / batch - normed * (total[1:2] / batch)))
+
+    t_n3 = pull(sent_n)[:, :h1]
+
+    def back_n3(at, a, b):
         g = grad_y(dn[2, at, :], yn[2, at, :], rstd_n3, gain_n(2)[0], t_n3)
-        gyn[2, at, :] = g
+        gyn[1, at, :] = g
         gz = nn(g, n23[1]) * dn[1, at, :]
         dn[1, at, :] = gz
-        a, b = a + column_sum(gz), b + column_sum(gz * yn[1, at, :])
+        return a + column_sum(gz), b + column_sum(gz * yn[1, at, :])
+
+    sent_n = push(7, *loop(back_n3, zero1, zero1))
+    q_out[...] = jnp.zeros_like(q_out)
+    q_out[:s1, h1 : 2 * h1] = weight_grad(gyn[1], un[1], mine, s1)
+    t_b2 = pull(sent_b)[:, :h2]
+
+    def back_b2(at, a, b):
         g = grad_y(db[1, at, :], yb[1, at, :], rstd_b2, gain_b(1)[0], t_b2)
-        gyb[1, at, :] = g
+        gyb[at, :] = g
         gz = nn(g, b2[...]) * db[0, at, :]
         db[0, at, :] = gz
-        c, d = c + column_sum(gz), d + column_sum(gz * yb[0, at, :])
-        return a, b, c, d
-
-    stats = lax.fori_loop(0, steps, back_one, (zero1, zero1, zero2, zero2))
-    for r in range(4):
-        put(4, r, stats[r])
-    sent.append(push(4))
-    q_out[:s1, h1 : 2 * h1] = weight_grad(gyn[2], un[1], s1)
-    q_out[n_rows : n_rows + s2, :] = weight_grad(gyb[1], ub[0], s2)
-    total = pull(4, sent[4])
-    t_n2, t_b1 = total[0:2, :h1], total[2:4, :h2]
-
-    def back_two(i, carry):
-        a, b = carry
-        at = rowset(i)
+        return a + column_sum(gz), b + column_sum(gz * yb[0, at, :])
+
+    sent_b = push(8, *loop(back_b2, zero2, zero2))
+    t_n2 = pull(sent_n)[:, :h1]
+
+    def back_n2(at, a, b):
         g = grad_y(dn[1, at, :], yn[1, at, :], rstd_n2, gain_n(1)[0], t_n2)
-        gyn[1, at, :] = g
+        gyn[0, at, :] = g
         gz = nn(g, n23[0]) * dn[0, at, :]
         dn[0, at, :] = gz
         return a + column_sum(gz), b + column_sum(gz * yn[0, at, :])
 
-    stats = lax.fori_loop(0, steps, back_two, (zero1, zero1))
-    for r in range(2):
-        put(5, r, stats[r])
-    sent.append(push(5))
+    sent_n = push(9, *loop(back_n2, zero1, zero1))
+    q_out[n_rows : n_rows + s2, :] = weight_grad(gyb[...], ub[0], mine, s2)
+    t_b1 = pull(sent_b)[:, :h2]
 
     def gate_back(k, at, grad):
         x = feat[at, :].astype(jnp.float32)
@@ -640,41 +688,35 @@
         grad_gate[k, at, :] = g
         return grad * value, g
 
-    def back_broad(i, carry):
-        at = rowset(i)
+    def back_b1(at):
         g = grad_y(db[0, at, :], yb[0, at, :], rstd_b1, gain_b(0)[0], t_b1)
-        gyb[0, at, :] = g
-        term, _ = gate_back(1, at, nn(g, b1[...]))
-        own_term[at, :] = term
-        return carry
-
-    lax.fori_loop(0, steps, back_broad, 0)
-    q_out[:s1, :h1] = weight_grad(gyn[1], un[0], s1)
-    p_out[2 * g_rows + n_rows : 2 * g_rows + n_rows + s2, :] = weight_grad(gyb[0], fields[1], s2)
-    p_out[g_rows : g_rows + gcols, :] = weight_grad(grad_gate[1], feat[...], gcols)
-    total = pull(5, sent[5])
-    t_n1 = total[0:2, :h1]
-
-    def back_narrow(i, carry):
-        ga, gb, ne = carry
-        at = rowset(i)
+        gyb1[at, :] = g
+        own_term[at, :] = gate_back(1, at, nn(g, b1[...]))[0]
+        return ()
+
+    loop(back_b1)
+    q_out[:s1, :h1] = weight_grad(gyn[0], un[0], mine, s1)
+    folded = jnp.zeros((16, h1), jnp.float32)
+    col = lax.broadcasted_iota(jnp.int32, (16, h1), 1)
+    for h in range(heads):
+        folded = folded + jnp.where(col // hx == h, pair_g[h * 16 : (h + 1) * 16, :], 0.0)
+    q_out[n_rows + b_rows : n_rows + b_rows + 16, :h1] = low(folded)
+    t_n1 = pull(sent_n)[:, :h1]
+
+    def back_n1(at, ga, gb, ne):
         g = grad_y(dn[0, at, :], yn[0, at, :], rstd_n1, gain_n(0)[0], t_n1)
-        gyn[0, at, :] = g
+        gyn1[at, :] = g
         term, g0 = gate_back(0, at, nn(g, n1[...]))
         g1 = grad_gate[1, at, :]
         whole = nn(g0, gates[0]) + nn(g1, gates[1]) + term + own_term[at, :]
         whole = low(whole).astype(jnp.float32)
         own_term[at, :] = whole
-        ne = ne + column_sum(whole[:, :num] * widen_dense(dense[at, :], 16))
+        ne = ne + column_sum(whole[:, :num] * widen_dense(dense_t[:, at], 16))
         return ga + column_sum(g0.astype(jnp.float32)), gb + column_sum(g1.astype(jnp.float32)), ne
 
     zero_g = jnp.zeros((1, wide), jnp.float32)
-    ga, gb, ne = lax.fori_loop(
-        0, steps, back_narrow, (zero_g, zero_g, jnp.zeros((1, num), jnp.float32))
-    )
+    ga, gb, ne = loop(back_n1, zero_g, zero_g, jnp.zeros((1, num), jnp.float32))
     grads_t[...] = low(jnp.transpose(own_term[:, num:]))
-    p_out[:gcols, :] = weight_grad(grad_gate[0], feat[...], gcols)
-    p_out[2 * g_rows : 2 * g_rows + s1, :] = weight_grad(gyn[0], fields[0], s1)
     small[...] = jnp.zeros_like(small)
     small[0:1, :gcols] = own_columns(ga, mine, gcols, mp)
     small[1:2, :gcols] = own_columns(gb, mine, gcols, mp)
@@ -685,34 +727,34 @@
     for layer, t in enumerate((t_b1, t_b2)):
         b_shift_g[layer : layer + 1, :] = own_columns(t[0:1], mine, s2, mp)
         b_gain_g[layer : layer + 1, :] = own_columns(t[1:2], mine, s2, mp)
-    total = pull(6, join_sent)
-    left_g[...] = total[0:1, :h1]
-    right_g[...] = total[1:2, :h2]
-    bias_g[...] = total[2:3, 0:1]
+    total = pull(sent_join)
+    right_g[...] = total[0:1, :h2]
+    left_g[...] = total[1:2, :h1]
+    bias_g[...] = total[1:2, 512:513]
     copy_a.wait_send()
     copy_b.wait_send()
     for copy in copies:
         copy.wait_send()
-    for group in sent + [join_sent]:
+    for group in started:
         for copy in group:
             copy.wait_send()
 
 
 def reduce_kernel(
     dp, mp,
-    grads, p_in, q_in, small,
-    table_g, gate_g, n_first_g, n_rest_g, b_first_g, b_rest_g, pair_g, small_out,
-    landed, shares, s_slots, p_work, q_work, p_land, q_land, p_full, q_full,
+    grads, feat, fields, grad_gate, gyn1, gyb1, q_in, small,
+    shares, p_full, q_full, small_out,
+    landed, s_slots, p_work, q_work, p_land, q_land,
     send, recv, send2, recv2, send3, recv3, psend, precv,
 ):
     tall = grads.shape[0] // dp
     me, mine = lax.axis_index("dp"), lax.axis_index("mp")
-    greet(dp, mp)
+    hail(dp, mp)
     levels = dp.bit_length() - 1
     orders = (list(range(levels)), list(range(1, levels)) + [0])
-    p_work[...] = p_in[...]
     q_work[...] = q_in[...]
     s_slots[me] = small[...]
+    all_in(dp, mp)
     works = (p_work, q_work)
     lands = (p_land, q_land)
     fulls = (p_full, q_full)
@@ -757,7 +799,6 @@
         sizes[w] = sizes[w] * 2
         return copy
 
-    pend = [halve(w, 0) for w in (0, 1)]
     copies = []
     for step in range(1, dp):
         to = lax.rem(me + step, dp)
@@ -768,6 +809,17 @@
         copy.start()
         copies.append(copy)
     small_copies = spread_dp(dp, lambda k: s_slots.at[k], send3, recv3)
+    pend = [None, halve(1, 0)]
+    gcols, s1, s2 = feat.shape[1] // mp, gyn1.shape[1] // mp, gyb1.shape[1] // mp
+    g_rows, n_rows, b_rows = up16(gcols), up16(s1), up16(s2)
+    p_work[...] = jnp.zeros_like(p_work)
+    for k in range(2):
+        p_work[k * g_rows : k * g_rows + gcols, :] = weight_grad(grad_gate[k], feat[...], mine, gcols)
+    row = 2 * g_rows
+    p_work[row : row + s1, :] = weight_grad(gyn1[...], fields[0], mine, s1)
+    row += n_rows
+    p_work[row : row + s2, :] = weight_grad(gyb1[...], fields[1], mine, s2)
+    pend[0] = halve(0, 0)
     for level in range(1, levels):
         for w in (0, 1):
             add(w, *pend[w])
@@ -789,12 +841,6 @@
         fulls[w][at, :] = works[w][at, :]
         back.append(double(w, levels - 1))
     relay_rest(mp, slot, send2, recv2, started)
-    blocks = tall // 16
-    for m in range(mp):
-        for b in range(blocks):
-            table_g[:, (m * blocks + b) * HI : (m * blocks + b + 1) * HI] = shares[
-                m, b * 16 : (b + 1) * 16, :
-            ].astype(jnp.float32)
     for level in range(levels - 2, -1, -1):
         for w in (0, 1):
             back[w].wait_recv()
@@ -809,26 +855,61 @@
     for w in (0, 1):
         back[w].wait_recv()
         waits.append(back[w])
-    def up16(x):
-        return -(-x // 16) * 16
-
-    gcols, s1, s2, h1 = gate_g.shape[1], n_first_g.shape[0], b_first_g.shape[0], n_rest_g.shape[2]
+    for copy in copies + small_copies + waits:
+        copy.wait_send()
+
+
+def final_kernel(
+    mp, hx, shares, p_full, q_full, small, logits_in, n_gain_in, n_shift_in, b_gain_in, b_shift_in,
+    left_in, right_in, bias_in,
+    logits, num_g, table_g, gate_g, gate_bias_g, n_first_g, n_rest_g, n_gain_g, n_shift_g,
+    b_first_g, b_rest_g, b_gain_g, b_shift_g, left_g, right_g, pair_g, bias_g,
+):
+    gcols, s1, s2, h1 = gate_g.shape[0], n_first_g.shape[0], b_first_g.shape[0], n_rest_g.shape[2]
     g_rows, n_rows, b_rows = up16(gcols), up16(s1), up16(s2)
+    wide = n_first_g.shape[1]
 
     def full(work, row, count, col, width):
         return work[row : row + count, col : col + width].astype(jnp.float32)
 
-    wide = n_first_g.shape[1]
-    gate_g[0] = full(p_full, 0, gcols, 0, wide)
-    gate_g[1] = full(p_full, g_rows, gcols, 0, wide)
+    blocks = shares.shape[1] // 16
+    for m in range(mp):
+        for b in range(blocks):
+            table_g[:, (m * blocks + b) * HI : (m * blocks + b + 1) * HI] = shares[
+                m, b * 16 : (b + 1) * 16, :
+            ].astype(jnp.float32)
+    gate_g[:, 0, :] = full(p_full, 0, gcols, 0, wide)
+    gate_g[:, 1, :] = full(p_full, g_rows, gcols, 0, wide)
     n_first_g[...] = full(p_full, 2 * g_rows, s1, 0, wide)
     b_first_g[...] = full(p_full, 2 * g_rows + n_rows, s2, 0, wide)
-    n_rest_g[0] = full(q_full, 0, s1, 0, h1)
-    n_rest_g[1] = full(q_full, 0, s1, h1, h1)
+    n_rest_g[:, 0, :] = full(q_full, 0, s1, 0, h1)
+    n_rest_g[:, 1, :] = full(q_full, 0, s1, h1, h1)
     b_rest_g[...] = full(q_full, n_rows, s2, 0, 2 * h1)
-    pair_g[...] = jnp.transpose(full(q_full, n_rows + b_rows, 16, 0, 512))[:h1, :]
-    for copy in copies + small_copies + waits:
-        copy.wait_send()
+    heads = pair_g.shape[2]
+    pairs = q_full[n_rows + b_rows : n_rows + b_rows + 16, :h1]
+    row = lax.broadcasted_iota(jnp.int32, (h1, heads), 0)
+    col = lax.broadcasted_iota(jnp.int32, (h1, heads), 1)
+    for i in range(hx):
+        choose = jnp.where(row == col * hx + i, 1.0, 0.0).astype(jnp.bfloat16)
+        pair_g[i] = nn(pairs, choose)
+    fields, width = num_g.shape
+    gate_bias_g[...] = small[0:2, :gcols]
+    spread = jnp.broadcast_to(small[2:3, : fields * width], (fields, fields * width))
+    row = lax.broadcasted_iota(jnp.int32, spread.shape, 0)
+    col = lax.broadcasted_iota(jnp.int32, spread.shape, 1)
+    spread = jnp.where(col // width == row, spread, 0.0)
+    total = spread[:, :width]
+    for i in range(1, fields):
+        total = total + spread[:, i * width : (i + 1) * width]
+    num_g[...] = total
+    logits[...] = logits_in[...]
+    n_gain_g[...] = n_gain_in[...]
+    n_shift_g[...] = n_shift_in[...]
+    b_gain_g[...] = b_gain_in[...]
+    b_shift_g[...] = b_shift_in[...]
+    left_g[...] = left_in[...]
+    right_g[...] = right_in[...].reshape(right_g.shape)
+    bias_g[...] = bias_in[...]
 
 
 def f32(*shape):
@@ -885,9 +966,15 @@
     h1, h2 = s1 * mp, s2 * mp
     hx = joining_pair.shape[1]
     bits = (cats * rows - 1).bit_length()
+    dense_t = dense_values.T
     tall = own_rows // mp // HI * 16
     vregs = 1 << (-(-(cats * slots * rows) // 1024) - 1).bit_length()
-    t2, keys, numeric, gates, n1, b1, vec = pl.pallas_call(
+    first_args = (
+        embed_table, jnp.transpose(gate_weight, (1, 0, 2)), narrow_first, gate_bias,
+        narrow_gain, narrow_shift, broad_gain, broad_shift,
+        field_ids, lengths, dense_t, num_embed, jnp.transpose(narrow_rest, (1, 0, 2)),
+    )
+    t2, keys, numeric, gates, n1, vec, n_own = pl.pallas_call(
         functools.partial(first_kernel, dp, mp, own_rows, bits),
         out_shape=(
             b16(dp * tall, HI),
@@ -895,35 +982,33 @@
             b16(rows, num),
             b16(2, wide, wide),
             b16(h1, wide),
-            b16(h2, wide),
             f32(16, 896),
+            b16(2, s1, h1),
         ),
-        in_specs=[VM] * 13,
+        in_specs=[ANY] * 13,
         out_specs=(VM,) * 7,
-        scratch_shapes=[
+        scratch_shapes=[pltpu.VMEM(x.shape, x.dtype) for x in first_args]
+        + [
             pltpu.VMEM((vregs * 8, 128), jnp.int32),
             held16(mp, 2, gcols, wide),
             held16(mp, s1, wide),
-            held16(mp, s2, wide),
             held(mp, 16, 256),
             dma(dp - 1),
             dma(dp - 1),
-            dma(4, mp),
-            dma(4, mp),
+            dma(3, mp),
+            dma(3, mp),
+            dma(13),
         ],
-        compiler_params=params(0),
+        compiler_params=params(0, 54),
         name="first",
-    )(
-        field_ids, lengths, embed_table, dense_values, num_embed.reshape(1, num), gate_weight, gate_bias,
-        narrow_first, narrow_gain, narrow_shift, broad_first, broad_gain, broad_shift,
-    )
+    )(*first_args)
     partial = pl.pallas_call(
         functools.partial(lookup_kernel, cats, rows, bits),
         out_shape=f32(cats * 16, rows),
         in_specs=[VM] * 2,
         out_specs=VM,
         scratch_shapes=[held(cats * 16, rows)],
-        compiler_params=params(None),
+        compiler_params=params(None, 12),
         name="lookup",
     )(keys, t2)
 
@@ -932,15 +1017,23 @@
 
     p_rows = up(2 * up(gcols, 16) + up(s1, 16) + up(s2, 16), 16 * dp)
     q_rows = up(up(s1, 16) + up(s2, 16) + 16, 16 * dp)
+    dense_args = (
+        broad_first, broad_rest, joining_left.reshape(1, h1), joining_right,
+        jnp.transpose(joining_pair, (1, 2, 0)), joining_bias.reshape(1, 1), labels.reshape(1, rows), dense_t,
+    )
     (
-        logits, grads_t, p_part, q_part, small,
+        logits, grads_t, feat, fields, grad_gate, gyn1, gyb1, q_part, small,
         n_gain_g, n_shift_g, b_gain_g, b_shift_g, left_g, right_g, bias_g,
     ) = pl.pallas_call(
         functools.partial(dense_kernel, dp, mp, hx, float(rows * dp)),
         out_shape=(
             f32(1, rows),
             b16(cats * 16, rows),
-            b16(p_rows, wide),
+            b16(rows, wide),
+            b16(2, rows, wide),
+            b16(2, rows, wide),
+            b16(rows, h1),
+            b16(rows, h2),
             b16(q_rows, h2),
             f32(8, 256),
             f32(3, s1),
@@ -951,19 +1044,18 @@
             f32(1, h2),
             f32(1, 1),
         ),
-        in_specs=[VM] * 14,
-        out_specs=(VM,) * 12,
+        in_specs=[VM] * 6 + [ANY] * 8,
+        out_specs=(VM,) * 16,
         scratch_shapes=[
             held(cats * 8, rows),
             held16(chips, cats * 8, rows),
             held16(cats * 16, rows),
-            held16(rows, wide),
             held(2, rows, wide),
-            held16(2, rows, wide),
             held(rows, wide),
-            held16(2, rows, wide),
+            held16(mp, s2, wide),
             held16(mp, 2, s1, h1),
             held16(mp, s2, h2),
+            held16(h2, wide),
             held16(2, h1, h1),
             held16(h2, h2),
             held(3, rows, h1),
@@ -972,58 +1064,47 @@
             held(2, rows, h2),
             held16(3, rows, h1),
             held16(2, rows, h2),
-            held16(3, rows, h1),
-            held16(2, rows, h2),
+            held16(2, rows, h1),
+            held16(rows, h2),
             held16(h1, h2),
             held16(h1, h2),
             held(h2, h1),
-            held(7, dp, 4, 896),
+            held(rows, h1),
+            held(11, dp, 2, 896),
             dma(chips + 1),
             dma(chips + 1),
-            dma(2, mp),
-            dma(2, mp),
-            dma(7, dp - 1),
-            dma(7, dp - 1),
-        ],
-        compiler_params=params(1, 60),
+            dma(3, mp),
+            dma(3, mp),
+            dma(11, dp - 1),
+            dma(11, dp - 1),
+        ]
+        + [pltpu.VMEM(x.shape, x.dtype) for x in dense_args]
+        + [dma(8)],
+        compiler_params=params(1, 39),
         name="dense",
-    )(
-        partial, numeric, gates, n1, b1, narrow_rest, broad_rest, vec,
-        joining_left.reshape(1, h1), joining_right.reshape(1, h2), joining_pair.reshape(h1, width),
-        joining_bias.reshape(1, 1), labels.reshape(1, rows), dense_values,
-    )
+    )(partial, numeric, gates, n1, n_own, vec, *dense_args)
     row_sums = pl.pallas_call(
         functools.partial(scatter_kernel, cats, rows, bits),
         out_shape=b16(dp * tall, HI),
         in_specs=[VM] * 2,
         out_specs=VM,
         scratch_shapes=[held(dp * tall, HI)],
-        compiler_params=params(None),
+        compiler_params=params(None, 12),
         name="scatter",
     )(keys, grads_t)
-    (
-        embed_table_grad, gate_weight_grad, narrow_first_grad, narrow_rest_grad,
-        broad_first_grad, broad_rest_grad, pair_g, small,
-    ) = pl.pallas_call(
+    shares, p_full, q_full, small = pl.pallas_call(
         functools.partial(reduce_kernel, dp, mp),
         out_shape=(
-            f32(width, own_rows),
-            f32(2, gcols, wide),
-            f32(s1, wide),
-            f32(2, s1, h1),
-            f32(s2, wide),
-            f32(s2, h2),
-            f32(h1, width),
+            b16(mp, tall, HI),
+            b16(p_rows, wide),
+            b16(q_rows, h2),
             f32(8, 256),
         ),
-        in_specs=[VM] * 4,
-        out_specs=(VM,) * 8,
+        in_specs=[VM] * 8,
+        out_specs=(VM,) * 4,
         scratch_shapes=[
             held16(dp - 1, tall, HI),
-            held16(mp, tall, HI),
             held(dp, 8, 256),
-            held16(p_rows, wide),
-            held16(q_rows, h2),
             held16(p_rows, wide),
             held16(q_rows, h2),
             held16(p_rows, wide),
@@ -1037,28 +1118,46 @@
             dma(2, 2 * (dp.bit_length() - 1)),
             dma(2, 2 * (dp.bit_length() - 1)),
         ],
-        compiler_params=params(2),
+        compiler_params=params(2, 24),
         name="reduce",
-    )(row_sums, p_part, q_part, small)
-    return (
-        logits.reshape(rows),
-        small[2, :num].reshape(-1, width),
-        embed_table_grad,
-        gate_weight_grad,
-        small[:2, :gcols],
-        narrow_first_grad,
-        narrow_rest_grad,
-        n_gain_g,
-        n_shift_g,
-        broad_first_grad,
-        broad_rest_grad,
-        b_gain_g,
-        b_shift_g,
-        left_g.reshape(h1),
-        right_g.reshape(h2),
-        pair_g.reshape(joining_pair.shape),
-        bias_g.reshape(1),
+    )(row_sums, feat, fields, grad_gate, gyn1, gyb1, q_part, small)
+    outs = pl.pallas_call(
+        functools.partial(final_kernel, mp, hx),
+        out_shape=(
+            f32(1, rows),
+            f32(*num_embed.shape),
+            f32(width, own_rows),
+            f32(gcols, 2, wide),
+            f32(2, gcols),
+            f32(s1, wide),
+            f32(s1, 2, h1),
+            f32(3, s1),
+            f32(3, s1),
+            f32(s2, wide),
+            f32(s2, h2),
+            f32(2, s2),
+            f32(2, s2),
+            f32(1, h1),
+            f32(h2),
+            f32(hx, width, joining_pair.shape[0]),
+            f32(1, 1),
+        ),
+        in_specs=[VM] * 12,
+        out_specs=(VM,) * 17,
+        compiler_params=params(None, 16),
+        name="final",
+    )(
+        shares, p_full, q_full, small, logits, n_gain_g, n_shift_g, b_gain_g, b_shift_g,
+        left_g, right_g, bias_g,
     )
+    outs = list(outs)
+    outs[0] = outs[0].reshape(rows)
+    outs[3] = jnp.transpose(outs[3], (1, 0, 2))
+    outs[6] = jnp.transpose(outs[6], (1, 0, 2))
+    outs[13] = outs[13].reshape(h1)
+    outs[15] = jnp.transpose(outs[15], (2, 0, 1))
+    outs[16] = outs[16].reshape(1)
+    return tuple(outs)
 
 
 def solution(mesh):

time: 216 us -> 178 us (0.82); the launches traced: 214 us -> 178 us
  local copies, waits for them, and re-layouts: 30.7 us -> 5.87 us
  Pallas kernels: 178 us -> 171 us
    unnamed x79 -> x30, local copies, waits for them, and re-layouts: 27.4 us -> 5.87 us
    pallas_call x1, Pallas kernels: 70.6 us -> 63.1 us  [shards(): pl.pallas_call(functools.partial(dense_kernel, dp, mp, hx, float(rows * d...]
    pallas_call x1 -> x2, Pallas kernels: 56.8 us -> 61 us  [the longest x1 58.2 us: shards(): pl.pallas_call(functools.partial(reduce_kernel, dp, mp), out_shape=(b16(m...]
    pallas_call x1, Pallas kernels: 28.3 us -> 24.3 us  [shards(): pl.pallas_call(functools.partial(first_kernel, dp, mp, own_rows, bits), o...]
where the time goes in v3:
time: 178 us
  Pallas kernels  171 us (96%)
  local copies, waits for them, and re-layouts  5.87 us (3%)
    pallas_call x1, Pallas kernels, shards(): pl.pallas_call(functools.partial(dense_kernel, dp, mp, hx, float(rows * d...  63.1 us
    pallas_call x1, Pallas kernels, shards(): pl.pallas_call(functools.partial(reduce_kernel, dp, mp), out_shape=(b16(m...  58.2 us
    pallas_call x1, Pallas kernels, shards(): pl.pallas_call(functools.partial(first_kernel, dp, mp, own_rows, bits), o...  24.3 us
    pallas_call x1, Pallas kernels, shards(): pl.pallas_call(functools.partial(scatter_kernel, cats, rows, bits), out_s...  11.2 us
    pallas_call x1, Pallas kernels, shards(): pl.pallas_call(functools.partial(lookup_kernel, cats, rows, bits), out_sh...  11.2 us
    unnamed x30, local copies, waits for them, and re-layouts  5.87 us

profile of v3, /device:TPU:0, one launch (start us, length us, event | category | flops | bytes accessed | tf_op | source)
XLA Modules:
  0.0 178.2 jit_solution(5779520663942503962)
XLA Ops:
  1.3 0.0 copy-start.5
  1.3 0.0 copy-start.7
  1.3 0.0 copy-start.9
  1.4 24.3 %first.1 = (bf16[1024,256]{1,0:T(8,128)(2,1)}, s32[128,512]{1,0:T(8,128)}, bf16[512,208]{1,0:T(8,128)(2,1)}, bf16[2,624,624]{2,1,0:T(8,128)(2,1)}, bf16[400,624]...) custom-call(f32[16,8192]{1,0:T(8,128)} %refs_0_.1, bf16[156,2,624]{2,1,0:T(2,128)(2,1)} %bitcast.19, ...), custom_call_target="tpu_custom_call" | custom-call | tf_op jit(solution)/shard_map/first/pallas_call | solution.py:977
  25.7 1.1 copy-done.1
  26.8 1.0 copy-done.3
  27.8 11.2 %lookup.1.partial = f32[416,512]{1,0:T(8,128)S(1)} custom-call(s32[128,512]{1,0:T(8,128)S(1)} %copy-done.1, bf16[1024,256]{1,0:T(8,128)(2,1)S(1)} %copy-done.3), custom_call_target="tpu_custom_call" | custom-call | tf_op jit(solution)/shard_map/lookup/pallas_call | solution.py:1005
  39.0 0.0 copy-done.5
  39.0 0.0 copy-done.7
  39.0 0.0 copy-done.9
  39.0 0.0 copy-done.10
  39.0 0.0 copy-done.12
  39.1 0.0 copy-done.13
  39.1 0.0 copy-done.14
  39.1 0.0 copy-done
  39.1 0.0 copy-start.4
  39.1 1.0 copy-done.4
  40.1 0.9 copy-done.6
  41.1 0.9 copy-done.8
  42.0 0.8 copy-done.11
  42.8 63.1 %dense.1 = (f32[1,512]{1,0:T(1,128)S(1)}, bf16[416,512]{1,0:T(8,128)(2,1)S(1)}, bf16[512,624]{1,0:T(8,128)(2,1)S(1)}, bf16[2,512,624]{2,1,0:T(8,128)(2,1)S(1)}, ...) custom-call(f32[416,512]{1,0:T(8,128)S(1)} %lookup.1.partial, ...), custom_call_target="tpu_custom_call" | custom-call | tf_op jit(solution)/shard_map/dense/pallas_call | solution.py:1027
  106.0 11.2 %scatter.1.grads = bf16[1024,256]{1,0:T(8,128)(2,1)S(1)} custom-call(s32[128,512]{1,0:T(8,128)S(1)} %copy-done.2, bf16[416,512]{1,0:T(8,128)(2,1)S(1)} %get-tuple-element.68.grad), custom_call_target="tpu_custom_call" | custom-call | tf_op jit(solution)/shard_map/scatter/pallas_call | solution.py:1086
  117.1 58.2 %reduce.1 = (bf16[4,128,256]{2,1,0:T(8,128)(2,1)S(1)}, bf16[640,624]{1,0:T(8,128)(2,1)S(1)}, bf16[384,800]{1,0:T(8,128)(2,1)S(1)}, f32[8,256]{1,0:T(8,128)S(1)}) custom-call(bf16[1024,256]{1,0:T(8,128)(2,1)S(1)} %scatter.1.grads, bf16[512,624]{1,0:T(8,128)(2,1)S(1)} %get-tuple-element.69.feat, bf16[2,512,624]{2,1,0:T(8,128)(2,1)S(1)} %get-tuple-element.70.fields, ...), custom_call_target="tpu_custom_call" | custom-call | tf_op jit(solution)/shard_map/reduce/pallas_call | solution.py:1095
  175.3 2.9 %final.1 = (f32[1,512]{1,0:T(1,128)}, f32[13,16]{1,0:T(8,128)}, f32[16,8192]{1,0:T(8,128)}, f32[156,2,624]{2,1,0:T(2,128)}, f32[2,156]{1,0:T(2,128)}, /*index=5*...) custom-call(bf16[4,128,256]{2,1,0:T(8,128)(2,1)S(1)} %get-tuple-elem, ...), custom_call_target="tpu_custom_call" | custom-call | tf_op jit(solution)/shard_map/final/pallas_call | solution.py:1124
  (12 shorter events, 0.0 us)
Async XLA Ops:
  1.3 37.7 %copy-start.5 = (bf16[200,800]{1,0:T(8,128)(2,1)S(1)}, bf16[200,800]{1,0:T(8,128)(2,1)}, u32[]{:S(2)}) copy-start(bf16[200,800]{1,0:T(8,128)(2,1)} %b_rest_hbm.1) | copy-start | bytes 960004
  1.3 37.7 %copy-start.7 = (bf16[200,624]{1,0:T(8,128)(2,1)S(1)}, bf16[200,624]{1,0:T(8,128)(2,1)}, u32[]{:S(2)}) copy-start(bf16[200,624]{1,0:T(8,128)(2,1)} %b_first_hbm.1) | copy-start | bytes 748804
  1.3 37.7 %copy-start.9 = (f32[512,13]{0,1:T(8,128)S(1)}, f32[512,13]{0,1:T(8,128)}, u32[]{:S(2)}) copy-start(f32[512,13]{0,1:T(8,128)} %param.20) | copy-start | bytes 79876
  1.3 37.7 %copy-start.10 = (f32[50,8,16]{0,2,1:T(8,128)S(1)}, f32[50,8,16]{0,2,1:T(8,128)}, u32[]{:S(2)}) copy-start(f32[50,8,16]{0,2,1:T(8,128)} %param.38) | copy-start | bytes 76804
  1.4 37.7 %copy-start.12 = (f32[800]{0:T(1024)S(1)}, f32[800]{0:T(1024)}, u32[]{:S(2)}) copy-start(f32[800]{0:T(1024)} %right_hbm.1) | copy-start | bytes 9604
  1.4 37.7 %copy-start.13 = (f32[400]{0:T(512)S(1)}, f32[400]{0:T(512)}, u32[]{:S(2)}) copy-start(f32[400]{0:T(512)} %param.36) | copy-start | bytes 4804
  1.4 37.7 %copy-start.14 = (s32[512]{0:T(512)S(1)}, s32[512]{0:T(512)}, u32[]{:S(2)}) copy-start(s32[512]{0:T(512)} %param.23) | copy-start | bytes 6148
  25.7 13.4 %copy-start = (bf16[2,624,624]{2,1,0:T(8,128)(2,1)S(1)}, bf16[2,624,624]{2,1,0:T(8,128)(2,1)}, u32[]{:S(2)}) copy-start(bf16[2,624,624]{2,1,0:T(8,128)(2,1)} %get-tuple-element.64.gates) | copy-start | bytes 4672516
  25.7 1.1 copy-start.1
  26.8 1.0 copy-start.3
  39.1 1.0 copy-start.4
  40.1 0.9 copy-start.6
  41.1 0.9 copy-start.8
  42.0 0.8 copy-start.11
  42.8 63.1 %copy-start.2 = (s32[128,512]{1,0:T(8,128)S(1)}, s32[128,512]{1,0:T(8,128)}, u32[]{:S(2)}) copy-start(s32[128,512]{1,0:T(8,128)} %get-tuple-element.61.keys) | copy-start | bytes 786436

commit v4 on v3

--- a/solution.py
+++ b/solution.py
@@ -114,7 +114,11 @@
     return key, shift
 
 
-def make_keys(ids, lens, scratch, own_rows, mp, bits):
+def seat(i, dp):
+    return i % 2 * (dp // 2) + i // 2
+
+
+def make_keys(ids, lens, scratch, own_rows, dp, mp, bits):
     cats, slots, rows = ids.shape
     part = own_rows // mp
     mine = lax.axis_index("mp")
@@ -127,7 +131,7 @@
         holder = values // own_rows
         inner = values - holder * own_rows
         owner = inner // part
-        place = holder * part + inner - owner * part
+        place = seat(holder, dp) * part + inner - owner * part
         live = (slot < lens[pl.ds(c, 1), :]) & (owner == mine)
         key = jnp.where(live, place * (1 << bits) + c * rows + event, -1)
         for q in range(rows // 128):
@@ -310,7 +314,7 @@
         copy.wait()
     own = table[:, pl.ds(pl.multiple_of(mine * part, HI), part)].astype(jnp.bfloat16)
     for b in range(blocks):
-        t2[pl.ds(pl.multiple_of(me * tall + b * 16, 16), 16), :] = own[:, b * HI : (b + 1) * HI]
+        t2[pl.ds(pl.multiple_of(seat(me, dp) * tall + b * 16, 16), 16), :] = own[:, b * HI : (b + 1) * HI]
     for k in range(2):
         gate_slots[mine, k] = gate_w[:, k, :]
     n_slots[mine] = n_first[...]
@@ -321,7 +325,7 @@
     all_in(dp, mp)
 
     def slot(i):
-        return t2.at[pl.ds(pl.multiple_of(i * tall, 16), tall), :]
+        return t2.at[pl.ds(pl.multiple_of(seat(i, dp) * tall, 16), tall), :]
 
     groups = []
     for i, ref in enumerate((gate_slots, n_slots, v_slots)):
@@ -338,7 +342,7 @@
     col = lax.broadcasted_iota(jnp.int32, tiled.shape, 1)
     num_row = column_sum(jnp.where(col // width == row, tiled, 0.0))
     numeric[...] = low(widen_dense(dense_t[...], width) * num_row)
-    make_keys(ids, lens, scratch, own_rows, mp, bits)
+    make_keys(ids, lens, scratch, own_rows, dp, mp, bits)
     count = scratch.shape[0] // 8
     packed = compact_keys(scratch[...].reshape(count, 8, 128))
     keys[...] = jnp.transpose(packed.reshape(count * 8, 128))
@@ -384,15 +388,40 @@
     return low(tn(own_part(grad_y, mine, width), inputs)[:width, :])
 
 
+def flip(me, level):
+    bit = 1 << level
+    return me + bit - 2 * bit * lax.rem(me // bit, 2)
+
+
+def upper(me, level):
+    return lax.rem(me // (1 << level), 2)
+
+
+def give_half(me, level, start, size, work, land, send, recv):
+    half = size // 2
+    mine = upper(me, level)
+    at = pl.ds(pl.multiple_of(start + (1 - mine) * half, 16), half)
+    copy = remote(work.at[at, :], land, send, recv, {"dp": flip(me, level)})
+    copy.start()
+    return copy, start + mine * half
+
+
+def add_half(copy, start, half, work, land):
+    copy.wait_recv()
+    at = pl.ds(pl.multiple_of(start, 16), half)
+    return low(work[at, :].astype(jnp.float32) + land[...].astype(jnp.float32))
+
+
 def dense_kernel(
     dp, mp, hx, batch,
     partial, numeric, gates, n1, n_rest, vec,
     b_first_hbm, b_rest_hbm, left_hbm, right_hbm, pair_hbm, bias_hbm, labels_hbm, dense_hbm,
-    logits, grads_t, feat, fields, grad_gate, gyn1, gyb1, q_out, small,
+    logits, grads_t, feat, fields, grad_gate, gyn1, a_out, b_out, small,
     n_gain_g, n_shift_g, b_gain_g, b_shift_g, left_g, right_g, bias_g,
     half_a, half_c, pooled, gate, own_term, b1_slots, n_slots, b_slots, b1, n23, b2,
-    yn, dn, yb, db, un, ub, gyn, gyb, pair_hi, pair_lo, pair_g, to_first, sums,
+    yn, dn, yb, db, un, ub, gyn, gyb, pair_hi, pair_lo, pair_g, to_first, sums, spill,
     fsend, frecv, wsend, wrecv, ssend, srecv,
+    gyb1, a_work, b_work, a_land, b_land, hsend, hrecv,
     b_first, b_rest, left, right, pair_t, bias, labels, dense_t, sem,
 ):
     brought = bring(
@@ -641,7 +670,6 @@
     sums[10, me, 1:2, 512:513] = g_sum
     sent_join = push(10, r_sum, l_sum)
     logits[...] = jnp.transpose(own_term[:, 0:128])[1:2, :]
-    n_rows, b_rows = up16(s1), up16(s2)
 
     def grad_y(gz, normed, rstd, gain, total):
         return low(gain * rstd * (gz - total[0:1] / batch - normed * (total[1:2] / batch)))
@@ -656,8 +684,14 @@
         return a + column_sum(gz), b + column_sum(gz * yn[1, at, :])
 
     sent_n = push(7, *loop(back_n3, zero1, zero1))
-    q_out[...] = jnp.zeros_like(q_out)
-    q_out[:s1, h1 : 2 * h1] = weight_grad(gyn[1], un[1], mine, s1)
+    main = a_work.shape[1]
+    rest = h2 - main
+    parts = main // rest
+    tall_a = s2 + s1
+    short = -(-tall_a // parts)
+    a_work[...] = jnp.zeros_like(a_work)
+    b_work[...] = jnp.zeros_like(b_work)
+    grad_n3 = weight_grad(gyn[1], un[1], mine, s1)
     t_b2 = pull(sent_b)[:, :h2]
 
     def back_b2(at, a, b):
@@ -678,7 +712,22 @@
         return a + column_sum(gz), b + column_sum(gz * yn[0, at, :])
 
     sent_n = push(9, *loop(back_n2, zero1, zero1))
-    q_out[n_rows : n_rows + s2, :] = weight_grad(gyb[...], ub[0], mine, s2)
+    grad_n2 = weight_grad(gyn[0], un[0], mine, s1)
+    grad_b2 = weight_grad(gyb[...], ub[0], mine, s2)
+    a_work[:s2, :] = grad_b2[:, :main]
+    a_work[s2:tall_a, :] = jnp.concatenate([grad_n2, grad_n3], axis=1)[:, :main]
+    spill[:s2, :] = grad_b2[:, main:]
+    spill[s2:tall_a, :] = jnp.concatenate([grad_n2, grad_n3], axis=1)[:, main:]
+    for p in range(parts):
+        n = min(short, tall_a - p * short)
+        a_work[tall_a : tall_a + n, p * rest : (p + 1) * rest] = spill[p * short : p * short + n, :]
+    size_a, size_b = a_work.shape[0], b_work.shape[0]
+    copy_ax, start_a = give_half(me, 0, 0, size_a, a_work, a_land.at[pl.ds(0, size_a // 2), :], hsend.at[0], hrecv.at[0])
+    folded = jnp.zeros((16, h1), jnp.float32)
+    col = lax.broadcasted_iota(jnp.int32, (16, h1), 1)
+    for h in range(heads):
+        folded = folded + jnp.where(col // hx == h, pair_g[h * 16 : (h + 1) * 16, :], 0.0)
+    b_work[size_b - 16 :, :h1] = low(folded)
     t_b1 = pull(sent_b)[:, :h2]
 
     def gate_back(k, at, grad):
@@ -695,12 +744,15 @@
         return ()
 
     loop(back_b1)
-    q_out[:s1, :h1] = weight_grad(gyn[0], un[0], mine, s1)
-    folded = jnp.zeros((16, h1), jnp.float32)
-    col = lax.broadcasted_iota(jnp.int32, (16, h1), 1)
-    for h in range(heads):
-        folded = folded + jnp.where(col // hx == h, pair_g[h * 16 : (h + 1) * 16, :], 0.0)
-    q_out[n_rows + b_rows : n_rows + b_rows + 16, :h1] = low(folded)
+    b_work[:s2, :wide] = weight_grad(gyb1[...], fields[1], mine, s2)
+    b_work[s2 : s2 + gcols, :wide] = weight_grad(grad_gate[1], feat[...], mine, gcols)
+    copy_bx, start_b = give_half(me, 0, 0, size_b, b_work, b_land, hsend.at[2], hrecv.at[2])
+    a_work[pl.ds(pl.multiple_of(start_a, 16), size_a // 2), :] = add_half(
+        copy_ax, start_a, size_a // 2, a_work, a_land.at[pl.ds(0, size_a // 2), :]
+    )
+    copy_az, start_a = give_half(
+        me, 1, start_a, size_a // 2, a_work, a_land.at[pl.ds(size_a // 2, size_a // 4), :], hsend.at[1], hrecv.at[1]
+    )
     t_n1 = pull(sent_n)[:, :h1]
 
     def back_n1(at, ga, gb, ne):
@@ -731,9 +783,11 @@
     right_g[...] = total[0:1, :h2]
     left_g[...] = total[1:2, :h1]
     bias_g[...] = total[1:2, 512:513]
-    copy_a.wait_send()
-    copy_b.wait_send()
-    for copy in copies:
+    a_out[...] = add_half(
+        copy_az, start_a, size_a // 4, a_work, a_land.at[pl.ds(size_a // 2, size_a // 4), :]
+    )
+    b_out[...] = add_half(copy_bx, start_b, size_b // 2, b_work, b_land)
+    for copy in [copy_a, copy_b, copy_ax, copy_az, copy_bx] + copies:
         copy.wait_send()
     for group in started:
         for copy in group:
@@ -742,131 +796,179 @@
 
 def reduce_kernel(
     dp, mp,
-    grads, feat, fields, grad_gate, gyn1, gyb1, q_in, small,
-    shares, p_full, q_full, small_out,
-    landed, s_slots, p_work, q_work, p_land, q_land,
-    send, recv, send2, recv2, send3, recv3, psend, precv,
+    grads, feat, fields, grad_gate, gyn1, a_in, b_in, small,
+    shares, a_full, b_full, c_full, small_out,
+    t_work, t_land, t_slots, s_slots, a_work, a_land, b_work, b_land, c_work, c_land, c_slots,
+    tsend, trecv, ysend, yrecv, ssend, srecv, asend, arecv, bsend, brecv, csend, crecv,
 ):
     tall = grads.shape[0] // dp
     me, mine = lax.axis_index("dp"), lax.axis_index("mp")
     hail(dp, mp)
     levels = dp.bit_length() - 1
-    orders = (list(range(levels)), list(range(1, levels)) + [0])
-    q_work[...] = q_in[...]
+    far = dp // 2
+    side, place = upper(me, 0), me // 2
+    size_a, size_b, size_c = a_full.shape[0], b_full.shape[0], c_full.shape[0]
     s_slots[me] = small[...]
+    pending = []
     all_in(dp, mp)
-    works = (p_work, q_work)
-    lands = (p_land, q_land)
-    fulls = (p_full, q_full)
-    starts = [0, 0]
-    sizes = [p_work.shape[0], q_work.shape[0]]
-    waits = []
-
-    def flip(bit):
-        return me + (1 << bit) - 2 * (1 << bit) * lax.rem(me // (1 << bit), 2)
-
-    def halve(w, level):
-        bit = orders[w][level]
-        size = sizes[w] // 2
-        up = lax.rem(me // (1 << bit), 2)
-        keep = starts[w] + up * size
-        give = starts[w] + (1 - up) * size
-        offset = works[w].shape[0] - 2 * size
-        where = pl.ds(offset, size)
-        copy = remote(
-            works[w].at[pl.ds(pl.multiple_of(give, 16), size), :], lands[w].at[where, :],
-            psend.at[w, level], precv.at[w, level], {"dp": flip(bit)},
+
+    def send_to(copy):
+        copy.start()
+        pending.append(copy)
+        return copy
+
+    def across(k):
+        return {"dp": lax.rem(me + 2 * k, dp)}
+
+    def rows_at(start, size):
+        return pl.ds(pl.multiple_of(start, 16), size)
+
+    half_t = grads.shape[0] // 2
+    copy_t = send_to(
+        remote(grads.at[rows_at((1 - side) * half_t, half_t), :], t_land, tsend.at[0], trecv.at[0], {"dp": flip(me, 0)})
+    )
+    start_a, start_b = 0, side * (size_b // 2)
+    for level in range(2):
+        start_a = start_a + upper(me, level) * (size_a >> (level + 1))
+    a_work[...] = a_in[...]
+    b_work[...] = b_in[...]
+
+    def halves(name, level, work, land, size, sems, off):
+        half = size // 2
+        mine_up = upper(me, level)
+        copy = send_to(
+            remote(
+                work.at[rows_at(off + (1 - mine_up) * half, half), :], land.at[pl.ds(0, half), :],
+                sems[0].at[level], sems[1].at[level], {"dp": flip(me, level)},
+            )
         )
-        copy.start()
-        starts[w], sizes[w] = keep, size
-        return copy, where
-
-    def add(w, copy, where):
+        return copy, off + mine_up * half, half
+
+    def fold(step, work, land):
+        copy, off, half = step
         copy.wait_recv()
-        at = pl.ds(pl.multiple_of(starts[w], 16), sizes[w])
-        works[w][at, :] = low(
-            works[w][at, :].astype(jnp.float32) + lands[w][where, :].astype(jnp.float32)
+        at = rows_at(off, half)
+        work[at, :] = low(work[at, :].astype(jnp.float32) + land[pl.ds(0, half), :].astype(jnp.float32))
+        return off, half
+
+    def double(level, full, start, size, sems):
+        at = full.at[rows_at(start, size), :]
+        copy = send_to(
+            remote(at, at, sems[0].at[levels + level], sems[1].at[levels + level], {"dp": flip(me, level)})
         )
-        waits.append(copy)
-
-    def double(w, level):
-        bit = orders[w][level]
-        at = fulls[w].at[pl.ds(pl.multiple_of(starts[w], 16), sizes[w]), :]
-        copy = remote(at, at, psend.at[w, levels + level], precv.at[w, levels + level], {"dp": flip(bit)})
-        copy.start()
-        up = lax.rem(me // (1 << bit), 2)
-        starts[w] = starts[w] - up * sizes[w]
-        sizes[w] = sizes[w] * 2
-        return copy
-
-    copies = []
-    for step in range(1, dp):
-        to = lax.rem(me + step, dp)
-        copy = remote(
-            grads.at[pl.ds(pl.multiple_of(to * tall, 16), tall), :],
-            landed.at[step - 1], send.at[step - 1], recv.at[step - 1], {"dp": to},
+        return copy, start - upper(me, level) * size, size * 2
+
+    sems_a, sems_b = (asend, arecv), (bsend, brecv)
+    step_b = halves("b", 1, b_work, b_land.at[0], size_b // 2, sems_b, 0)
+    step_a = halves("a", 2, a_work, a_land.at[0], size_a // 4, sems_a, 0) if levels > 2 else None
+    gcols, s1 = feat.shape[1] // mp, gyn1.shape[1] // mp
+    wide = feat.shape[1]
+    c_work[...] = jnp.zeros_like(c_work)
+    c_work[:gcols, :wide] = weight_grad(grad_gate[0], feat[...], mine, gcols)
+    c_work[gcols : gcols + s1, :wide] = weight_grad(gyn1[...], fields[0], mine, s1)
+    half_c = size_c // 2
+    copy_c = send_to(
+        remote(c_work.at[rows_at((1 - side) * half_c, half_c), :], c_land, csend.at[0], crecv.at[0], {"dp": flip(me, 0)})
+    )
+    small_copies = spread_dp(dp, lambda k: s_slots.at[k], ssend, srecv)
+    off_b, held_b = fold(step_b, b_work, b_land.at[0])
+    step_b = halves("b", 2, b_work, b_land.at[1], held_b, sems_b, off_b)
+    off_a, held_a = fold(step_a, a_work, a_land.at[0])
+    for level in range(3, levels):
+        step_a = halves("a", level, a_work, a_land.at[level - 2], held_a, sems_a, off_a)
+        off_a, held_a = fold(step_a, a_work, a_land.at[level - 2])
+    start_a = start_a + off_a
+    a_full[rows_at(start_a, held_a), :] = a_work[rows_at(off_a, held_a), :]
+    back_a = double(levels - 1, a_full, start_a, held_a, sems_a)
+    copy_t.wait_recv()
+    at = rows_at(side * half_t, half_t)
+    t_work[...] = low(grads[at, :].astype(jnp.float32) + t_land[...].astype(jnp.float32))
+    t_copies = []
+    for k in range(1, far):
+        to = lax.rem(place + k, far)
+        t_copies.append(
+            send_to(
+                remote(t_work.at[rows_at(to * tall, tall), :], t_slots.at[k - 1], tsend.at[k], trecv.at[k], across(k))
+            )
         )
-        copy.start()
-        copies.append(copy)
-    small_copies = spread_dp(dp, lambda k: s_slots.at[k], send3, recv3)
-    pend = [None, halve(1, 0)]
-    gcols, s1, s2 = feat.shape[1] // mp, gyn1.shape[1] // mp, gyb1.shape[1] // mp
-    g_rows, n_rows, b_rows = up16(gcols), up16(s1), up16(s2)
-    p_work[...] = jnp.zeros_like(p_work)
-    for k in range(2):
-        p_work[k * g_rows : k * g_rows + gcols, :] = weight_grad(grad_gate[k], feat[...], mine, gcols)
-    row = 2 * g_rows
-    p_work[row : row + s1, :] = weight_grad(gyn1[...], fields[0], mine, s1)
-    row += n_rows
-    p_work[row : row + s2, :] = weight_grad(gyb1[...], fields[1], mine, s2)
-    pend[0] = halve(0, 0)
-    for level in range(1, levels):
-        for w in (0, 1):
-            add(w, *pend[w])
-            pend[w] = halve(w, level)
-    total = grads[pl.ds(pl.multiple_of(me * tall, 16), tall), :].astype(jnp.float32)
-    for step in range(1, dp):
-        copies[step - 1].wait_recv()
-        total = total + landed[step - 1].astype(jnp.float32)
-    shares[mine] = total.astype(jnp.bfloat16)
-
-    def slot(i):
-        return shares.at[i]
-
-    started = relay_own(mp, slot, send2, recv2)
-    back = []
-    for w in (0, 1):
-        add(w, *pend[w])
-        at = pl.ds(pl.multiple_of(starts[w], 16), sizes[w])
-        fulls[w][at, :] = works[w][at, :]
-        back.append(double(w, levels - 1))
-    relay_rest(mp, slot, send2, recv2, started)
-    for level in range(levels - 2, -1, -1):
-        for w in (0, 1):
-            back[w].wait_recv()
-            waits.append(back[w])
-            back[w] = double(w, level)
+    copy_c.wait_recv()
+    at = rows_at(side * half_c, half_c)
+    c_work[at, :] = low(c_work[at, :].astype(jnp.float32) + c_land[...].astype(jnp.float32))
+    piece = half_c // far
+    c_copies = []
+    for k in range(1, far):
+        to = lax.rem(place + k, far)
+        c_copies.append(
+            send_to(
+                remote(
+                    c_work.at[rows_at(side * half_c + to * piece, piece), :], c_slots.at[k - 1],
+                    csend.at[k], crecv.at[k], across(k),
+                )
+            )
+        )
+    off_b, held_b = fold(step_b, b_work, b_land.at[1])
+    for level in range(3, levels):
+        step_b = halves("b", level, b_work, b_land.at[level - 1], held_b, sems_b, off_b)
+        off_b, held_b = fold(step_b, b_work, b_land.at[level - 1])
+    start_b = start_b + off_b
+    b_full[rows_at(start_b, held_b), :] = b_work[rows_at(off_b, held_b), :]
+    back_b = double(levels - 1, b_full, start_b, held_b, sems_b)
+
+    def onward(back, level, full, sems):
+        copy, start, size = back
+        copy.wait_recv()
+        return double(level, full, start, size, sems)
+
+    for level in range(levels - 2, 0, -1):
+        back_a = onward(back_a, level, a_full, sems_a)
+    total = t_work[rows_at(place * tall, tall), :].astype(jnp.float32)
+    for k in range(1, far):
+        t_copies[k - 1].wait_recv()
+        total = total + t_slots[k - 1].astype(jnp.float32)
+    shares[mine] = low(total)
+    started = relay_own(mp, lambda k: shares.at[k], ysend, yrecv)
+    own = rows_at(side * half_c + place * piece, piece)
+    total = c_work[own, :].astype(jnp.float32)
+    for k in range(1, far):
+        c_copies[k - 1].wait_recv()
+        total = total + c_slots[k - 1].astype(jnp.float32)
+    c_full[own, :] = low(total)
+    c_back = []
+    for k in range(1, far):
+        c_back.append(
+            send_to(
+                remote(c_full.at[own, :], c_full.at[own, :], csend.at[far + k], crecv.at[far + k], across(k))
+            )
+        )
+    back_a = onward(back_a, 0, a_full, sems_a)
+    for level in range(levels - 2, 0, -1):
+        back_b = onward(back_b, level, b_full, sems_b)
+    relay_rest(mp, lambda k: shares.at[k], ysend, yrecv, started)
+    for copy in c_back:
+        copy.wait_recv()
+    at = c_full.at[rows_at(side * half_c, half_c), :]
+    last_c = send_to(remote(at, at, csend.at[far], crecv.at[far], {"dp": flip(me, 0)}))
+    back_b = onward(back_b, 0, b_full, sems_b)
     for copy in small_copies:
         copy.wait_recv()
     value = s_slots[0]
     for d in range(1, dp):
         value = value + s_slots[d]
     small_out[...] = value
-    for w in (0, 1):
-        back[w].wait_recv()
-        waits.append(back[w])
-    for copy in copies + small_copies + waits:
+    back_a[0].wait_recv()
+    last_c.wait_recv()
+    back_b[0].wait_recv()
+    for copy in pending + small_copies:
         copy.wait_send()
 
 
 def final_kernel(
-    mp, hx, shares, p_full, q_full, small, logits_in, n_gain_in, n_shift_in, b_gain_in, b_shift_in,
+    mp, hx, shares, a_full, b_full, c_full, small, logits_in, n_gain_in, n_shift_in, b_gain_in, b_shift_in,
     left_in, right_in, bias_in,
     logits, num_g, table_g, gate_g, gate_bias_g, n_first_g, n_rest_g, n_gain_g, n_shift_g,
     b_first_g, b_rest_g, b_gain_g, b_shift_g, left_g, right_g, pair_g, bias_g,
 ):
     gcols, s1, s2, h1 = gate_g.shape[0], n_first_g.shape[0], b_first_g.shape[0], n_rest_g.shape[2]
-    g_rows, n_rows, b_rows = up16(gcols), up16(s1), up16(s2)
     wide = n_first_g.shape[1]
 
     def full(work, row, count, col, width):
@@ -878,15 +980,29 @@
             table_g[:, (m * blocks + b) * HI : (m * blocks + b + 1) * HI] = shares[
                 m, b * 16 : (b + 1) * 16, :
             ].astype(jnp.float32)
-    gate_g[:, 0, :] = full(p_full, 0, gcols, 0, wide)
-    gate_g[:, 1, :] = full(p_full, g_rows, gcols, 0, wide)
-    n_first_g[...] = full(p_full, 2 * g_rows, s1, 0, wide)
-    b_first_g[...] = full(p_full, 2 * g_rows + n_rows, s2, 0, wide)
-    n_rest_g[:, 0, :] = full(q_full, 0, s1, 0, h1)
-    n_rest_g[:, 1, :] = full(q_full, 0, s1, h1, h1)
-    b_rest_g[...] = full(q_full, n_rows, s2, 0, 2 * h1)
+    gate_g[:, 0, :] = full(c_full, 0, gcols, 0, wide)
+    gate_g[:, 1, :] = full(b_full, s2, gcols, 0, wide)
+    n_first_g[...] = full(c_full, gcols, s1, 0, wide)
+    b_first_g[...] = full(b_full, 0, s2, 0, wide)
+    main = a_full.shape[1]
+    rest = 2 * h1 - main
+    parts = main // rest
+    tall_a = s2 + s1
+    short = -(-tall_a // parts)
+    tail = jnp.concatenate(
+        [
+            full(a_full, tall_a, min(short, tall_a - p * short), p * rest, rest)
+            for p in range(parts)
+        ],
+        axis=0,
+    )
+    b_rest_g[:, :main] = full(a_full, 0, s2, 0, main)
+    b_rest_g[:, main:] = tail[:s2]
+    both = jnp.concatenate([full(a_full, s2, s1, 0, main), tail[s2:]], axis=1)
+    n_rest_g[:, 0, :] = both[:, :h1]
+    n_rest_g[:, 1, :] = both[:, h1:]
     heads = pair_g.shape[2]
-    pairs = q_full[n_rows + b_rows : n_rows + b_rows + 16, :h1]
+    pairs = b_full[b_full.shape[0] - 16 :, :h1]
     row = lax.broadcasted_iota(jnp.int32, (h1, heads), 0)
     col = lax.broadcasted_iota(jnp.int32, (h1, heads), 1)
     for i in range(hx):
@@ -1015,14 +1131,19 @@
     def up(x, n):
         return -(-x // n) * n
 
-    p_rows = up(2 * up(gcols, 16) + up(s1, 16) + up(s2, 16), 16 * dp)
-    q_rows = up(up(s1, 16) + up(s2, 16) + 16, 16 * dp)
+    main = wide // 128 * 128 + 128
+    short = -(-(s1 + s2) // (main // (h2 - main)))
+    a_rows = up(s1 + s2 + short, 16 * dp)
+    b_rows = up(s2 + gcols, 16) + 16
+    b_rows = up(b_rows, 16 * dp)
+    c_rows = up(gcols + s1, 16 * dp)
+    levels = dp.bit_length() - 1
     dense_args = (
         broad_first, broad_rest, joining_left.reshape(1, h1), joining_right,
         jnp.transpose(joining_pair, (1, 2, 0)), joining_bias.reshape(1, 1), labels.reshape(1, rows), dense_t,
     )
     (
-        logits, grads_t, feat, fields, grad_gate, gyn1, gyb1, q_part, small,
+        logits, grads_t, feat, fields, grad_gate, gyn1, a_part, b_part, small,
         n_gain_g, n_shift_g, b_gain_g, b_shift_g, left_g, right_g, bias_g,
     ) = pl.pallas_call(
         functools.partial(dense_kernel, dp, mp, hx, float(rows * dp)),
@@ -1033,8 +1154,8 @@
             b16(2, rows, wide),
             b16(2, rows, wide),
             b16(rows, h1),
-            b16(rows, h2),
-            b16(q_rows, h2),
+            b16(a_rows // 4, main),
+            b16(b_rows // 2, main),
             f32(8, 256),
             f32(3, s1),
             f32(3, s1),
@@ -1071,16 +1192,24 @@
             held(h2, h1),
             held(rows, h1),
             held(11, dp, 2, 896),
+            held16(s1 + s2, h2 - main),
             dma(chips + 1),
             dma(chips + 1),
             dma(3, mp),
             dma(3, mp),
             dma(11, dp - 1),
             dma(11, dp - 1),
+            held16(rows, h2),
+            held16(a_rows, main),
+            held16(b_rows, main),
+            held16(a_rows * 3 // 4, main),
+            held16(b_rows // 2, main),
+            dma(3),
+            dma(3),
         ]
         + [pltpu.VMEM(x.shape, x.dtype) for x in dense_args]
         + [dma(8)],
-        compiler_params=params(1, 39),
+        compiler_params=params(1, 39 + dp // 16),
         name="dense",
     )(partial, numeric, gates, n1, n_own, vec, *dense_args)
     row_sums = pl.pallas_call(
@@ -1092,35 +1221,45 @@
         compiler_params=params(None, 12),
         name="scatter",
     )(keys, grads_t)
-    shares, p_full, q_full, small = pl.pallas_call(
+    shares, a_full, b_full, c_full, small = pl.pallas_call(
         functools.partial(reduce_kernel, dp, mp),
         out_shape=(
             b16(mp, tall, HI),
-            b16(p_rows, wide),
-            b16(q_rows, h2),
+            b16(a_rows, main),
+            b16(b_rows, main),
+            b16(c_rows, main),
             f32(8, 256),
         ),
         in_specs=[VM] * 8,
-        out_specs=(VM,) * 4,
+        out_specs=(VM,) * 5,
         scratch_shapes=[
-            held16(dp - 1, tall, HI),
+            held16(dp // 2 * tall, HI),
+            held16(dp // 2 * tall, HI),
+            held16(dp // 2 - 1, tall, HI),
             held(dp, 8, 256),
-            held16(p_rows, wide),
-            held16(q_rows, h2),
-            held16(p_rows, wide),
-            held16(q_rows, h2),
-            dma(dp - 1),
-            dma(dp - 1),
+            held16(a_rows // 4, main),
+            held16(max(levels - 2, 1), a_rows // 8, main),
+            held16(b_rows // 2, main),
+            held16(max(levels - 1, 1), b_rows // 4, main),
+            held16(c_rows, main),
+            held16(c_rows // 2, main),
+            held16(dp // 2 - 1, c_rows // dp, main),
+            dma(dp // 2),
+            dma(dp // 2),
             dma(mp),
             dma(mp),
             dma(dp - 1),
             dma(dp - 1),
-            dma(2, 2 * (dp.bit_length() - 1)),
-            dma(2, 2 * (dp.bit_length() - 1)),
+            dma(2 * levels),
+            dma(2 * levels),
+            dma(2 * levels),
+            dma(2 * levels),
+            dma(dp),
+            dma(dp),
         ],
         compiler_params=params(2, 24),
         name="reduce",
-    )(row_sums, feat, fields, grad_gate, gyn1, gyb1, q_part, small)
+    )(row_sums, feat, fields, grad_gate, gyn1, a_part, b_part, small)
     outs = pl.pallas_call(
         functools.partial(final_kernel, mp, hx),
         out_shape=(
@@ -1142,12 +1281,12 @@
             f32(hx, width, joining_pair.shape[0]),
             f32(1, 1),
         ),
-        in_specs=[VM] * 12,
+        in_specs=[VM] * 13,
         out_specs=(VM,) * 17,
         compiler_params=params(None, 16),
         name="final",
     )(
-        shares, p_full, q_full, small, logits, n_gain_g, n_shift_g, b_gain_g, b_shift_g,
+        shares, a_full, b_full, c_full, small, logits, n_gain_g, n_shift_g, b_gain_g, b_shift_g,
         left_g, right_g, bias_g,
     )
     outs = list(outs)

time: 178 us -> 165 us (0.927); the launches traced: 178 us -> 163 us
  Pallas kernels: 171 us -> 156 us
    pallas_call x1, Pallas kernels: 58.2 us -> 39.9 us  [shards(): pl.pallas_call(functools.partial(reduce_kernel, dp, mp), out_shape=(b16(m...]
    pallas_call x1, Pallas kernels: 63.1 us -> 67.7 us  [shards(): pl.pallas_call(functools.partial(dense_kernel, dp, mp, hx, float(rows * d...]
where the time goes in v4:
time: 165 us; the launch traced here: 163 us
  Pallas kernels  156 us (95%)
  local copies, waits for them, and re-layouts  5.87 us (4%)
    pallas_call x1, Pallas kernels, shards(): pl.pallas_call(functools.partial(dense_kernel, dp, mp, hx, float(rows * d...  67.7 us
    pallas_call x1, Pallas kernels, shards(): pl.pallas_call(functools.partial(reduce_kernel, dp, mp), out_shape=(b16(m...  39.9 us
    pallas_call x1, Pallas kernels, shards(): pl.pallas_call(functools.partial(first_kernel, dp, mp, own_rows, bits), o...  24.3 us
    pallas_call x1, Pallas kernels, shards(): pl.pallas_call(functools.partial(scatter_kernel, cats, rows, bits), out_s...  10.3 us
    pallas_call x1, Pallas kernels, shards(): pl.pallas_call(functools.partial(lookup_kernel, cats, rows, bits), out_sh...  10.3 us
    unnamed x30, local copies, waits for them, and re-layouts  5.87 us

profile of v4, /device:TPU:0, one launch (start us, length us, event | category | flops | bytes accessed | tf_op | source)
XLA Modules:
  0.0 163.0 jit_solution(6103221817458342015)
XLA Ops:
  1.3 0.0 copy-start.5
  1.3 0.0 copy-start.7
  1.3 0.0 copy-start.9
  1.3 0.0 copy-start.10
  1.4 0.0 copy-start.12
  1.4 0.0 copy-start.13
  1.4 0.0 copy-start.14
  1.4 24.3 %first.1 = (bf16[1024,256]{1,0:T(8,128)(2,1)}, s32[128,512]{1,0:T(8,128)}, bf16[512,208]{1,0:T(8,128)(2,1)}, bf16[2,624,624]{2,1,0:T(8,128)(2,1)}, bf16[400,624]...) custom-call(f32[16,8192]{1,0:T(8,128)} %refs_0_.1, bf16[156,2,624]{2,1,0:T(2,128)(2,1)} %bitcast.19, ...), custom_call_target="tpu_custom_call" | custom-call | tf_op jit(solution)/shard_map/first/pallas_call | solution.py:1093
  25.7 0.0 copy-start
  25.7 0.0 copy-start.1
  25.7 1.1 copy-done.1
  26.8 1.0 copy-done.3
  27.8 10.3 %lookup.1.partial = f32[416,512]{1,0:T(8,128)S(1)} custom-call(s32[128,512]{1,0:T(8,128)S(1)} %copy-done.1, bf16[1024,256]{1,0:T(8,128)(2,1)S(1)} %copy-done.3), custom_call_target="tpu_custom_call" | custom-call | tf_op jit(solution)/shard_map/lookup/pallas_call | solution.py:1121
  38.2 0.0 copy-done.5
  38.2 0.0 copy-done.7
  38.2 0.0 copy-done.9
  38.3 1.0 copy-done.4
  39.3 0.9 copy-done.6
  40.2 0.9 copy-done.8
  41.2 0.8 copy-done.11
  42.0 67.7 %dense.1 = (f32[1,512]{1,0:T(1,128)S(1)}, bf16[416,512]{1,0:T(8,128)(2,1)S(1)}, bf16[512,624]{1,0:T(8,128)(2,1)S(1)}, bf16[2,512,624]{2,1,0:T(8,128)(2,1)S(1)}, ...) custom-call(f32[416,512]{1,0:T(8,128)S(1)} %lookup.1.partial, ...), custom_call_target="tpu_custom_call" | custom-call | tf_op jit(solution)/shard_map/dense/pallas_call | solution.py:1148
  109.7 10.3 %scatter.1.grads = bf16[1024,256]{1,0:T(8,128)(2,1)S(1)} custom-call(s32[128,512]{1,0:T(8,128)S(1)} %copy-done.2, bf16[416,512]{1,0:T(8,128)(2,1)S(1)} %get-tuple-element.69.grad), custom_call_target="tpu_custom_call" | custom-call | tf_op jit(solution)/shard_map/scatter/pallas_call | solution.py:1215
  120.1 39.9 %reduce.1 = (bf16[4,128,256]{2,1,0:T(8,128)(2,1)S(1)}, bf16[384,640]{1,0:T(8,128)(2,1)S(1)}, bf16[384,640]{1,0:T(8,128)(2,1)S(1)}, bf16[256,640]{1,0:T(8,128)(2,1)S(1)}, f32[8,256]{1,0:T(8,128)S(1)}) custom-call(bf16[1024,256]{1,0:T(8,128)(2,1)S(1)} %scatter.1.grads, bf16[512,624]{1,0:T(8,128)(2,1)S(1)} %get-tuple-element.70.feat, ...), custom_call_target="tpu_custom_call" | custom-call | tf_op jit(solution)/shard_map/reduce/pallas_call | solution.py:1224
  160.0 3.0 %final.1 = (f32[1,512]{1,0:T(1,128)}, f32[13,16]{1,0:T(8,128)}, f32[16,8192]{1,0:T(8,128)}, f32[156,2,624]{2,1,0:T(2,128)}, f32[2,156]{1,0:T(2,128)}, /*index=5*...) custom-call(bf16[4,128,256]{2,1,0:T(8,128)(2,1)S(1)} %get-tuple-elem, ...), custom_call_target="tpu_custom_call" | custom-call | tf_op jit(solution)/shard_map/final/pallas_call | solution.py:1263
  (12 shorter events, 0.0 us)
Async XLA Ops:
  1.3 36.9 %copy-start.5 = (bf16[200,800]{1,0:T(8,128)(2,1)S(1)}, bf16[200,800]{1,0:T(8,128)(2,1)}, u32[]{:S(2)}) copy-start(bf16[200,800]{1,0:T(8,128)(2,1)} %b_rest_hbm.1) | copy-start | bytes 960004
  1.3 36.9 %copy-start.7 = (bf16[200,624]{1,0:T(8,128)(2,1)S(1)}, bf16[200,624]{1,0:T(8,128)(2,1)}, u32[]{:S(2)}) copy-start(bf16[200,624]{1,0:T(8,128)(2,1)} %b_first_hbm.1) | copy-start | bytes 748804
  1.3 36.9 %copy-start.9 = (f32[512,13]{0,1:T(8,128)S(1)}, f32[512,13]{0,1:T(8,128)}, u32[]{:S(2)}) copy-start(f32[512,13]{0,1:T(8,128)} %param.20) | copy-start | bytes 79876
  1.3 36.9 %copy-start.10 = (f32[50,8,16]{0,2,1:T(8,128)S(1)}, f32[50,8,16]{0,2,1:T(8,128)}, u32[]{:S(2)}) copy-start(f32[50,8,16]{0,2,1:T(8,128)} %param.38) | copy-start | bytes 76804
  1.4 36.9 %copy-start.12 = (f32[800]{0:T(1024)S(1)}, f32[800]{0:T(1024)}, u32[]{:S(2)}) copy-start(f32[800]{0:T(1024)} %right_hbm.1) | copy-start | bytes 9604
  1.4 36.9 %copy-start.13 = (f32[400]{0:T(512)S(1)}, f32[400]{0:T(512)}, u32[]{:S(2)}) copy-start(f32[400]{0:T(512)} %param.36) | copy-start | bytes 4804
  1.4 36.9 %copy-start.14 = (s32[512]{0:T(512)S(1)}, s32[512]{0:T(512)}, u32[]{:S(2)}) copy-start(s32[512]{0:T(512)} %param.23) | copy-start | bytes 6148
  25.7 12.5 %copy-start = (bf16[2,624,624]{2,1,0:T(8,128)(2,1)S(1)}, bf16[2,624,624]{2,1,0:T(8,128)(2,1)}, u32[]{:S(2)}) copy-start(bf16[2,624,624]{2,1,0:T(8,128)(2,1)} %get-tuple-element.65.gates) | copy-start | bytes 4672516
  25.7 1.1 copy-start.1
  26.8 1.0 copy-start.3
  38.3 1.0 copy-start.4
  39.3 0.9 copy-start.6
  40.2 0.9 copy-start.8
  41.2 0.8 copy-start.11
  42.0 67.7 %copy-start.2 = (s32[128,512]{1,0:T(8,128)S(1)}, s32[128,512]{1,0:T(8,128)}, u32[]{:S(2)}) copy-start(s32[128,512]{1,0:T(8,128)} %get-tuple-element.62.keys) | copy-start | bytes 786436

commit v5 on v4

--- a/solution.py
+++ b/solution.py
@@ -10,7 +10,7 @@
 VM = pl.BlockSpec(memory_space=pltpu.VMEM)
 ANY = pl.BlockSpec(memory_space=pltpu.HBM)
 HI = 256
-CHUNK = 512
+CHUNK = 1024
 
 
 def params(cid, mib=48):
@@ -56,53 +56,49 @@
     return out
 
 
+def over(x, n):
+    if n & (n - 1) == 0:
+        return lax.shift_right_logical(x, n.bit_length() - 1)
+    return x // n
+
+
 def compact_keys(key):
     count = key.shape[0]
-    dead = (key < 0).astype(jnp.int32)
+    rows = count * 8
+    dead = jnp.where(key.reshape(rows, 128) < 0, 1.0, 0.0).astype(jnp.bfloat16)
+    row = lax.broadcasted_iota(jnp.int32, (128, 128), 0)
+    col = lax.broadcasted_iota(jnp.int32, (128, 128), 1)
+    in_row = jnp.dot(dead, jnp.where(row < col, 1.0, 0.0).astype(jnp.bfloat16), preferred_element_type=jnp.float32)
+    row_sum = jnp.dot(dead, jnp.ones((128, 128), jnp.bfloat16), preferred_element_type=jnp.float32)
+    row = lax.broadcasted_iota(jnp.int32, (rows, rows), 0)
+    col = lax.broadcasted_iota(jnp.int32, (rows, rows), 1)
+    above = jnp.where(col < row, 1.0, 0.0).astype(jnp.bfloat16)
+    before = jnp.dot(above, row_sum.astype(jnp.bfloat16), preferred_element_type=jnp.float32)
+    shift = (in_row + before).astype(jnp.int32).reshape(count, 8, 128)
+    shift = jnp.where(key < 0, 0, shift)
     sub = lax.broadcasted_iota(jnp.int32, (8, 128), 0)
     lane = lax.broadcasted_iota(jnp.int32, (8, 128), 1)
-    running = jnp.zeros((8, 128), jnp.int32)
-    before = []
-    for v in range(count):
-        before.append(running)
-        running = running + dead[v]
-    scan = running
-    for k in (1, 2, 4):
-        scan = scan + jnp.where(sub >= k, pltpu.roll(scan, k, 0), 0)
-    over_sub = scan - running
-    column = jnp.broadcast_to(jnp.sum(running, axis=0, keepdims=True), (8, 128))
-    scan = column
-    for k in (1, 2, 4, 8, 16, 32, 64):
-        scan = scan + jnp.where(lane >= k, pltpu.roll(scan, k, 1), 0)
-    base = over_sub + scan - column
-    shift = jnp.stack([jnp.where(dead[v] > 0, 0, before[v] + base) for v in range(count)])
-
-    def next_place(x):
-        n = x.shape[0]
-        flat = x.reshape(n * 8, 128)
-        y = jnp.stack([pltpu.roll(x[v], 7, 0) for v in range(n)])
-        z = jnp.stack([pltpu.roll(y[v], 127, 1) for v in range(n)])
-        return jnp.where(sub[None] < 7, y, z)
+
+    def rows_up(x, j):
+        t = [pltpu.roll(x[v], 8 - j, 0) for v in range(count)]
+        return jnp.stack([jnp.where(sub < 8 - j, t[v], t[(v + 1) % count]) for v in range(count)])
 
     bit = 0
+    for j in (1, 2, 4, 8, 16, 32, 64):
+        def lanes_up(x):
+            y = jnp.stack([pltpu.roll(x[v], 128 - j, 1) for v in range(count)])
+            return jnp.where(lane[None] < 128 - j, y, rows_up(y, 1))
+        key, shift = settle(key, shift, lanes_up(key), lanes_up(shift), bit)
+        bit += 1
+    for j in (1, 2, 4):
+        key, shift = settle(key, shift, rows_up(key, j), rows_up(shift, j), bit)
+        bit += 1
     step = 1
     while step < count:
-        moved_key = jnp.concatenate([key[step:], next_place(key[:step])], axis=0)
-        moved_shift = jnp.concatenate([shift[step:], next_place(shift[:step])], axis=0)
+        moved_key = jnp.concatenate([key[step:], key[:step]], axis=0)
+        moved_shift = jnp.concatenate([shift[step:], shift[:step]], axis=0)
         key, shift = settle(key, shift, moved_key, moved_shift, bit)
         bit, step = bit + 1, step * 2
-    for j in (1, 2, 4):
-        def roll_sub(x):
-            y = jnp.stack([pltpu.roll(x[v], 8 - j, 0) for v in range(count)])
-            z = jnp.stack([pltpu.roll(y[v], 127, 1) for v in range(count)])
-            return jnp.where(sub[None] < 8 - j, y, z)
-        key, shift = settle(key, shift, roll_sub(key), roll_sub(shift), bit)
-        bit += 1
-    for j in (1, 2, 4, 8, 16, 32, 64):
-        def roll_lane(x):
-            return jnp.stack([pltpu.roll(x[v], 128 - j, 1) for v in range(count)])
-        key, shift = settle(key, shift, roll_lane(key), roll_lane(shift), bit)
-        bit += 1
     return key
 
 
@@ -141,75 +137,140 @@
     lax.fori_loop(0, cats, body, 0)
 
 
+WINDOW = 16
+
+
+def chunk_parts(key, rows, bits):
+    place = lax.shift_right_arithmetic(key, bits)
+    bag = key & ((1 << bits) - 1)
+    cat = over(bag, rows)
+    return place, cat, bag - cat * rows
+
+
+def short(row):
+    return jnp.broadcast_to(row, (16, row.shape[1])).astype(jnp.int16)
+
+
+def one_hot(row, size):
+    apart = short(row) - lax.broadcasted_iota(jnp.int32, (16, row.shape[1]), 0).astype(jnp.int16)
+    one = jnp.ones(apart.shape, jnp.bfloat16)
+    zero = jnp.zeros(apart.shape, jnp.bfloat16)
+    return jnp.concatenate([jnp.where(apart == i, one, zero) for i in range(0, size, 16)], axis=0)
+
+
+def spread_rows(row, values, first, size):
+    zero = jnp.zeros_like(values)
+    apart = short(row - first)
+    return jnp.concatenate([jnp.where(apart == i, values, zero) for i in range(size)], axis=0)
+
+
+def chunk_key(keys, half, k):
+    tall = CHUNK // 128
+    key = keys[half, pl.ds(pl.multiple_of(k * tall, tall), tall), :]
+    return jnp.concatenate([key[i : i + 1, :] for i in range(tall)], axis=1)
+
+
+def chunk_span(keys, half, k, cats, rows, bits):
+    tall = CHUNK // 128
+    most = keys.shape[1] // tall - 1
+    key = keys[half, pl.ds(pl.multiple_of(jnp.minimum(k, most) * tall, tall), tall), :]
+    cat = over(key & ((1 << bits) - 1), rows)
+    first = jnp.min(jnp.where(key >= 0, cat, cats - 1))
+    last = jnp.max(jnp.where(key >= 0, cat, 0))
+    return first, (last - first) // WINDOW + 1
+
+
+def each_chunk(keys, half, cats, rows, bits, body):
+    live = jnp.sum((keys[half] >= 0).astype(jnp.int32))
+    chunks = (live + CHUNK - 1) // CHUNK
+
+    def step(k, carry):
+        later = chunk_span(keys, half, k + 1, cats, rows, bits)
+        body(chunk_key(keys, half, k), *carry)
+        return later
+
+    lax.fori_loop(0, chunks, step, chunk_span(keys, half, 0, cats, rows, bits))
+
+
 def lookup_kernel(cats, rows, bits, keys, t2, pooled, total):
-    lows = t2.shape[0] // 16
-    filled = jnp.max(keys[...], axis=1, keepdims=True) >= 0
-    chunks = jnp.sum(filled.astype(jnp.int32))
+    lows = t2.shape[0] // 32
     total[...] = jnp.zeros_like(total)
-    hi_iota = lax.broadcasted_iota(jnp.int32, (HI, CHUNK), 0)
-    event_iota = lax.broadcasted_iota(jnp.int32, (rows, CHUNK), 0)
-
-    def body(k, carry):
-        key = keys[pl.ds(k, 1), :]
-        place = lax.shift_right_arithmetic(key, bits)
-        bag = key & ((1 << bits) - 1)
-        cat = bag // rows
-        event = bag - cat * rows
-        low = lax.shift_right_arithmetic(place, 8)
-        high = place & (HI - 1)
-        pick = jnp.where(hi_iota == high, 1.0, 0.0).astype(jnp.bfloat16)
-        z = jnp.zeros((16, CHUNK), jnp.float32)
-        for b in range(0, lows, 16):
-            n = min(16, lows - b)
-            y = jnp.dot(t2[b * 16 : (b + n) * 16, :], pick, preferred_element_type=jnp.float32)
-            for j in range(n):
-                z = z + jnp.where(low == b + j, y[j * 16 : (j + 1) * 16], 0.0)
-        z = z.astype(jnp.bfloat16)
-        zero = jnp.zeros_like(z)
-        wide = jnp.concatenate([jnp.where(cat == c, z, zero) for c in range(cats)], axis=0)
-        place_of = jnp.where(event_iota == event, 1.0, 0.0).astype(jnp.bfloat16)
-        total[...] += lax.dot_general(
-            wide, place_of, (((1,), (1,)), ((), ())), preferred_element_type=jnp.float32
-        )
+
+    def half_table(half, carry):
+        def body(key, first, windows):
+            place, cat, event = chunk_parts(key, rows, bits)
+            low = jnp.broadcast_to(lax.shift_right_arithmetic(place, 8) - half * lows, (16, CHUNK))
+            pick = one_hot(place & (HI - 1), HI)
+            z = jnp.zeros((16, CHUNK), jnp.float32)
+            for b in range(0, lows, 32):
+                n = min(32, lows - b)
+                at = pl.ds(pl.multiple_of((half * lows + b) * 16, 16), n * 16)
+                y = jnp.dot(t2[at, :], pick, preferred_element_type=jnp.float32)
+                for j in range(n):
+                    z = z + jnp.where(low == b + j, y[j * 16 : (j + 1) * 16], 0.0)
+            z = z.astype(jnp.bfloat16)
+            cat = jnp.where(key >= 0, cat, -1)
+            place_of = one_hot(event, rows)
+
+            def window(w):
+                start = first + w * WINDOW
+                at = pl.ds(pl.multiple_of(start * 16, 16), WINDOW * 16)
+                total[at, :] += lax.dot_general(
+                    spread_rows(cat, z, start, WINDOW), place_of, (((1,), (1,)), ((), ())),
+                    preferred_element_type=jnp.float32,
+                )
+
+            window(0)
+
+            def more(w, carry):
+                window(w)
+                return carry
+
+            lax.fori_loop(1, windows, more, 0)
+
+        each_chunk(keys, half, cats, rows, bits, body)
         return carry
 
-    lax.fori_loop(0, chunks, body, 0)
-    pooled[...] = total[...].astype(pooled.dtype)
-
-
-def scatter_kernel(cats, rows, bits, keys, grad, out, total):
-    lows = total.shape[0] // 16
-    filled = jnp.max(keys[...], axis=1, keepdims=True) >= 0
-    chunks = jnp.sum(filled.astype(jnp.int32))
+    lax.fori_loop(0, 2, half_table, 0)
+    pooled[...] = total[: cats * 16, :].astype(pooled.dtype)
+
+
+def scatter_kernel(cats, rows, bits, keys, grad, out, total, grad_pad):
+    lows = total.shape[0] // 32
     total[...] = jnp.zeros_like(total)
-    hi_iota = lax.broadcasted_iota(jnp.int32, (HI, CHUNK), 0)
-    event_iota = lax.broadcasted_iota(jnp.int32, (rows, CHUNK), 0)
-
-    def body(k, carry):
-        key = keys[pl.ds(k, 1), :]
-        place = lax.shift_right_arithmetic(key, bits)
-        bag = key & ((1 << bits) - 1)
-        cat = bag // rows
-        event = bag - cat * rows
-        low = lax.shift_right_arithmetic(place, 8)
-        high = place & (HI - 1)
-        place_of = jnp.where(event_iota == event, 1.0, 0.0).astype(jnp.bfloat16)
-        wide = jnp.dot(grad[...], place_of, preferred_element_type=jnp.float32)
-        g = jnp.zeros((16, CHUNK), jnp.float32)
-        for c in range(cats):
-            g = g + jnp.where(cat == c, wide[c * 16 : (c + 1) * 16], 0.0)
-        g = g.astype(jnp.bfloat16)
-        zero = jnp.zeros_like(g)
-        pick = jnp.where(hi_iota == high, 1.0, 0.0).astype(jnp.bfloat16)
-        for b in range(0, lows, 16):
-            n = min(16, lows - b)
-            tall = jnp.concatenate([jnp.where(low == b + j, g, zero) for j in range(n)], axis=0)
-            total[b * 16 : (b + n) * 16, :] += lax.dot_general(
-                tall, pick, (((1,), (1,)), ((), ())), preferred_element_type=jnp.float32
-            )
+    grad_pad[: cats * 16, :] = grad[...]
+    grad_pad[cats * 16 :, :] = jnp.zeros((WINDOW * 16, rows), jnp.bfloat16)
+
+    def half_table(half, carry):
+        def body(key, first, windows):
+            place, cat, event = chunk_parts(key, rows, bits)
+            low = lax.shift_right_arithmetic(place, 8) - half * lows
+            pick = one_hot(place & (HI - 1), HI)
+            place_of = one_hot(event, rows)
+            cat = jnp.broadcast_to(jnp.where(key >= 0, cat, -1), (16, CHUNK))
+
+            def window(w, g):
+                start = first + w * WINDOW
+                at = pl.ds(pl.multiple_of(start * 16, 16), WINDOW * 16)
+                wide = jnp.dot(grad_pad[at, :], place_of, preferred_element_type=jnp.float32)
+                for c in range(WINDOW):
+                    g = g + jnp.where(cat == start + c, wide[c * 16 : (c + 1) * 16], 0.0)
+                return g
+
+            g = window(0, jnp.zeros((16, CHUNK), jnp.float32))
+            g = lax.fori_loop(1, windows, window, g).astype(jnp.bfloat16)
+            for b in range(0, lows, 32):
+                n = min(32, lows - b)
+                at = pl.ds(pl.multiple_of((half * lows + b) * 16, 16), n * 16)
+                total[at, :] += lax.dot_general(
+                    spread_rows(low, g, b, n), pick, (((1,), (1,)), ((), ())),
+                    preferred_element_type=jnp.float32,
+                )
+
+        each_chunk(keys, half, cats, rows, bits, body)
         return carry
 
-    lax.fori_loop(0, chunks, body, 0)
+    lax.fori_loop(0, 2, half_table, 0)
     out[...] = total[...].astype(out.dtype)
 
 
@@ -285,6 +346,55 @@
     )
 
 
+def split_relay(dp, mp, ref, send, recv):
+    me, mine = lax.axis_index("dp"), lax.axis_index("mp")
+    other = mine + 1 - 2 * lax.rem(mine, 2)
+    chips = mp // 2
+    near = lax.rem(me, 2)
+    beside = {"dp": me + 1 - 2 * near}
+    started = []
+
+    def move(place, i, where):
+        return remote(place, place, send.at[i], recv.at[i], where)
+
+    def go(place, i, where):
+        copy = move(place, i, where)
+        copy.start()
+        started.append(copy)
+
+    def source(k):
+        return lax.rem(mine + mp - 2 * k, mp)
+
+    def begin():
+        for k in range(1, chips):
+            go(ref.at[mine, near], k, {"mp": lax.rem(mine + 2 * k, mp)})
+        go(ref.at[mine], 0, {"mp": other})
+
+    def middle():
+        for k in range(1, chips):
+            place = ref.at[source(k), near]
+            move(place, k, beside).wait_recv()
+            go(place, 2 * chips + k, beside)
+            go(place, chips + k, {"mp": other})
+
+    def later():
+        for k in range(1, chips):
+            place = ref.at[source(k), 1 - near]
+            move(place, 2 * chips + k, beside).wait_recv()
+            go(place, 3 * chips + k, {"mp": other})
+
+    def end():
+        move(ref.at[other], 0, beside).wait_recv()
+        for k in range(1, chips):
+            far = lax.rem(other + mp - 2 * k, mp)
+            move(ref.at[far, near], chips + k, beside).wait_recv()
+            move(ref.at[far, 1 - near], 3 * chips + k, beside).wait_recv()
+        for copy in started:
+            copy.wait_send()
+
+    return begin, middle, later, end
+
+
 def bring(sources, places, sem):
     copies = []
     for i, (source, place) in enumerate(zip(sources, places)):
@@ -295,14 +405,17 @@
 
 
 def first_kernel(dp, mp, own_rows, bits, *refs):
-    count = 13
+    count = 14
     sources, refs = refs[:count], refs[count:]
-    t2, keys, numeric, gates, n1, vec, n_own = refs[:7]
-    places, refs = refs[7 : 7 + count], refs[7 + count :]
-    scratch, gate_slots, n_slots, v_slots, send, recv, send2, recv2, sem = refs
+    t2, keys, numeric, weights, vec, n_own = refs[:6]
+    places, refs = refs[6 : 6 + count], refs[6 + count :]
+    (
+        scratch, gate_slots, n_slots, b_slots, v_slots,
+        send, recv, send2, recv2, send3, recv3, sem,
+    ) = refs
     brought = bring(sources, places, sem)
     (
-        table, gate_w, n_first, gate_b, n_gain, n_shift, b_gain, b_shift,
+        table, gate_w, n_first, gate_b, n_gain, n_shift, b_gain, b_shift, b_first,
         ids, lens, dense_t, num_embed, n_rest,
     ) = places
     part = own_rows // mp
@@ -310,14 +423,17 @@
     tall = blocks * 16
     me, mine = lax.axis_index("dp"), lax.axis_index("mp")
     hail(dp, mp)
-    for copy in brought[:8]:
+    for copy in brought[:9]:
         copy.wait()
     own = table[:, pl.ds(pl.multiple_of(mine * part, HI), part)].astype(jnp.bfloat16)
     for b in range(blocks):
         t2[pl.ds(pl.multiple_of(seat(me, dp) * tall + b * 16, 16), 16), :] = own[:, b * HI : (b + 1) * HI]
     for k in range(2):
         gate_slots[mine, k] = gate_w[:, k, :]
-    n_slots[mine] = n_first[...]
+    small, large = n_slots.shape[2], b_slots.shape[2]
+    for k in range(2):
+        n_slots[mine, k] = n_first[k * small : (k + 1) * small, :]
+        b_slots[mine, k] = b_first[k * large : (k + 1) * large, :]
     row = 0
     for ref in (gate_b, n_gain, n_shift, b_gain, b_shift):
         v_slots[mine, row : row + ref.shape[0], : ref.shape[1]] = ref[...]
@@ -327,12 +443,17 @@
     def slot(i):
         return t2.at[pl.ds(pl.multiple_of(seat(i, dp) * tall, 16), tall), :]
 
+    pairs = [
+        split_relay(dp, mp, ref, send3.at[i], recv3.at[i]) for i, ref in enumerate((n_slots, b_slots))
+    ]
+    for steps in pairs:
+        steps[0]()
     groups = []
-    for i, ref in enumerate((gate_slots, n_slots, v_slots)):
+    for i, ref in enumerate((gate_slots, v_slots)):
         started = relay_own(mp, lambda k, ref=ref: ref.at[k], send2.at[i], recv2.at[i])
         groups.append((ref, i, started))
     copies = spread_dp(dp, slot, send, recv)
-    for copy in brought[8:]:
+    for copy in brought[9:]:
         copy.wait()
     for k in range(2):
         n_own[k] = n_rest[:, k, :]
@@ -344,15 +465,34 @@
     numeric[...] = low(widen_dense(dense_t[...], width) * num_row)
     make_keys(ids, lens, scratch, own_rows, dp, mp, bits)
     count = scratch.shape[0] // 8
-    packed = compact_keys(scratch[...].reshape(count, 8, 128))
-    keys[...] = jnp.transpose(packed.reshape(count * 8, 128))
+    middle = (dp * part // 2) << bits
+
+    def pack(half, carry):
+        key = scratch[...]
+        key = jnp.where((key < middle) == (half == 0), key, -1)
+        keys[half] = compact_keys(key.reshape(count, 8, 128)).reshape(count * 8, 128)
+        return carry
+
+    lax.fori_loop(0, 2, pack, 0)
+    for steps in pairs:
+        steps[1]()
     for ref, i, started in groups:
         relay_rest(mp, lambda k, ref=ref: ref.at[k], send2.at[i], recv2.at[i], started)
-    cols, small = gate_slots.shape[2], n_first.shape[0]
+    cols, wide = gate_slots.shape[2], gate_slots.shape[3]
     for m in range(mp):
         for k in range(2):
-            gates[k, m * cols : (m + 1) * cols, :] = gate_slots[m, k]
-        n1[m * small : (m + 1) * small, :] = n_slots[m]
+            row = k * wide + m * cols
+            weights[row : row + cols, :] = gate_slots[m, k]
+    for steps in pairs:
+        steps[2]()
+    row = 2 * wide
+    for ref, steps in zip((n_slots, b_slots), pairs):
+        steps[3]()
+        tall = ref.shape[2]
+        for m in range(mp):
+            for k in range(2):
+                weights[row : row + tall, :] = ref[m, k]
+                row += tall
     row = 0
     for ref in (gate_b, n_gain, n_shift, b_gain, b_shift):
         r, w = ref.shape
@@ -375,17 +515,14 @@
     return -(-x // 16) * 16
 
 
-def own_part(x, mine, width):
-    full = x.shape[1]
-    pad = -(-width // 128) * 128
-    row = lax.broadcasted_iota(jnp.int32, (full, pad), 0)
-    col = lax.broadcasted_iota(jnp.int32, (full, pad), 1)
-    choose = jnp.where((row == col + mine * width) & (col < width), 1.0, 0.0).astype(jnp.bfloat16)
-    return low(nn(x, choose))
-
-
-def weight_grad(grad_y, inputs, mine, width):
-    return low(tn(own_part(grad_y, mine, width), inputs)[:width, :])
+def weight_grad(grad_y, inputs, own, mine, width, mp):
+    for m in range(mp):
+
+        @pl.when(mine == m)
+        def _():
+            own[:, :width] = grad_y[:, m * width : (m + 1) * width]
+
+    return low(tn(own[:, :width], inputs))
 
 
 def flip(me, level):
@@ -414,19 +551,19 @@
 
 def dense_kernel(
     dp, mp, hx, batch,
-    partial, numeric, gates, n1, n_rest, vec,
-    b_first_hbm, b_rest_hbm, left_hbm, right_hbm, pair_hbm, bias_hbm, labels_hbm, dense_hbm,
+    partial, numeric, weights, n_rest, vec,
+    b_rest_hbm, left_hbm, right_hbm, pair_hbm, bias_hbm, labels_hbm, dense_hbm,
     logits, grads_t, feat, fields, grad_gate, gyn1, a_out, b_out, small,
     n_gain_g, n_shift_g, b_gain_g, b_shift_g, left_g, right_g, bias_g,
-    half_a, half_c, pooled, gate, own_term, b1_slots, n_slots, b_slots, b1, n23, b2,
+    half_a, half_c, pooled, gate, own_term, n_slots, b_slots, n23, b2,
     yn, dn, yb, db, un, ub, gyn, gyb, pair_hi, pair_lo, pair_g, to_first, sums, spill,
     fsend, frecv, wsend, wrecv, ssend, srecv,
-    gyb1, a_work, b_work, a_land, b_land, hsend, hrecv,
-    b_first, b_rest, left, right, pair_t, bias, labels, dense_t, sem,
+    gyb1, a_work, b_work, a_land, b_land, hsend, hrecv, own_cols,
+    b_rest, left, right, pair_t, bias, labels, dense_t, sem,
 ):
     brought = bring(
-        (b_first_hbm, b_rest_hbm, left_hbm, right_hbm, pair_hbm, bias_hbm, labels_hbm, dense_hbm),
-        (b_first, b_rest, left, right, pair_t, bias, labels, dense_t),
+        (b_rest_hbm, left_hbm, right_hbm, pair_hbm, bias_hbm, labels_hbm, dense_hbm),
+        (b_rest, left, right, pair_t, bias, labels, dense_t),
         sem,
     )
     me, mine = lax.axis_index("dp"), lax.axis_index("mp")
@@ -435,11 +572,14 @@
     chips = mp // 2
     other = mine + 1 - 2 * core
     rows = feat.shape[0]
-    block = 128
+    block = 256
     steps = rows // block
-    h1, h2 = n1.shape[0], b1.shape[0]
+    h1, h2 = n23.shape[1], b2.shape[0]
     s1, s2 = h1 // mp, h2 // mp
     wide = feat.shape[1]
+    gates = (weights.at[pl.ds(0, wide), :], weights.at[pl.ds(wide, wide), :])
+    n1 = weights.at[pl.ds(2 * wide, h1), :]
+    b1 = weights.at[pl.ds(2 * wide + h1, h2), :]
     num = numeric.shape[1]
     gcols = wide // mp
     half = partial.shape[0] // 2
@@ -453,22 +593,31 @@
     def part(c):
         return pl.ds(pl.multiple_of(c * half, 16), half)
 
-    copy_a = remote(partial.at[part(1 - core), :], half_a, fsend.at[0], frecv.at[0], {"mp": other})
-    copy_a.start()
+    def events(h):
+        return pl.ds(h * (rows // 2), rows // 2)
+
+    copies_a, copies_y, copies_b = [], [], []
+    for h in range(2):
+        copy = remote(
+            partial.at[part(1 - core), events(h)], half_a.at[:, events(h)], fsend.at[h, 0], frecv.at[h, 0],
+            {"mp": other},
+        )
+        copy.start()
+        copies_a.append(copy)
     for copy in brought:
         copy.wait()
-    b1_slots[mine] = b_first[...]
-    b_slots[mine] = b_rest[...]
-    copy_a.wait_recv()
-    half_c[chip] = low(partial[part(core), :] + half_a[...])
-    copies = []
-    for k in range(1, chips):
-        copy = remote(
-            half_c.at[chip], half_c.at[chip], fsend.at[k], frecv.at[k],
-            {"mp": lax.rem(mine + 2 * k, mp)},
-        )
-        copy.start()
-        copies.append(copy)
+    for k in range(2):
+        b_slots[mine, k] = b_rest[k * (s2 // 2) : (k + 1) * (s2 // 2), :]
+    for h in range(2):
+        copies_a[h].wait_recv()
+        half_c[chip, :, events(h)] = low(partial[part(core), events(h)] + half_a[:, events(h)])
+        for k in range(1, chips):
+            place = half_c.at[chip, :, events(h)]
+            copy = remote(
+                place, place, fsend.at[h, k], frecv.at[h, k], {"mp": lax.rem(mine + 2 * k, mp)}
+            )
+            copy.start()
+            copies_y.append(copy)
     heads = pair_t.shape[2]
     by_head = jnp.transpose(pair_t[...].reshape(hx * 16, heads))
     row = lax.broadcasted_iota(jnp.int32, (h1, heads), 0)
@@ -487,28 +636,22 @@
         high = low(spread)
         pair_hi[i : i + 80, :] = high
         pair_lo[i : i + 80, :] = low(spread - high.astype(jnp.float32))
-    for copy in copies:
-        copy.wait_recv()
-    total = half_c[0].astype(jnp.float32)
-    for k in range(1, chips):
-        total = total + half_c[k].astype(jnp.float32)
-    pooled[part(core), :] = low(total)
-    copy_b = remote(
-        pooled.at[part(core), :], pooled.at[part(core), :], fsend.at[chips], frecv.at[chips], {"mp": other}
-    )
-    copy_b.start()
-    weights = (b1_slots, n_slots, b_slots)
-    moving = [
-        relay_own(mp, lambda k, ref=ref: ref.at[k], wsend.at[i], wrecv.at[i])
-        for i, ref in enumerate(weights)
-    ]
-
-    def arrive(i):
-        relay_rest(mp, lambda k: weights[i].at[k], wsend.at[i], wrecv.at[i], moving[i])
-
+    for h in range(2):
+        for copy in copies_y[h * (chips - 1) : (h + 1) * (chips - 1)]:
+            copy.wait_recv()
+        total = half_c[0, :, events(h)].astype(jnp.float32)
+        for k in range(1, chips):
+            total = total + half_c[k, :, events(h)].astype(jnp.float32)
+        pooled[part(core), events(h)] = low(total)
+        place = pooled.at[part(core), events(h)]
+        copy = remote(place, place, fsend.at[h, chips], frecv.at[h, chips], {"mp": other})
+        copy.start()
+        copies_b.append(copy)
+    n_steps = split_relay(dp, mp, n_slots, wsend.at[0], wrecv.at[0])
+    b_steps = split_relay(dp, mp, b_slots, wsend.at[1], wrecv.at[1])
+    n_steps[0]()
+    b_steps[0]()
     feat[:, :num] = numeric[...]
-    copy_b.wait_recv()
-    feat[:, num:] = low(jnp.transpose(pooled[...].astype(jnp.float32)))
     started = []
 
     def push(slot, *values):
@@ -568,17 +711,21 @@
         x = feat[at, :]
         wide_x = x.astype(jnp.float32)
         for k in range(2):
-            value = 2.0 * sigmoid(nt(x, gates[k]) + vec[k : k + 1, :wide])
+            value = 2.0 * sigmoid(nt(x, gates[k][...]) + vec[k : k + 1, :wide])
             gate[k, at, :] = value
             fields[k, at, :] = low(wide_x * value)
         y = nt(fields[0, at, :], n1[...])
         yn[0, at, :] = y
         return a + column_sum(y), b + column_sum(y * y)
 
-    sent_n = push(0, *loop(gates_and_first, zero1, zero1))
-    arrive(0)
-    for m in range(mp):
-        b1[m * s2 : (m + 1) * s2, :] = b1_slots[m]
+    a, b = zero1, zero1
+    for h in range(2):
+        copies_b[h].wait_recv()
+        at = events(h)
+        feat[at, num:] = low(jnp.transpose(pooled[:, at].astype(jnp.float32)))
+        a, b = gates_and_first(at, a, b)
+    sent_n = push(0, a, b)
+    n_steps[1]()
 
     def broad_first(at, a, b):
         y = nt(fields[1, at, :], b1[...])
@@ -586,7 +733,9 @@
         return a + column_sum(y), b + column_sum(y * y)
 
     sent_b = push(1, *loop(broad_first, zero2, zero2))
-    arrive(1)
+    b_steps[1]()
+    n_steps[2]()
+    n_steps[3]()
     for m in range(mp):
         for k in range(2):
             n23[k, m * s1 : (m + 1) * s1, :] = n_slots[m, k]
@@ -598,9 +747,12 @@
         return a + column_sum(y), b + column_sum(y * y)
 
     sent_n = push(2, *loop(narrow_second, zero1, zero1))
-    arrive(2)
+    b_steps[2]()
+    b_steps[3]()
     for m in range(mp):
-        b2[m * s2 : (m + 1) * s2, :] = b_slots[m]
+        for k in range(2):
+            row = (2 * m + k) * (s2 // 2)
+            b2[row : row + s2 // 2, :] = b_slots[m, k]
     mean_b1, rstd_b1 = norm(sent_b, h2)
 
     def broad_second(at, a, b):
@@ -691,7 +843,7 @@
     short = -(-tall_a // parts)
     a_work[...] = jnp.zeros_like(a_work)
     b_work[...] = jnp.zeros_like(b_work)
-    grad_n3 = weight_grad(gyn[1], un[1], mine, s1)
+    grad_n3 = weight_grad(gyn.at[1], un[1], own_cols, mine, s1, mp)
     t_b2 = pull(sent_b)[:, :h2]
 
     def back_b2(at, a, b):
@@ -712,8 +864,8 @@
         return a + column_sum(gz), b + column_sum(gz * yn[0, at, :])
 
     sent_n = push(9, *loop(back_n2, zero1, zero1))
-    grad_n2 = weight_grad(gyn[0], un[0], mine, s1)
-    grad_b2 = weight_grad(gyb[...], ub[0], mine, s2)
+    grad_n2 = weight_grad(gyn.at[0], un[0], own_cols, mine, s1, mp)
+    grad_b2 = weight_grad(gyb, ub[0], own_cols, mine, s2, mp)
     a_work[:s2, :] = grad_b2[:, :main]
     a_work[s2:tall_a, :] = jnp.concatenate([grad_n2, grad_n3], axis=1)[:, :main]
     spill[:s2, :] = grad_b2[:, main:]
@@ -744,8 +896,8 @@
         return ()
 
     loop(back_b1)
-    b_work[:s2, :wide] = weight_grad(gyb1[...], fields[1], mine, s2)
-    b_work[s2 : s2 + gcols, :wide] = weight_grad(grad_gate[1], feat[...], mine, gcols)
+    b_work[:s2, :wide] = weight_grad(gyb1, fields[1], own_cols, mine, s2, mp)
+    b_work[s2 : s2 + gcols, :wide] = weight_grad(grad_gate.at[1], feat[...], own_cols, mine, gcols, mp)
     copy_bx, start_b = give_half(me, 0, 0, size_b, b_work, b_land, hsend.at[2], hrecv.at[2])
     a_work[pl.ds(pl.multiple_of(start_a, 16), size_a // 2), :] = add_half(
         copy_ax, start_a, size_a // 2, a_work, a_land.at[pl.ds(0, size_a // 2), :]
@@ -760,7 +912,7 @@
         gyn1[at, :] = g
         term, g0 = gate_back(0, at, nn(g, n1[...]))
         g1 = grad_gate[1, at, :]
-        whole = nn(g0, gates[0]) + nn(g1, gates[1]) + term + own_term[at, :]
+        whole = nn(g0, gates[0][...]) + nn(g1, gates[1][...]) + term + own_term[at, :]
         whole = low(whole).astype(jnp.float32)
         own_term[at, :] = whole
         ne = ne + column_sum(whole[:, :num] * widen_dense(dense_t[:, at], 16))
@@ -787,7 +939,7 @@
         copy_az, start_a, size_a // 4, a_work, a_land.at[pl.ds(size_a // 2, size_a // 4), :]
     )
     b_out[...] = add_half(copy_bx, start_b, size_b // 2, b_work, b_land)
-    for copy in [copy_a, copy_b, copy_ax, copy_az, copy_bx] + copies:
+    for copy in [copy_ax, copy_az, copy_bx] + copies_a + copies_y + copies_b:
         copy.wait_send()
     for group in started:
         for copy in group:
@@ -798,7 +950,7 @@
     dp, mp,
     grads, feat, fields, grad_gate, gyn1, a_in, b_in, small,
     shares, a_full, b_full, c_full, small_out,
-    t_work, t_land, t_slots, s_slots, a_work, a_land, b_work, b_land, c_work, c_land, c_slots,
+    t_work, t_land, t_slots, s_slots, a_work, a_land, b_work, b_land, c_work, c_land, c_slots, own_cols,
     tsend, trecv, ysend, yrecv, ssend, srecv, asend, arecv, bsend, brecv, csend, crecv,
 ):
     tall = grads.shape[0] // dp
@@ -864,8 +1016,8 @@
     gcols, s1 = feat.shape[1] // mp, gyn1.shape[1] // mp
     wide = feat.shape[1]
     c_work[...] = jnp.zeros_like(c_work)
-    c_work[:gcols, :wide] = weight_grad(grad_gate[0], feat[...], mine, gcols)
-    c_work[gcols : gcols + s1, :wide] = weight_grad(gyn1[...], fields[0], mine, s1)
+    c_work[:gcols, :wide] = weight_grad(grad_gate.at[0], feat[...], own_cols, mine, gcols, mp)
+    c_work[gcols : gcols + s1, :wide] = weight_grad(gyn1, fields[0], own_cols, mine, s1, mp)
     half_c = size_c // 2
     copy_c = send_to(
         remote(c_work.at[rows_at((1 - side) * half_c, half_c), :], c_land, csend.at[0], crecv.at[0], {"dp": flip(me, 0)})
@@ -1084,36 +1236,38 @@
     bits = (cats * rows - 1).bit_length()
     dense_t = dense_values.T
     tall = own_rows // mp // HI * 16
-    vregs = 1 << (-(-(cats * slots * rows) // 1024) - 1).bit_length()
+    vregs = -(-(cats * slots * rows) // (2 * CHUNK)) * (2 * CHUNK) // 1024
     first_args = (
         embed_table, jnp.transpose(gate_weight, (1, 0, 2)), narrow_first, gate_bias,
-        narrow_gain, narrow_shift, broad_gain, broad_shift,
+        narrow_gain, narrow_shift, broad_gain, broad_shift, broad_first,
         field_ids, lengths, dense_t, num_embed, jnp.transpose(narrow_rest, (1, 0, 2)),
     )
-    t2, keys, numeric, gates, n1, vec, n_own = pl.pallas_call(
+    t2, keys, numeric, weights, vec, n_own = pl.pallas_call(
         functools.partial(first_kernel, dp, mp, own_rows, bits),
         out_shape=(
             b16(dp * tall, HI),
-            jax.ShapeDtypeStruct((128, vregs * 8), jnp.int32),
+            jax.ShapeDtypeStruct((2, vregs * 8, 128), jnp.int32),
             b16(rows, num),
-            b16(2, wide, wide),
-            b16(h1, wide),
+            b16(2 * wide + h1 + h2, wide),
             f32(16, 896),
             b16(2, s1, h1),
         ),
-        in_specs=[ANY] * 13,
-        out_specs=(VM,) * 7,
+        in_specs=[ANY] * 14,
+        out_specs=(VM,) * 6,
         scratch_shapes=[pltpu.VMEM(x.shape, x.dtype) for x in first_args]
         + [
             pltpu.VMEM((vregs * 8, 128), jnp.int32),
             held16(mp, 2, gcols, wide),
-            held16(mp, s1, wide),
+            held16(mp, 2, s1 // 2, wide),
+            held16(mp, 2, s2 // 2, wide),
             held(mp, 16, 256),
             dma(dp - 1),
             dma(dp - 1),
-            dma(3, mp),
-            dma(3, mp),
-            dma(13),
+            dma(2, mp),
+            dma(2, mp),
+            dma(2, 4 * chips),
+            dma(2, 4 * chips),
+            dma(14),
         ],
         compiler_params=params(0, 54),
         name="first",
@@ -1123,8 +1277,8 @@
         out_shape=f32(cats * 16, rows),
         in_specs=[VM] * 2,
         out_specs=VM,
-        scratch_shapes=[held(cats * 16, rows)],
-        compiler_params=params(None, 12),
+        scratch_shapes=[held((cats + WINDOW) * 16, rows)],
+        compiler_params=params(None, 16),
         name="lookup",
     )(keys, t2)
 
@@ -1139,7 +1293,7 @@
     c_rows = up(gcols + s1, 16 * dp)
     levels = dp.bit_length() - 1
     dense_args = (
-        broad_first, broad_rest, joining_left.reshape(1, h1), joining_right,
+        broad_rest, joining_left.reshape(1, h1), joining_right,
         jnp.transpose(joining_pair, (1, 2, 0)), joining_bias.reshape(1, 1), labels.reshape(1, rows), dense_t,
     )
     (
@@ -1165,7 +1319,7 @@
             f32(1, h2),
             f32(1, 1),
         ),
-        in_specs=[VM] * 6 + [ANY] * 8,
+        in_specs=[VM] * 5 + [ANY] * 7,
         out_specs=(VM,) * 16,
         scratch_shapes=[
             held(cats * 8, rows),
@@ -1173,10 +1327,8 @@
             held16(cats * 16, rows),
             held(2, rows, wide),
             held(rows, wide),
-            held16(mp, s2, wide),
             held16(mp, 2, s1, h1),
-            held16(mp, s2, h2),
-            held16(h2, wide),
+            held16(mp, 2, s2 // 2, h2),
             held16(2, h1, h1),
             held16(h2, h2),
             held(3, rows, h1),
@@ -1193,10 +1345,10 @@
             held(rows, h1),
             held(11, dp, 2, 896),
             held16(s1 + s2, h2 - main),
-            dma(chips + 1),
-            dma(chips + 1),
-            dma(3, mp),
-            dma(3, mp),
+            dma(2, chips + 1),
+            dma(2, chips + 1),
+            dma(2, 4 * chips),
+            dma(2, 4 * chips),
             dma(11, dp - 1),
             dma(11, dp - 1),
             held16(rows, h2),
@@ -1206,19 +1358,20 @@
             held16(b_rows // 2, main),
             dma(3),
             dma(3),
+            held16(rows, up(max(gcols, s1, s2), 128)),
         ]
         + [pltpu.VMEM(x.shape, x.dtype) for x in dense_args]
-        + [dma(8)],
+        + [dma(7)],
         compiler_params=params(1, 39 + dp // 16),
         name="dense",
-    )(partial, numeric, gates, n1, n_own, vec, *dense_args)
+    )(partial, numeric, weights, n_own, vec, *dense_args)
     row_sums = pl.pallas_call(
         functools.partial(scatter_kernel, cats, rows, bits),
         out_shape=b16(dp * tall, HI),
         in_specs=[VM] * 2,
         out_specs=VM,
-        scratch_shapes=[held(dp * tall, HI)],
-        compiler_params=params(None, 12),
+        scratch_shapes=[held(dp * tall, HI), held16((cats + WINDOW) * 16, rows)],
+        compiler_params=params(None, 16),
         name="scatter",
     )(keys, grads_t)
     shares, a_full, b_full, c_full, small = pl.pallas_call(
@@ -1244,6 +1397,7 @@
             held16(c_rows, main),
             held16(c_rows // 2, main),
             held16(dp // 2 - 1, c_rows // dp, main),
+            held16(rows, up(max(gcols, s1, s2), 128)),
             dma(dp // 2),
             dma(dp // 2),
             dma(mp),

time: 165 us -> 148 us (0.90)
  Pallas kernels: 156 us -> 141 us
  local copies, waits for them, and re-layouts: 5.87 us -> 3.98 us
    pallas_call x1, Pallas kernels: 67.7 us -> 58.9 us  [shards(): pl.pallas_call(functools.partial(dense_kernel, dp, mp, hx, float(rows * d...]
    pallas_call x1, Pallas kernels: 10.3 us -> 4.22 us  [shards(): pl.pallas_call(functools.partial(lookup_kernel, cats, rows, bits), out_sh...]
    pallas_call x1, Pallas kernels: 10.3 us -> 5.47 us  [shards(): pl.pallas_call(functools.partial(scatter_kernel, cats, rows, bits), out_s...]
    pallas_call x1, Pallas kernels: 24.3 us -> 28.2 us  [shards(): pl.pallas_call(functools.partial(first_kernel, dp, mp, own_rows, bits), o...]
    unnamed x30 -> x26, local copies, waits for them, and re-layouts: 5.87 us -> 3.98 us
where the time goes in v5:
time: 148 us; the launch traced here: 147 us
  Pallas kernels  141 us (95%)
  local copies, waits for them, and re-layouts  3.98 us (3%)
  between operations  1.52 us (1%)
    pallas_call x1, Pallas kernels, shards(): pl.pallas_call(functools.partial(dense_kernel, dp, mp, hx, float(rows * d...  58.9 us
    pallas_call x1, Pallas kernels, shards(): pl.pallas_call(functools.partial(reduce_kernel, dp, mp), out_shape=(b16(m...  41.4 us
    pallas_call x1, Pallas kernels, shards(): pl.pallas_call(functools.partial(first_kernel, dp, mp, own_rows, bits), o...  28.2 us
    pallas_call x1, Pallas kernels, shards(): pl.pallas_call(functools.partial(scatter_kernel, cats, rows, bits), out_s...  5.47 us
    pallas_call x1, Pallas kernels, shards(): pl.pallas_call(functools.partial(lookup_kernel, cats, rows, bits), out_sh...  4.22 us
    unnamed x26, local copies, waits for them, and re-layouts  3.98 us

profile of v5, /device:TPU:0, one launch (start us, length us, event | category | flops | bytes accessed | tf_op | source)
XLA Modules:
  0.0 146.7 jit_solution(17536014628032504475)
XLA Ops:
  1.3 0.0 copy-start.4
  1.3 0.0 copy-start.7
  1.3 0.0 copy-start.8
  1.3 28.2 %first.1 = (bf16[1024,256]{1,0:T(8,128)(2,1)}, s32[2,416,128]{2,1,0:T(8,128)}, bf16[512,208]{1,0:T(8,128)(2,1)}, bf16[2448,624]{1,0:T(8,128)(2,1)}, f32[16,896]{1,0:T(8,128)}, /*index=5*/bf16[2,100,400]{2,1,0:T(8,128)(2,1)}) custom-call(f32[16,8192]{1,0:T(8,128)} %refs_0_.1, bf16[156,2,624]{2,1,0:T(2,128)(2,1)} %bitcast.19, bf16[100,624]{1,0:T(8,128)(2,1)} %refs_2_.1, ...), custom_call_target="tpu_custom_call" | custom-call | tf_op jit(solution)/shard_map/first/pallas_call | solution.py:1245
  29.6 0.0 copy-start.10
  29.6 0.0 copy-start.11
  29.6 0.0 copy-start.12
  29.6 0.0 copy-start.1
  29.6 1.0 copy-done.1
  30.6 1.0 copy-done.3
  31.7 4.2 %lookup.1.partial = f32[416,512]{1,0:T(8,128)S(1)} custom-call(s32[2,416,128]{2,1,0:T(8,128)S(1)} %copy-done.1, bf16[1024,256]{1,0:T(8,128)(2,1)S(1)} %copy-done.3), custom_call_target="tpu_custom_call" | custom-call | tf_op jit(solution)/shard_map/lookup/pallas_call | solution.py:1275
  35.9 0.0 copy-done.4
  35.9 0.0 copy-done.7
  35.9 0.0 copy-done.8
  35.9 0.0 copy-done.10
  36.0 0.0 copy-done.11
  36.0 0.0 copy-done.12
  36.0 0.0 copy-done.5
  36.0 0.0 copy-done.6
  36.0 1.9 %copy-done = bf16[2448,624]{1,0:T(8,128)(2,1)S(1)} copy-done((bf16[2448,624]{1,0:T(8,128)(2,1)S(1)}, bf16[2448,624]{1,0:T(8,128)(2,1)}, u32[]{:S(2)}) %copy-start) | copy-done | bytes 3055128
  37.9 58.9 %dense.1 = (f32[1,512]{1,0:T(1,128)S(1)}, bf16[416,512]{1,0:T(8,128)(2,1)S(1)}, bf16[512,624]{1,0:T(8,128)(2,1)S(1)}, bf16[2,512,624]{2,1,0:T(8,128)(2,1)S(1)}, ...) custom-call(f32[416,512]{1,0:T(8,128)S(1)} %lookup.1.partial, ...), custom_call_target="tpu_custom_call" | custom-call | tf_op jit(solution)/shard_map/dense/pallas_call | solution.py:1302
  96.9 5.5 %scatter.1.grads = bf16[1024,256]{1,0:T(8,128)(2,1)S(1)} custom-call(s32[2,416,128]{2,1,0:T(8,128)S(1)} %copy-done.2, bf16[416,512]{1,0:T(8,128)(2,1)S(1)} %get-tuple-element.67.grad), custom_call_target="tpu_custom_call" | custom-call | tf_op jit(solution)/shard_map/scatter/pallas_call | solution.py:1368
  102.3 41.4 %reduce.1 = (bf16[4,128,256]{2,1,0:T(8,128)(2,1)S(1)}, bf16[384,640]{1,0:T(8,128)(2,1)S(1)}, bf16[384,640]{1,0:T(8,128)(2,1)S(1)}, bf16[256,640]{1,0:T(8,128)(2,1)S(1)}, f32[8,256]{1,0:T(8,128)S(1)}) custom-call(bf16[1024,256]{1,0:T(8,128)(2,1)S(1)} %scatter.1.grads, bf16[512,624]{1,0:T(8,128)(2,1)S(1)} %get-tuple-element.68.feat, ...), custom_call_target="tpu_custom_call" | custom-call | tf_op jit(solution)/shard_map/reduce/pallas_call | solution.py:1377
  143.8 2.9 %final.1 = (f32[1,512]{1,0:T(1,128)}, f32[13,16]{1,0:T(8,128)}, f32[16,8192]{1,0:T(8,128)}, f32[156,2,624]{2,1,0:T(2,128)}, f32[2,156]{1,0:T(2,128)}, /*index=5*...) custom-call(bf16[4,128,256]{2,1,0:T(8,128)(2,1)S(1)} %get-tuple-elem, ...), custom_call_target="tpu_custom_call" | custom-call | tf_op jit(solution)/shard_map/final/pallas_call | solution.py:1417
  (8 shorter events, 0.0 us)
Async XLA Ops:
  1.3 34.6 %copy-start.4 = (bf16[200,800]{1,0:T(8,128)(2,1)S(1)}, bf16[200,800]{1,0:T(8,128)(2,1)}, u32[]{:S(2)}) copy-start(bf16[200,800]{1,0:T(8,128)(2,1)} %b_rest_hbm.1) | copy-start | bytes 960004
  1.3 34.6 %copy-start.7 = (f32[512,13]{0,1:T(8,128)S(1)}, f32[512,13]{0,1:T(8,128)}, u32[]{:S(2)}) copy-start(f32[512,13]{0,1:T(8,128)} %param.20) | copy-start | bytes 79876
  1.3 34.6 %copy-start.8 = (f32[50,8,16]{0,2,1:T(8,128)S(1)}, f32[50,8,16]{0,2,1:T(8,128)}, u32[]{:S(2)}) copy-start(f32[50,8,16]{0,2,1:T(8,128)} %param.38) | copy-start | bytes 76804
  29.6 6.4 %copy-start.10 = (f32[800]{0:T(1024)S(1)}, f32[800]{0:T(1024)}, u32[]{:S(2)}) copy-start(f32[800]{0:T(1024)} %right_hbm.1) | copy-start | bytes 9604
  29.6 6.4 %copy-start.11 = (f32[400]{0:T(512)S(1)}, f32[400]{0:T(512)}, u32[]{:S(2)}) copy-start(f32[400]{0:T(512)} %param.36) | copy-start | bytes 4804
  29.6 6.4 %copy-start.12 = (s32[512]{0:T(512)S(1)}, s32[512]{0:T(512)}, u32[]{:S(2)}) copy-start(s32[512]{0:T(512)} %param.23) | copy-start | bytes 6148
  29.6 1.0 copy-start.1
  30.6 1.0 copy-start.3
  31.7 4.3 %copy-start.5 = (bf16[512,208]{1,0:T(8,128)(2,1)S(1)}, bf16[512,208]{1,0:T(8,128)(2,1)}, u32[]{:S(2)}) copy-start(bf16[512,208]{1,0:T(8,128)(2,1)} %get-tuple-element.63.numeric) | copy-start | bytes 638980
  31.7 4.3 %copy-start.6 = (bf16[2,100,400]{2,1,0:T(8,128)(2,1)S(1)}, bf16[2,100,400]{2,1,0:T(8,128)(2,1)}, u32[]{:S(2)}) copy-start(bf16[2,100,400]{2,1,0:T(8,128)(2,1)} %get-tuple-element.65.n_rest) | copy-start | bytes 480004
  31.7 4.3 %copy-start.9 = (f32[16,896]{1,0:T(8,128)S(1)}, f32[16,896]{1,0:T(8,128)}, u32[]{:S(2)}) copy-start(f32[16,896]{1,0:T(8,128)} %get-tuple-element.66.vec) | copy-start | bytes 172036
  36.0 1.9 %copy-start = (bf16[2448,624]{1,0:T(8,128)(2,1)S(1)}, bf16[2448,624]{1,0:T(8,128)(2,1)}, u32[]{:S(2)}) copy-start(bf16[2448,624]{1,0:T(8,128)(2,1)} %get-tuple-element.64.weights) | copy-start | bytes 9165316
  37.9 59.0 %copy-start.2 = (s32[2,416,128]{2,1,0:T(8,128)S(1)}, s32[2,416,128]{2,1,0:T(8,128)}, u32[]{:S(2)}) copy-start(s32[2,416,128]{2,1,0:T(8,128)} %get-tuple-element.61.keys) | copy-start | bytes 1277956

commit v6 on v5

--- a/solution.py
+++ b/solution.py
@@ -346,7 +346,7 @@
     )
 
 
-def split_relay(dp, mp, ref, send, recv):
+def split_relay(dp, mp, ref, send, recv, fetched=False):
     me, mine = lax.axis_index("dp"), lax.axis_index("mp")
     other = mine + 1 - 2 * lax.rem(mine, 2)
     chips = mp // 2
@@ -366,14 +366,25 @@
         return lax.rem(mine + mp - 2 * k, mp)
 
     def begin():
+        if not fetched:
+            fetch()
+        go(ref.at[mine], 0, {"mp": other})
+
+    def fetch():
         for k in range(1, chips):
             go(ref.at[mine, near], k, {"mp": lax.rem(mine + 2 * k, mp)})
-        go(ref.at[mine], 0, {"mp": other})
+
+    def arrive():
+        for k in range(1, chips):
+            move(ref.at[source(k), near], k, beside).wait_recv()
+        for copy in started:
+            copy.wait_send()
 
     def middle():
         for k in range(1, chips):
             place = ref.at[source(k), near]
-            move(place, k, beside).wait_recv()
+            if not fetched:
+                move(place, k, beside).wait_recv()
             go(place, 2 * chips + k, beside)
             go(place, chips + k, {"mp": other})
 
@@ -392,7 +403,7 @@
         for copy in started:
             copy.wait_send()
 
-    return begin, middle, later, end
+    return begin, middle, later, end, fetch, arrive
 
 
 def bring(sources, places, sem):
@@ -405,18 +416,18 @@
 
 
 def first_kernel(dp, mp, own_rows, bits, *refs):
-    count = 14
+    count = 15
     sources, refs = refs[:count], refs[count:]
-    t2, keys, numeric, weights, vec, n_own = refs[:6]
-    places, refs = refs[6 : 6 + count], refs[6 + count :]
+    t2, keys, numeric, weights, vec, n_next, b_next = refs[:7]
+    places, refs = refs[7 : 7 + count], refs[7 + count :]
     (
-        scratch, gate_slots, n_slots, b_slots, v_slots,
-        send, recv, send2, recv2, send3, recv3, sem,
+        scratch, gate_slots, g_slots, n_slots, b_slots, v_slots,
+        send, recv, send2, recv2, send3, recv3, send4, recv4, sem,
     ) = refs
     brought = bring(sources, places, sem)
     (
         table, gate_w, n_first, gate_b, n_gain, n_shift, b_gain, b_shift, b_first,
-        ids, lens, dense_t, num_embed, n_rest,
+        ids, lens, dense_t, num_embed, n_rest, b_rest,
     ) = places
     part = own_rows // mp
     blocks = part // HI
@@ -428,8 +439,11 @@
     own = table[:, pl.ds(pl.multiple_of(mine * part, HI), part)].astype(jnp.bfloat16)
     for b in range(blocks):
         t2[pl.ds(pl.multiple_of(seat(me, dp) * tall + b * 16, 16), 16), :] = own[:, b * HI : (b + 1) * HI]
+    gate_slots[mine] = gate_w[:, 0, :]
+    second = gate_w[:, 1, :]
+    cols = g_slots.shape[2]
     for k in range(2):
-        gate_slots[mine, k] = gate_w[:, k, :]
+        g_slots[mine, k] = second[k * cols : (k + 1) * cols, :]
     small, large = n_slots.shape[2], b_slots.shape[2]
     for k in range(2):
         n_slots[mine, k] = n_first[k * small : (k + 1) * small, :]
@@ -444,7 +458,7 @@
         return t2.at[pl.ds(pl.multiple_of(seat(i, dp) * tall, 16), tall), :]
 
     pairs = [
-        split_relay(dp, mp, ref, send3.at[i], recv3.at[i]) for i, ref in enumerate((n_slots, b_slots))
+        split_relay(dp, mp, ref, send3.at[i], recv3.at[i]) for i, ref in enumerate((g_slots, n_slots, b_slots))
     ]
     for steps in pairs:
         steps[0]()
@@ -455,8 +469,10 @@
     copies = spread_dp(dp, slot, send, recv)
     for copy in brought[9:]:
         copy.wait()
+    half_b = b_next.shape[2]
     for k in range(2):
-        n_own[k] = n_rest[:, k, :]
+        n_next[mine, k] = n_rest[:, k, :]
+        b_next[mine, k] = b_rest[k * half_b : (k + 1) * half_b, :]
     fields, width = num_embed.shape
     tiled = jnp.concatenate([num_embed[...]] * fields, axis=1)
     row = lax.broadcasted_iota(jnp.int32, tiled.shape, 0)
@@ -476,17 +492,20 @@
     lax.fori_loop(0, 2, pack, 0)
     for steps in pairs:
         steps[1]()
+    nexts = [
+        split_relay(dp, mp, ref, send4.at[i], recv4.at[i]) for i, ref in enumerate((n_next, b_next))
+    ]
+    for steps in nexts:
+        steps[4]()
     for ref, i, started in groups:
         relay_rest(mp, lambda k, ref=ref: ref.at[k], send2.at[i], recv2.at[i], started)
-    cols, wide = gate_slots.shape[2], gate_slots.shape[3]
+    cols, wide = gate_slots.shape[1:]
     for m in range(mp):
-        for k in range(2):
-            row = k * wide + m * cols
-            weights[row : row + cols, :] = gate_slots[m, k]
+        weights[m * cols : (m + 1) * cols, :] = gate_slots[m]
     for steps in pairs:
         steps[2]()
-    row = 2 * wide
-    for ref, steps in zip((n_slots, b_slots), pairs):
+    row = wide
+    for ref, steps in zip((g_slots, n_slots, b_slots), pairs):
         steps[3]()
         tall = ref.shape[2]
         for m in range(mp):
@@ -500,6 +519,8 @@
             [v_slots[m, row : row + r, :w] for m in range(mp)], axis=1
         )
         row += r
+    for steps in nexts:
+        steps[5]()
     for copy in copies:
         copy.wait()
 
@@ -551,19 +572,19 @@
 
 def dense_kernel(
     dp, mp, hx, batch,
-    partial, numeric, weights, n_rest, vec,
-    b_rest_hbm, left_hbm, right_hbm, pair_hbm, bias_hbm, labels_hbm, dense_hbm,
+    partial, numeric, weights, n_next, b_next, vec,
+    left_hbm, right_hbm, pair_hbm, bias_hbm, labels_hbm, dense_hbm,
     logits, grads_t, feat, fields, grad_gate, gyn1, a_out, b_out, small,
     n_gain_g, n_shift_g, b_gain_g, b_shift_g, left_g, right_g, bias_g,
     half_a, half_c, pooled, gate, own_term, n_slots, b_slots, n23, b2,
     yn, dn, yb, db, un, ub, gyn, gyb, pair_hi, pair_lo, pair_g, to_first, sums, spill,
     fsend, frecv, wsend, wrecv, ssend, srecv,
     gyb1, a_work, b_work, a_land, b_land, hsend, hrecv, own_cols,
-    b_rest, left, right, pair_t, bias, labels, dense_t, sem,
+    left, right, pair_t, bias, labels, dense_t, sem,
 ):
     brought = bring(
-        (b_rest_hbm, left_hbm, right_hbm, pair_hbm, bias_hbm, labels_hbm, dense_hbm),
-        (b_rest, left, right, pair_t, bias, labels, dense_t),
+        (left_hbm, right_hbm, pair_hbm, bias_hbm, labels_hbm, dense_hbm),
+        (left, right, pair_t, bias, labels, dense_t),
         sem,
     )
     me, mine = lax.axis_index("dp"), lax.axis_index("mp")
@@ -584,7 +605,12 @@
     gcols = wide // mp
     half = partial.shape[0] // 2
     hail(dp, mp)
-    n_slots[mine] = n_rest[...]
+    near = lax.rem(me, 2)
+    for slots, given in ((n_slots, n_next), (b_slots, b_next)):
+        slots[mine] = given[mine]
+        for k in range(1, chips):
+            source = lax.rem(mine + 2 * k, mp)
+            slots[source, near] = given[source, near]
     all_in(dp, mp)
 
     def rowset(i):
@@ -606,8 +632,6 @@
         copies_a.append(copy)
     for copy in brought:
         copy.wait()
-    for k in range(2):
-        b_slots[mine, k] = b_rest[k * (s2 // 2) : (k + 1) * (s2 // 2), :]
     for h in range(2):
         copies_a[h].wait_recv()
         half_c[chip, :, events(h)] = low(partial[part(core), events(h)] + half_a[:, events(h)])
@@ -618,6 +642,11 @@
             )
             copy.start()
             copies_y.append(copy)
+    n_steps = split_relay(dp, mp, n_slots, wsend.at[0], wrecv.at[0], True)
+    b_steps = split_relay(dp, mp, b_slots, wsend.at[1], wrecv.at[1], True)
+    for relay in (n_steps, b_steps):
+        relay[0]()
+        relay[1]()
     heads = pair_t.shape[2]
     by_head = jnp.transpose(pair_t[...].reshape(hx * 16, heads))
     row = lax.broadcasted_iota(jnp.int32, (h1, heads), 0)
@@ -647,10 +676,6 @@
         copy = remote(place, place, fsend.at[h, chips], frecv.at[h, chips], {"mp": other})
         copy.start()
         copies_b.append(copy)
-    n_steps = split_relay(dp, mp, n_slots, wsend.at[0], wrecv.at[0])
-    b_steps = split_relay(dp, mp, b_slots, wsend.at[1], wrecv.at[1])
-    n_steps[0]()
-    b_steps[0]()
     feat[:, :num] = numeric[...]
     started = []
 
@@ -725,7 +750,6 @@
         feat[at, num:] = low(jnp.transpose(pooled[:, at].astype(jnp.float32)))
         a, b = gates_and_first(at, a, b)
     sent_n = push(0, a, b)
-    n_steps[1]()
 
     def broad_first(at, a, b):
         y = nt(fields[1, at, :], b1[...])
@@ -733,8 +757,8 @@
         return a + column_sum(y), b + column_sum(y * y)
 
     sent_b = push(1, *loop(broad_first, zero2, zero2))
-    b_steps[1]()
     n_steps[2]()
+    b_steps[2]()
     n_steps[3]()
     for m in range(mp):
         for k in range(2):
@@ -747,7 +771,6 @@
         return a + column_sum(y), b + column_sum(y * y)
 
     sent_n = push(2, *loop(narrow_second, zero1, zero1))
-    b_steps[2]()
     b_steps[3]()
     for m in range(mp):
         for k in range(2):
@@ -1023,6 +1046,12 @@
         remote(c_work.at[rows_at((1 - side) * half_c, half_c), :], c_land, csend.at[0], crecv.at[0], {"dp": flip(me, 0)})
     )
     small_copies = spread_dp(dp, lambda k: s_slots.at[k], ssend, srecv)
+
+    def onward(back, level, full, sems):
+        copy, start, size = back
+        copy.wait_recv()
+        return double(level, full, start, size, sems)
+
     off_b, held_b = fold(step_b, b_work, b_land.at[0])
     step_b = halves("b", 2, b_work, b_land.at[1], held_b, sems_b, off_b)
     off_a, held_a = fold(step_a, a_work, a_land.at[0])
@@ -1032,6 +1061,15 @@
     start_a = start_a + off_a
     a_full[rows_at(start_a, held_a), :] = a_work[rows_at(off_a, held_a), :]
     back_a = double(levels - 1, a_full, start_a, held_a, sems_a)
+    off_b, held_b = fold(step_b, b_work, b_land.at[1])
+    for level in range(3, levels):
+        step_b = halves("b", level, b_work, b_land.at[level - 1], held_b, sems_b, off_b)
+        off_b, held_b = fold(step_b, b_work, b_land.at[level - 1])
+    start_b = start_b + off_b
+    b_full[rows_at(start_b, held_b), :] = b_work[rows_at(off_b, held_b), :]
+    back_b = double(levels - 1, b_full, start_b, held_b, sems_b)
+    for level in range(levels - 2, 0, -1):
+        back_a = onward(back_a, level, a_full, sems_a)
     copy_t.wait_recv()
     at = rows_at(side * half_t, half_t)
     t_work[...] = low(grads[at, :].astype(jnp.float32) + t_land[...].astype(jnp.float32))
@@ -1058,27 +1096,9 @@
                 )
             )
         )
-    off_b, held_b = fold(step_b, b_work, b_land.at[1])
-    for level in range(3, levels):
-        step_b = halves("b", level, b_work, b_land.at[level - 1], held_b, sems_b, off_b)
-        off_b, held_b = fold(step_b, b_work, b_land.at[level - 1])
-    start_b = start_b + off_b
-    b_full[rows_at(start_b, held_b), :] = b_work[rows_at(off_b, held_b), :]
-    back_b = double(levels - 1, b_full, start_b, held_b, sems_b)
-
-    def onward(back, level, full, sems):
-        copy, start, size = back
-        copy.wait_recv()
-        return double(level, full, start, size, sems)
-
     for level in range(levels - 2, 0, -1):
-        back_a = onward(back_a, level, a_full, sems_a)
-    total = t_work[rows_at(place * tall, tall), :].astype(jnp.float32)
-    for k in range(1, far):
-        t_copies[k - 1].wait_recv()
-        total = total + t_slots[k - 1].astype(jnp.float32)
-    shares[mine] = low(total)
-    started = relay_own(mp, lambda k: shares.at[k], ysend, yrecv)
+        back_b = onward(back_b, level, b_full, sems_b)
+    back_a = onward(back_a, 0, a_full, sems_a)
     own = rows_at(side * half_c + place * piece, piece)
     total = c_work[own, :].astype(jnp.float32)
     for k in range(1, far):
@@ -1092,15 +1112,18 @@
                 remote(c_full.at[own, :], c_full.at[own, :], csend.at[far + k], crecv.at[far + k], across(k))
             )
         )
-    back_a = onward(back_a, 0, a_full, sems_a)
-    for level in range(levels - 2, 0, -1):
-        back_b = onward(back_b, level, b_full, sems_b)
-    relay_rest(mp, lambda k: shares.at[k], ysend, yrecv, started)
+    total = t_work[rows_at(place * tall, tall), :].astype(jnp.float32)
+    for k in range(1, far):
+        t_copies[k - 1].wait_recv()
+        total = total + t_slots[k - 1].astype(jnp.float32)
+    shares[mine] = low(total)
+    started = relay_own(mp, lambda k: shares.at[k], ysend, yrecv)
+    back_b = onward(back_b, 0, b_full, sems_b)
     for copy in c_back:
         copy.wait_recv()
     at = c_full.at[rows_at(side * half_c, half_c), :]
     last_c = send_to(remote(at, at, csend.at[far], crecv.at[far], {"dp": flip(me, 0)}))
-    back_b = onward(back_b, 0, b_full, sems_b)
+    relay_rest(mp, lambda k: shares.at[k], ysend, yrecv, started)
     for copy in small_copies:
         copy.wait_recv()
     value = s_slots[0]
@@ -1240,9 +1263,9 @@
     first_args = (
         embed_table, jnp.transpose(gate_weight, (1, 0, 2)), narrow_first, gate_bias,
         narrow_gain, narrow_shift, broad_gain, broad_shift, broad_first,
-        field_ids, lengths, dense_t, num_embed, jnp.transpose(narrow_rest, (1, 0, 2)),
+        field_ids, lengths, dense_t, num_embed, jnp.transpose(narrow_rest, (1, 0, 2)), broad_rest,
     )
-    t2, keys, numeric, weights, vec, n_own = pl.pallas_call(
+    t2, keys, numeric, weights, vec, n_next, b_next = pl.pallas_call(
         functools.partial(first_kernel, dp, mp, own_rows, bits),
         out_shape=(
             b16(dp * tall, HI),
@@ -1250,14 +1273,16 @@
             b16(rows, num),
             b16(2 * wide + h1 + h2, wide),
             f32(16, 896),
-            b16(2, s1, h1),
+            b16(mp, 2, s1, h1),
+            b16(mp, 2, s2 // 2, h2),
         ),
-        in_specs=[ANY] * 14,
-        out_specs=(VM,) * 6,
+        in_specs=[ANY] * 15,
+        out_specs=(VM,) * 7,
         scratch_shapes=[pltpu.VMEM(x.shape, x.dtype) for x in first_args]
         + [
             pltpu.VMEM((vregs * 8, 128), jnp.int32),
-            held16(mp, 2, gcols, wide),
+            held16(mp, gcols, wide),
+            held16(mp, 2, gcols // 2, wide),
             held16(mp, 2, s1 // 2, wide),
             held16(mp, 2, s2 // 2, wide),
             held(mp, 16, 256),
@@ -1265,9 +1290,11 @@
             dma(dp - 1),
             dma(2, mp),
             dma(2, mp),
+            dma(3, 4 * chips),
+            dma(3, 4 * chips),
             dma(2, 4 * chips),
             dma(2, 4 * chips),
-            dma(14),
+            dma(15),
         ],
         compiler_params=params(0, 54),
         name="first",
@@ -1279,6 +1306,7 @@
         out_specs=VM,
         scratch_shapes=[held((cats + WINDOW) * 16, rows)],
         compiler_params=params(None, 16),
+        cost_estimate=pl.CostEstimate(flops=8 * 10**9, bytes_accessed=2 * 10**6, transcendentals=0),
         name="lookup",
     )(keys, t2)
 
@@ -1293,7 +1321,7 @@
     c_rows = up(gcols + s1, 16 * dp)
     levels = dp.bit_length() - 1
     dense_args = (
-        broad_rest, joining_left.reshape(1, h1), joining_right,
+        joining_left.reshape(1, h1), joining_right,
         jnp.transpose(joining_pair, (1, 2, 0)), joining_bias.reshape(1, 1), labels.reshape(1, rows), dense_t,
     )
     (
@@ -1319,7 +1347,7 @@
             f32(1, h2),
             f32(1, 1),
         ),
-        in_specs=[VM] * 5 + [ANY] * 7,
+        in_specs=[VM] * 6 + [ANY] * 6,
         out_specs=(VM,) * 16,
         scratch_shapes=[
             held(cats * 8, rows),
@@ -1361,10 +1389,10 @@
             held16(rows, up(max(gcols, s1, s2), 128)),
         ]
         + [pltpu.VMEM(x.shape, x.dtype) for x in dense_args]
-        + [dma(7)],
+        + [dma(6)],
         compiler_params=params(1, 39 + dp // 16),
         name="dense",
-    )(partial, numeric, weights, n_own, vec, *dense_args)
+    )(partial, numeric, weights, n_next, b_next, vec, *dense_args)
     row_sums = pl.pallas_call(
         functools.partial(scatter_kernel, cats, rows, bits),
         out_shape=b16(dp * tall, HI),
@@ -1372,6 +1400,7 @@
         out_specs=VM,
         scratch_shapes=[held(dp * tall, HI), held16((cats + WINDOW) * 16, rows)],
         compiler_params=params(None, 16),
+        cost_estimate=pl.CostEstimate(flops=8 * 10**9, bytes_accessed=2 * 10**6, transcendentals=0),
         name="scatter",
     )(keys, grads_t)
     shares, a_full, b_full, c_full, small = pl.pallas_call(

time: 148 us -> 140 us (0.946)
  Pallas kernels: 141 us -> 136 us
  local copies, waits for them, and re-layouts: 3.98 us -> 2.1 us
    pallas_call x1, Pallas kernels: 58.9 us -> 52.3 us  [shards(): pl.pallas_call(functools.partial(dense_kernel, dp, mp, hx, float(rows * d...]
    unnamed x26, local copies, waits for them, and re-layouts: 3.98 us -> 2.1 us
where the time goes in v6:
time: 140 us; the launch traced here: 139 us
  Pallas kernels  136 us (97%)
  local copies, waits for them, and re-layouts  2.1 us (2%)
  between operations  1.55 us (1%)
    pallas_call x1, Pallas kernels, shards(): pl.pallas_call(functools.partial(dense_kernel, dp, mp, hx, float(rows * d...  52.3 us
    pallas_call x1, Pallas kernels, shards(): pl.pallas_call(functools.partial(reduce_kernel, dp, mp), out_shape=(b16(m...  41.2 us
    pallas_call x1, Pallas kernels, shards(): pl.pallas_call(functools.partial(first_kernel, dp, mp, own_rows, bits), o...  29.5 us
    pallas_call x1, Pallas kernels, shards(): pl.pallas_call(functools.partial(scatter_kernel, cats, rows, bits), out_s...  5.49 us
    pallas_call x1, Pallas kernels, shards(): pl.pallas_call(functools.partial(lookup_kernel, cats, rows, bits), out_sh...  4.22 us
    pallas_call x1, Pallas kernels, shards(): pl.pallas_call(functools.partial(final_kernel, mp, hx), out_shape=(f32(1,...  2.93 us

profile of v6, /device:TPU:0, one launch (start us, length us, event | category | flops | bytes accessed | tf_op | source)
XLA Modules:
  0.0 139.3 jit_solution(14067007268235562772)
XLA Ops:
  1.3 29.5 %first.1 = (bf16[1024,256]{1,0:T(8,128)(2,1)}, s32[2,416,128]{2,1,0:T(8,128)}, bf16[512,208]{1,0:T(8,128)(2,1)}, bf16[2448,624]{1,0:T(8,128)(2,1)}, f32[16,896]{...) custom-call(f32[16,8192]{1,0:T(8,128)} %refs_0_.1, bf16[156,2,624]{2,1,0:T(2,128)(2,1)} %bitcast.19, ...), custom_call_target="tpu_custom_call" | custom-call | tf_op jit(solution)/shard_map/first/pallas_call | solution.py:1268
  30.8 0.0 copy-start.10
  30.9 1.0 copy-done.10
  31.9 1.0 copy-done.11
  32.9 0.0 copy-start.4
  32.9 0.0 copy-start.5
  32.9 0.0 copy-start.6
  32.9 0.0 copy-start.7
  33.0 0.0 copy-start.8
  33.0 0.0 copy-start.9
  33.0 4.2 %lookup.1.partial = f32[416,512]{1,0:T(8,128)S(1)} custom-call(s32[2,416,128]{2,1,0:T(8,128)S(1)} %copy-done.11, bf16[1024,256]{1,0:T(8,128)(2,1)S(1)} %copy-done.10), custom_call_target="tpu_custom_call" | custom-call | flops 8000000000 | bytes 2000000 | tf_op jit(solution)/shard_map/lookup/pallas_call | solution.py:1302
  37.2 0.0 copy-done
  37.2 0.0 copy-done.1
  37.2 0.0 copy-done.2
  37.2 0.0 copy-done.3
  37.3 0.0 copy-done.4
  37.3 0.0 copy-done.5
  37.3 0.0 copy-done.6
  37.3 0.0 copy-done.7
  37.3 0.0 copy-done.8
  37.3 52.3 %dense.1 = (f32[1,512]{1,0:T(1,128)S(1)}, bf16[416,512]{1,0:T(8,128)(2,1)S(1)}, bf16[512,624]{1,0:T(8,128)(2,1)S(1)}, bf16[2,512,624]{2,1,0:T(8,128)(2,1)S(1)}, ...) custom-call(f32[416,512]{1,0:T(8,128)S(1)} %lookup.1.partial, ...), custom_call_target="tpu_custom_call" | custom-call | tf_op jit(solution)/shard_map/dense/pallas_call | solution.py:1330
  89.7 5.5 %scatter.1.grads = bf16[1024,256]{1,0:T(8,128)(2,1)S(1)} custom-call(s32[2,416,128]{2,1,0:T(8,128)S(1)} %copy-done.12, bf16[416,512]{1,0:T(8,128)(2,1)S(1)} %get-tuple-element.69.grad), custom_call_target="tpu_custom_call" | custom-call | flops 8000000000 | bytes 2000000 | tf_op jit(solution)/shard_map/scatter/pallas_call | solution.py:1396
  95.2 41.2 %reduce.1 = (bf16[4,128,256]{2,1,0:T(8,128)(2,1)S(1)}, bf16[384,640]{1,0:T(8,128)(2,1)S(1)}, bf16[384,640]{1,0:T(8,128)(2,1)S(1)}, bf16[256,640]{1,0:T(8,128)(2,1)S(1)}, f32[8,256]{1,0:T(8,128)S(1)}) custom-call(bf16[1024,256]{1,0:T(8,128)(2,1)S(1)} %scatter.1.grads, bf16[512,624]{1,0:T(8,128)(2,1)S(1)} %get-tuple-element.70.feat, ...), custom_call_target="tpu_custom_call" | custom-call | tf_op jit(solution)/shard_map/reduce/pallas_call | solution.py:1406
  136.3 2.9 %final.1 = (f32[1,512]{1,0:T(1,128)}, f32[13,16]{1,0:T(8,128)}, f32[16,8192]{1,0:T(8,128)}, f32[156,2,624]{2,1,0:T(2,128)}, f32[2,156]{1,0:T(2,128)}, /*index=5*...) custom-call(bf16[4,128,256]{2,1,0:T(8,128)(2,1)S(1)} %get-tuple-elem, ...), custom_call_target="tpu_custom_call" | custom-call | tf_op jit(solution)/shard_map/final/pallas_call | solution.py:1446
  (8 shorter events, 0.0 us)
Async XLA Ops:
  30.8 1.0 copy-start.10
  31.9 1.0 copy-start.11
  32.9 4.3 %copy-start = (bf16[2448,624]{1,0:T(8,128)(2,1)S(1)}, bf16[2448,624]{1,0:T(8,128)(2,1)}, u32[]{:S(2)}) copy-start(bf16[2448,624]{1,0:T(8,128)(2,1)} %get-tuple-element.65.weights) | copy-start | bytes 9165316
  32.9 4.3 %copy-start.1 = (bf16[4,2,100,800]{3,2,1,0:T(8,128)(2,1)S(1)}, bf16[4,2,100,800]{3,2,1,0:T(8,128)(2,1)}, u32[]{:S(2)}) copy-start(bf16[4,2,100,800]{3,2,1,0:T(8,128)(2,1)} %get-tuple-element.67.b_next) | copy-start | bytes 3840004
  32.9 4.3 %copy-start.2 = (bf16[4,2,100,400]{3,2,1,0:T(8,128)(2,1)S(1)}, bf16[4,2,100,400]{3,2,1,0:T(8,128)(2,1)}, u32[]{:S(2)}) copy-start(bf16[4,2,100,400]{3,2,1,0:T(8,128)(2,1)} %get-tuple-element.66.n_next) | copy-start | bytes 1920004
  32.9 4.3 %copy-start.3 = (bf16[512,208]{1,0:T(8,128)(2,1)S(1)}, bf16[512,208]{1,0:T(8,128)(2,1)}, u32[]{:S(2)}) copy-start(bf16[512,208]{1,0:T(8,128)(2,1)} %get-tuple-element.64.numeric) | copy-start | bytes 638980
  32.9 4.3 %copy-start.4 = (f32[512,13]{0,1:T(8,128)S(1)}, f32[512,13]{0,1:T(8,128)}, u32[]{:S(2)}) copy-start(f32[512,13]{0,1:T(8,128)} %param.20) | copy-start | bytes 79876
  32.9 4.3 %copy-start.5 = (f32[50,8,16]{0,2,1:T(8,128)S(1)}, f32[50,8,16]{0,2,1:T(8,128)}, u32[]{:S(2)}) copy-start(f32[50,8,16]{0,2,1:T(8,128)} %param.38) | copy-start | bytes 76804
  32.9 4.3 %copy-start.6 = (f32[16,896]{1,0:T(8,128)S(1)}, f32[16,896]{1,0:T(8,128)}, u32[]{:S(2)}) copy-start(f32[16,896]{1,0:T(8,128)} %get-tuple-element.68.vec) | copy-start | bytes 172036
  32.9 4.3 %copy-start.7 = (f32[800]{0:T(1024)S(1)}, f32[800]{0:T(1024)}, u32[]{:S(2)}) copy-start(f32[800]{0:T(1024)} %right_hbm.1) | copy-start | bytes 9604
  33.0 4.3 %copy-start.8 = (f32[400]{0:T(512)S(1)}, f32[400]{0:T(512)}, u32[]{:S(2)}) copy-start(f32[400]{0:T(512)} %param.36) | copy-start | bytes 4804
  33.0 4.3 %copy-start.9 = (s32[512]{0:T(512)S(1)}, s32[512]{0:T(512)}, u32[]{:S(2)}) copy-start(s32[512]{0:T(512)} %param.23) | copy-start | bytes 6148
  37.3 52.4 %copy-start.12 = (s32[2,416,128]{2,1,0:T(8,128)S(1)}, s32[2,416,128]{2,1,0:T(8,128)}, u32[]{:S(2)}) copy-start(s32[2,416,128]{2,1,0:T(8,128)} %get-tuple-element.62.keys) | copy-start | bytes 1277956

commit v7 on v6

--- a/solution.py
+++ b/solution.py
@@ -138,6 +138,7 @@
 
 
 WINDOW = 16
+WINDOW_BACK = 12
 
 
 def chunk_parts(key, rows, bits):
@@ -170,26 +171,26 @@
     return jnp.concatenate([key[i : i + 1, :] for i in range(tall)], axis=1)
 
 
-def chunk_span(keys, half, k, cats, rows, bits):
+def chunk_span(keys, half, k, cats, rows, bits, window):
     tall = CHUNK // 128
     most = keys.shape[1] // tall - 1
     key = keys[half, pl.ds(pl.multiple_of(jnp.minimum(k, most) * tall, tall), tall), :]
     cat = over(key & ((1 << bits) - 1), rows)
     first = jnp.min(jnp.where(key >= 0, cat, cats - 1))
     last = jnp.max(jnp.where(key >= 0, cat, 0))
-    return first, (last - first) // WINDOW + 1
-
-
-def each_chunk(keys, half, cats, rows, bits, body):
+    return first, (last - first) // window + 1
+
+
+def each_chunk(keys, half, cats, rows, bits, window, body):
     live = jnp.sum((keys[half] >= 0).astype(jnp.int32))
     chunks = (live + CHUNK - 1) // CHUNK
 
     def step(k, carry):
-        later = chunk_span(keys, half, k + 1, cats, rows, bits)
+        later = chunk_span(keys, half, k + 1, cats, rows, bits, window)
         body(chunk_key(keys, half, k), *carry)
         return later
 
-    lax.fori_loop(0, chunks, step, chunk_span(keys, half, 0, cats, rows, bits))
+    lax.fori_loop(0, chunks, step, chunk_span(keys, half, 0, cats, rows, bits, window))
 
 
 def lookup_kernel(cats, rows, bits, keys, t2, pooled, total):
@@ -228,7 +229,7 @@
 
             lax.fori_loop(1, windows, more, 0)
 
-        each_chunk(keys, half, cats, rows, bits, body)
+        each_chunk(keys, half, cats, rows, bits, WINDOW, body)
         return carry
 
     lax.fori_loop(0, 2, half_table, 0)
@@ -239,7 +240,7 @@
     lows = total.shape[0] // 32
     total[...] = jnp.zeros_like(total)
     grad_pad[: cats * 16, :] = grad[...]
-    grad_pad[cats * 16 :, :] = jnp.zeros((WINDOW * 16, rows), jnp.bfloat16)
+    grad_pad[cats * 16 :, :] = jnp.zeros((WINDOW_BACK * 16, rows), jnp.bfloat16)
 
     def half_table(half, carry):
         def body(key, first, windows):
@@ -250,10 +251,10 @@
             cat = jnp.broadcast_to(jnp.where(key >= 0, cat, -1), (16, CHUNK))
 
             def window(w, g):
-                start = first + w * WINDOW
-                at = pl.ds(pl.multiple_of(start * 16, 16), WINDOW * 16)
+                start = first + w * WINDOW_BACK
+                at = pl.ds(pl.multiple_of(start * 16, 16), WINDOW_BACK * 16)
                 wide = jnp.dot(grad_pad[at, :], place_of, preferred_element_type=jnp.float32)
-                for c in range(WINDOW):
+                for c in range(WINDOW_BACK):
                     g = g + jnp.where(cat == start + c, wide[c * 16 : (c + 1) * 16], 0.0)
                 return g
 
@@ -267,7 +268,7 @@
                     preferred_element_type=jnp.float32,
                 )
 
-        each_chunk(keys, half, cats, rows, bits, body)
+        each_chunk(keys, half, cats, rows, bits, WINDOW_BACK, body)
         return carry
 
     lax.fori_loop(0, 2, half_table, 0)
@@ -679,15 +680,22 @@
     feat[:, :num] = numeric[...]
     started = []
 
+    def flipped(bits):
+        to = me
+        for level in range(dp.bit_length() - 1):
+            if bits >> level & 1:
+                to = flip(to, level)
+        return to
+
     def push(slot, *values):
         width = -(-values[0].shape[1] // 128) * 128
         for r, value in enumerate(values):
             sums[slot, me, r : r + 1, : value.shape[1]] = value
         out = []
-        for step in range(1, dp):
+        for step in range(dp - 1, 0, -1):
             at = sums.at[slot, me, :, pl.ds(0, width)]
             copy = remote(
-                at, at, ssend.at[slot, step - 1], srecv.at[slot, step - 1], {"dp": lax.rem(me + step, dp)}
+                at, at, ssend.at[slot, step - 1], srecv.at[slot, step - 1], {"dp": flipped(step)}
             )
             copy.start()
             out.append(copy)
@@ -732,14 +740,16 @@
     def loop(body, *start):
         return lax.fori_loop(0, steps, lambda i, carry: body(rowset(i), *carry), tuple(start))
 
+    def gated(k, at):
+        x = feat[at, :]
+        value = 2.0 * sigmoid(nt(x, gates[k][...]) + vec[k : k + 1, :wide])
+        gate[k, at, :] = value
+        x = low(x.astype(jnp.float32) * value)
+        fields[k, at, :] = x
+        return x
+
     def gates_and_first(at, a, b):
-        x = feat[at, :]
-        wide_x = x.astype(jnp.float32)
-        for k in range(2):
-            value = 2.0 * sigmoid(nt(x, gates[k][...]) + vec[k : k + 1, :wide])
-            gate[k, at, :] = value
-            fields[k, at, :] = low(wide_x * value)
-        y = nt(fields[0, at, :], n1[...])
+        y = nt(gated(0, at), n1[...])
         yn[0, at, :] = y
         return a + column_sum(y), b + column_sum(y * y)
 
@@ -752,7 +762,7 @@
     sent_n = push(0, a, b)
 
     def broad_first(at, a, b):
-        y = nt(fields[1, at, :], b1[...])
+        y = nt(gated(1, at), b1[...])
         yb[0, at, :] = y
         return a + column_sum(y), b + column_sum(y * y)
 
@@ -849,16 +859,6 @@
     def grad_y(gz, normed, rstd, gain, total):
         return low(gain * rstd * (gz - total[0:1] / batch - normed * (total[1:2] / batch)))
 
-    t_n3 = pull(sent_n)[:, :h1]
-
-    def back_n3(at, a, b):
-        g = grad_y(dn[2, at, :], yn[2, at, :], rstd_n3, gain_n(2)[0], t_n3)
-        gyn[1, at, :] = g
-        gz = nn(g, n23[1]) * dn[1, at, :]
-        dn[1, at, :] = gz
-        return a + column_sum(gz), b + column_sum(gz * yn[1, at, :])
-
-    sent_n = push(7, *loop(back_n3, zero1, zero1))
     main = a_work.shape[1]
     rest = h2 - main
     parts = main // rest
@@ -866,6 +866,22 @@
     short = -(-tall_a // parts)
     a_work[...] = jnp.zeros_like(a_work)
     b_work[...] = jnp.zeros_like(b_work)
+    size_a, size_b = a_work.shape[0], b_work.shape[0]
+    folded = jnp.zeros((16, h1), jnp.float32)
+    col = lax.broadcasted_iota(jnp.int32, (16, h1), 1)
+    for h in range(heads):
+        folded = folded + jnp.where(col // hx == h, pair_g[h * 16 : (h + 1) * 16, :], 0.0)
+    b_work[size_b - 16 :, :h1] = low(folded)
+    t_n3 = pull(sent_n)[:, :h1]
+
+    def back_n3(at, a, b):
+        g = grad_y(dn[2, at, :], yn[2, at, :], rstd_n3, gain_n(2)[0], t_n3)
+        gyn[1, at, :] = g
+        gz = nn(g, n23[1]) * dn[1, at, :]
+        dn[1, at, :] = gz
+        return a + column_sum(gz), b + column_sum(gz * yn[1, at, :])
+
+    sent_n = push(7, *loop(back_n3, zero1, zero1))
     grad_n3 = weight_grad(gyn.at[1], un[1], own_cols, mine, s1, mp)
     t_b2 = pull(sent_b)[:, :h2]
 
@@ -877,6 +893,9 @@
         return a + column_sum(gz), b + column_sum(gz * yb[0, at, :])
 
     sent_b = push(8, *loop(back_b2, zero2, zero2))
+    grad_b2 = weight_grad(gyb, ub[0], own_cols, mine, s2, mp)
+    a_work[:s2, :] = grad_b2[:, :main]
+    spill[:s2, :] = grad_b2[:, main:]
     t_n2 = pull(sent_n)[:, :h1]
 
     def back_n2(at, a, b):
@@ -888,21 +907,12 @@
 
     sent_n = push(9, *loop(back_n2, zero1, zero1))
     grad_n2 = weight_grad(gyn.at[0], un[0], own_cols, mine, s1, mp)
-    grad_b2 = weight_grad(gyb, ub[0], own_cols, mine, s2, mp)
-    a_work[:s2, :] = grad_b2[:, :main]
     a_work[s2:tall_a, :] = jnp.concatenate([grad_n2, grad_n3], axis=1)[:, :main]
-    spill[:s2, :] = grad_b2[:, main:]
     spill[s2:tall_a, :] = jnp.concatenate([grad_n2, grad_n3], axis=1)[:, main:]
     for p in range(parts):
         n = min(short, tall_a - p * short)
         a_work[tall_a : tall_a + n, p * rest : (p + 1) * rest] = spill[p * short : p * short + n, :]
-    size_a, size_b = a_work.shape[0], b_work.shape[0]
     copy_ax, start_a = give_half(me, 0, 0, size_a, a_work, a_land.at[pl.ds(0, size_a // 2), :], hsend.at[0], hrecv.at[0])
-    folded = jnp.zeros((16, h1), jnp.float32)
-    col = lax.broadcasted_iota(jnp.int32, (16, h1), 1)
-    for h in range(heads):
-        folded = folded + jnp.where(col // hx == h, pair_g[h * 16 : (h + 1) * 16, :], 0.0)
-    b_work[size_b - 16 :, :h1] = low(folded)
     t_b1 = pull(sent_b)[:, :h2]
 
     def gate_back(k, at, grad):
@@ -1398,7 +1408,7 @@
         out_shape=b16(dp * tall, HI),
         in_specs=[VM] * 2,
         out_specs=VM,
-        scratch_shapes=[held(dp * tall, HI), held16((cats + WINDOW) * 16, rows)],
+        scratch_shapes=[held(dp * tall, HI), held16((cats + WINDOW_BACK) * 16, rows)],
         compiler_params=params(None, 16),
         cost_estimate=pl.CostEstimate(flops=8 * 10**9, bytes_accessed=2 * 10**6, transcendentals=0),
         name="scatter",

time: 140 us -> 138 us (0.986)
  Pallas kernels: 136 us -> 133 us
    pallas_call x1, Pallas kernels: 41.2 us -> 36.3 us  [shards(): pl.pallas_call(functools.partial(reduce_kernel, dp, mp), out_shape=(b16(m...]
    pallas_call x1, Pallas kernels: 5.49 us -> 7.6 us  [shards(): pl.pallas_call(functools.partial(scatter_kernel, cats, rows, bits), out_s...]
    pallas_call x1, Pallas kernels: 52.3 us -> 50.7 us  [shards(): pl.pallas_call(functools.partial(dense_kernel, dp, mp, hx, float(rows * d...]
    pallas_call x1, Pallas kernels: 4.22 us -> 5.69 us  [shards(): pl.pallas_call(functools.partial(lookup_kernel, cats, rows, bits), out_sh...]
where the time goes in v7:
time: 138 us; the launch traced here: 136 us
  Pallas kernels  133 us (96%)
  local copies, waits for them, and re-layouts  2.1 us (2%)
  between operations  1.55 us (1%)
    pallas_call x1, Pallas kernels, shards(): pl.pallas_call(functools.partial(dense_kernel, dp, mp, hx, float(rows * d...  50.7 us
    pallas_call x1, Pallas kernels, shards(): pl.pallas_call(functools.partial(reduce_kernel, dp, mp), out_shape=(b16(m...  36.3 us
    pallas_call x1, Pallas kernels, shards(): pl.pallas_call(functools.partial(first_kernel, dp, mp, own_rows, bits), o...  29.5 us
    pallas_call x1, Pallas kernels, shards(): pl.pallas_call(functools.partial(scatter_kernel, cats, rows, bits), out_s...  7.6 us
    pallas_call x1, Pallas kernels, shards(): pl.pallas_call(functools.partial(lookup_kernel, cats, rows, bits), out_sh...  5.69 us
    pallas_call x1, Pallas kernels, shards(): pl.pallas_call(functools.partial(final_kernel, mp, hx), out_shape=(f32(1,...  2.93 us

profile of v7, /device:TPU:0, one launch (start us, length us, event | category | flops | bytes accessed | tf_op | source)
XLA Modules:
  0.0 136.4 jit_solution(13449205785985846729)
XLA Ops:
  1.3 29.5 %first.1 = (bf16[1024,256]{1,0:T(8,128)(2,1)}, s32[2,416,128]{2,1,0:T(8,128)}, bf16[512,208]{1,0:T(8,128)(2,1)}, bf16[2448,624]{1,0:T(8,128)(2,1)}, f32[16,896]{...) custom-call(f32[16,8192]{1,0:T(8,128)} %refs_0_.1, bf16[156,2,624]{2,1,0:T(2,128)(2,1)} %bitcast.19, ...), custom_call_target="tpu_custom_call" | custom-call | tf_op jit(solution)/shard_map/first/pallas_call | solution.py:1278
  30.8 0.0 copy-start.10
  30.9 1.0 copy-done.10
  31.9 1.0 copy-done.11
  32.9 0.0 copy-start.4
  32.9 0.0 copy-start.5
  32.9 0.0 copy-start.6
  32.9 0.0 copy-start.7
  33.0 0.0 copy-start.8
  33.0 0.0 copy-start.9
  33.0 5.7 %lookup.1.partial = f32[416,512]{1,0:T(8,128)S(1)} custom-call(s32[2,416,128]{2,1,0:T(8,128)S(1)} %copy-done.11, bf16[1024,256]{1,0:T(8,128)(2,1)S(1)} %copy-done.10), custom_call_target="tpu_custom_call" | custom-call | flops 8000000000 | bytes 2000000 | tf_op jit(solution)/shard_map/lookup/pallas_call | solution.py:1312
  38.7 0.0 copy-done
  38.7 0.0 copy-done.1
  38.7 0.0 copy-done.2
  38.7 0.0 copy-done.3
  38.7 0.0 copy-done.4
  38.7 0.0 copy-done.5
  38.7 0.0 copy-done.6
  38.7 0.0 copy-done.7
  38.8 50.7 %dense.1 = (f32[1,512]{1,0:T(1,128)S(1)}, bf16[416,512]{1,0:T(8,128)(2,1)S(1)}, bf16[512,624]{1,0:T(8,128)(2,1)S(1)}, bf16[2,512,624]{2,1,0:T(8,128)(2,1)S(1)}, ...) custom-call(f32[416,512]{1,0:T(8,128)S(1)} %lookup.1.partial, ...), custom_call_target="tpu_custom_call" | custom-call | tf_op jit(solution)/shard_map/dense/pallas_call | solution.py:1340
  89.5 0.0 copy-done.12
  89.5 7.6 %scatter.1.grads = bf16[1024,256]{1,0:T(8,128)(2,1)S(1)} custom-call(s32[2,416,128]{2,1,0:T(8,128)S(1)} %copy-done.12, bf16[416,512]{1,0:T(8,128)(2,1)S(1)} %get-tuple-element.69.grad), custom_call_target="tpu_custom_call" | custom-call | flops 8000000000 | bytes 2000000 | tf_op jit(solution)/shard_map/scatter/pallas_call | solution.py:1406
  97.1 36.3 %reduce.1 = (bf16[4,128,256]{2,1,0:T(8,128)(2,1)S(1)}, bf16[384,640]{1,0:T(8,128)(2,1)S(1)}, bf16[384,640]{1,0:T(8,128)(2,1)S(1)}, bf16[256,640]{1,0:T(8,128)(2,1)S(1)}, f32[8,256]{1,0:T(8,128)S(1)}) custom-call(bf16[1024,256]{1,0:T(8,128)(2,1)S(1)} %scatter.1.grads, bf16[512,624]{1,0:T(8,128)(2,1)S(1)} %get-tuple-element.70.feat, ...), custom_call_target="tpu_custom_call" | custom-call | tf_op jit(solution)/shard_map/reduce/pallas_call | solution.py:1416
  133.4 2.9 %final.1 = (f32[1,512]{1,0:T(1,128)}, f32[13,16]{1,0:T(8,128)}, f32[16,8192]{1,0:T(8,128)}, f32[156,2,624]{2,1,0:T(2,128)}, f32[2,156]{1,0:T(2,128)}, /*index=5*...) custom-call(bf16[4,128,256]{2,1,0:T(8,128)(2,1)S(1)} %get-tuple-elem, ...), custom_call_target="tpu_custom_call" | custom-call | tf_op jit(solution)/shard_map/final/pallas_call | solution.py:1456
  (8 shorter events, 0.0 us)
Async XLA Ops:
  30.8 1.0 copy-start.10
  31.9 1.0 copy-start.11
  32.9 5.8 %copy-start = (bf16[2448,624]{1,0:T(8,128)(2,1)S(1)}, bf16[2448,624]{1,0:T(8,128)(2,1)}, u32[]{:S(2)}) copy-start(bf16[2448,624]{1,0:T(8,128)(2,1)} %get-tuple-element.65.weights) | copy-start | bytes 9165316
  32.9 5.8 %copy-start.1 = (bf16[4,2,100,800]{3,2,1,0:T(8,128)(2,1)S(1)}, bf16[4,2,100,800]{3,2,1,0:T(8,128)(2,1)}, u32[]{:S(2)}) copy-start(bf16[4,2,100,800]{3,2,1,0:T(8,128)(2,1)} %get-tuple-element.67.b_next) | copy-start | bytes 3840004
  32.9 5.8 %copy-start.2 = (bf16[4,2,100,400]{3,2,1,0:T(8,128)(2,1)S(1)}, bf16[4,2,100,400]{3,2,1,0:T(8,128)(2,1)}, u32[]{:S(2)}) copy-start(bf16[4,2,100,400]{3,2,1,0:T(8,128)(2,1)} %get-tuple-element.66.n_next) | copy-start | bytes 1920004
  32.9 5.8 %copy-start.3 = (bf16[512,208]{1,0:T(8,128)(2,1)S(1)}, bf16[512,208]{1,0:T(8,128)(2,1)}, u32[]{:S(2)}) copy-start(bf16[512,208]{1,0:T(8,128)(2,1)} %get-tuple-element.64.numeric) | copy-start | bytes 638980
  32.9 5.8 %copy-start.4 = (f32[512,13]{0,1:T(8,128)S(1)}, f32[512,13]{0,1:T(8,128)}, u32[]{:S(2)}) copy-start(f32[512,13]{0,1:T(8,128)} %param.20) | copy-start | bytes 79876
  32.9 5.8 %copy-start.5 = (f32[50,8,16]{0,2,1:T(8,128)S(1)}, f32[50,8,16]{0,2,1:T(8,128)}, u32[]{:S(2)}) copy-start(f32[50,8,16]{0,2,1:T(8,128)} %param.38) | copy-start | bytes 76804
  32.9 5.8 %copy-start.6 = (f32[16,896]{1,0:T(8,128)S(1)}, f32[16,896]{1,0:T(8,128)}, u32[]{:S(2)}) copy-start(f32[16,896]{1,0:T(8,128)} %get-tuple-element.68.vec) | copy-start | bytes 172036
  32.9 5.8 %copy-start.7 = (f32[800]{0:T(1024)S(1)}, f32[800]{0:T(1024)}, u32[]{:S(2)}) copy-start(f32[800]{0:T(1024)} %right_hbm.1) | copy-start | bytes 9604
  33.0 5.8 %copy-start.8 = (f32[400]{0:T(512)S(1)}, f32[400]{0:T(512)}, u32[]{:S(2)}) copy-start(f32[400]{0:T(512)} %param.36) | copy-start | bytes 4804
  33.0 5.8 %copy-start.9 = (s32[512]{0:T(512)S(1)}, s32[512]{0:T(512)}, u32[]{:S(2)}) copy-start(s32[512]{0:T(512)} %param.23) | copy-start | bytes 6148
  38.8 50.8 %copy-start.12 = (s32[2,416,128]{2,1,0:T(8,128)S(1)}, s32[2,416,128]{2,1,0:T(8,128)}, u32[]{:S(2)}) copy-start(s32[2,416,128]{2,1,0:T(8,128)} %get-tuple-element.62.keys) | copy-start | bytes 1277956

commit v8 on v7

--- a/solution.py
+++ b/solution.py
@@ -1147,12 +1147,23 @@
         copy.wait_send()
 
 
-def final_kernel(
-    mp, hx, shares, a_full, b_full, c_full, small, logits_in, n_gain_in, n_shift_in, b_gain_in, b_shift_in,
-    left_in, right_in, bias_in,
-    logits, num_g, table_g, gate_g, gate_bias_g, n_first_g, n_rest_g, n_gain_g, n_shift_g,
-    b_first_g, b_rest_g, b_gain_g, b_shift_g, left_g, right_g, pair_g, bias_g,
-):
+def final_kernel(mp, hx, *refs):
+    (
+        shares, a_full, b_full, c_full, small, logits_in, n_gain_in, n_shift_in, b_gain_in, b_shift_in,
+        left_in, right_in, bias_in,
+    ) = refs[:13]
+    results, places, sem = refs[13:30], refs[30:47], refs[47]
+    (
+        logits, num_g, table_g, gate_g, gate_bias_g, n_first_g, n_rest_g, n_gain_g, n_shift_g,
+        b_first_g, b_rest_g, b_gain_g, b_shift_g, left_g, right_g, pair_g, bias_g,
+    ) = places
+    leaving = {}
+
+    def leave(*which):
+        for i in which:
+            leaving[i] = pltpu.make_async_copy(places[i], results[i], sem.at[i])
+            leaving[i].start()
+
     gcols, s1, s2, h1 = gate_g.shape[0], n_first_g.shape[0], b_first_g.shape[0], n_rest_g.shape[2]
     wide = n_first_g.shape[1]
 
@@ -1165,10 +1176,13 @@
             table_g[:, (m * blocks + b) * HI : (m * blocks + b + 1) * HI] = shares[
                 m, b * 16 : (b + 1) * 16, :
             ].astype(jnp.float32)
+    leave(2)
     gate_g[:, 0, :] = full(c_full, 0, gcols, 0, wide)
     gate_g[:, 1, :] = full(b_full, s2, gcols, 0, wide)
+    leave(3)
     n_first_g[...] = full(c_full, gcols, s1, 0, wide)
     b_first_g[...] = full(b_full, 0, s2, 0, wide)
+    leave(5, 9)
     main = a_full.shape[1]
     rest = 2 * h1 - main
     parts = main // rest
@@ -1183,9 +1197,11 @@
     )
     b_rest_g[:, :main] = full(a_full, 0, s2, 0, main)
     b_rest_g[:, main:] = tail[:s2]
+    leave(10)
     both = jnp.concatenate([full(a_full, s2, s1, 0, main), tail[s2:]], axis=1)
     n_rest_g[:, 0, :] = both[:, :h1]
     n_rest_g[:, 1, :] = both[:, h1:]
+    leave(6)
     heads = pair_g.shape[2]
     pairs = b_full[b_full.shape[0] - 16 :, :h1]
     row = lax.broadcasted_iota(jnp.int32, (h1, heads), 0)
@@ -1211,6 +1227,9 @@
     left_g[...] = left_in[...]
     right_g[...] = right_in[...].reshape(right_g.shape)
     bias_g[...] = bias_in[...]
+    leave(*[i for i in range(17) if i not in leaving])
+    for copy in leaving.values():
+        copy.wait()
 
 
 def f32(*shape):
@@ -1453,29 +1472,31 @@
         compiler_params=params(2, 24),
         name="reduce",
     )(row_sums, feat, fields, grad_gate, gyn1, a_part, b_part, small)
+    final_shapes = (
+        f32(1, rows),
+        f32(*num_embed.shape),
+        f32(width, own_rows),
+        f32(gcols, 2, wide),
+        f32(2, gcols),
+        f32(s1, wide),
+        f32(s1, 2, h1),
+        f32(3, s1),
+        f32(3, s1),
+        f32(s2, wide),
+        f32(s2, h2),
+        f32(2, s2),
+        f32(2, s2),
+        f32(1, h1),
+        f32(h2),
+        f32(hx, width, joining_pair.shape[0]),
+        f32(1, 1),
+    )
     outs = pl.pallas_call(
         functools.partial(final_kernel, mp, hx),
-        out_shape=(
-            f32(1, rows),
-            f32(*num_embed.shape),
-            f32(width, own_rows),
-            f32(gcols, 2, wide),
-            f32(2, gcols),
-            f32(s1, wide),
-            f32(s1, 2, h1),
-            f32(3, s1),
-            f32(3, s1),
-            f32(s2, wide),
-            f32(s2, h2),
-            f32(2, s2),
-            f32(2, s2),
-            f32(1, h1),
-            f32(h2),
-            f32(hx, width, joining_pair.shape[0]),
-            f32(1, 1),
-        ),
+        out_shape=final_shapes,
         in_specs=[VM] * 13,
-        out_specs=(VM,) * 17,
+        out_specs=(ANY,) * 17,
+        scratch_shapes=[pltpu.VMEM(x.shape, x.dtype) for x in final_shapes] + [dma(17)],
         compiler_params=params(None, 16),
         name="final",
     )(

time: 138 us -> 138 us (level)
    pallas_call x1, Pallas kernels: 36.3 us -> 39 us  [shards(): pl.pallas_call(functools.partial(reduce_kernel, dp, mp), out_shape=(b16(m...]
    pallas_call x1, Pallas kernels: 7.6 us -> 5.81 us  [shards(): pl.pallas_call(functools.partial(scatter_kernel, cats, rows, bits), out_s...]
    pallas_call x1, Pallas kernels: 50.7 us -> 52.4 us  [shards(): pl.pallas_call(functools.partial(dense_kernel, dp, mp, hx, float(rows * d...]
    pallas_call x1, Pallas kernels: 5.69 us -> 4.22 us  [shards(): pl.pallas_call(functools.partial(lookup_kernel, cats, rows, bits), out_sh...]
where the time goes in v8:
time: 138 us
  Pallas kernels  134 us (97%)
  local copies, waits for them, and re-layouts  2.1 us (2%)
  between operations  1.68 us (1%)
    pallas_call x1, Pallas kernels, shards(): pl.pallas_call(functools.partial(dense_kernel, dp, mp, hx, float(rows * d...  52.4 us
    pallas_call x1, Pallas kernels, shards(): pl.pallas_call(functools.partial(reduce_kernel, dp, mp), out_shape=(b16(m...  39 us
    pallas_call x1, Pallas kernels, shards(): pl.pallas_call(functools.partial(first_kernel, dp, mp, own_rows, bits), o...  29.5 us
    pallas_call x1, Pallas kernels, shards(): pl.pallas_call(functools.partial(scatter_kernel, cats, rows, bits), out_s...  5.81 us
    pallas_call x1, Pallas kernels, shards(): pl.pallas_call(functools.partial(lookup_kernel, cats, rows, bits), out_sh...  4.22 us
    pallas_call x1, Pallas kernels, shards(): pl.pallas_call(functools.partial(final_kernel, mp, hx), out_shape=final_s...  2.9 us

profile of v8, /device:TPU:0, one launch (start us, length us, event | category | flops | bytes accessed | tf_op | source)
XLA Modules:
  0.0 137.6 jit_solution(18177365128942875787)
XLA Ops:
  1.3 29.5 %first.1 = (bf16[1024,256]{1,0:T(8,128)(2,1)}, s32[2,416,128]{2,1,0:T(8,128)}, bf16[512,208]{1,0:T(8,128)(2,1)}, bf16[2448,624]{1,0:T(8,128)(2,1)}, f32[16,896]{...) custom-call(f32[16,8192]{1,0:T(8,128)} %refs_0_.1, bf16[156,2,624]{2,1,0:T(2,128)(2,1)} %bitcast.19, ...), custom_call_target="tpu_custom_call" | custom-call | tf_op jit(solution)/shard_map/first/pallas_call | solution.py:1297
  30.8 0.0 copy-start.10
  30.9 1.0 copy-done.10
  31.9 1.0 copy-done.11
  32.9 0.0 copy-start.4
  32.9 0.0 copy-start.5
  32.9 0.0 copy-start.6
  32.9 0.0 copy-start.7
  33.0 0.0 copy-start.8
  33.0 0.0 copy-start.9
  33.0 4.2 %lookup.1.partial = f32[416,512]{1,0:T(8,128)S(1)} custom-call(s32[2,416,128]{2,1,0:T(8,128)S(1)} %copy-done.11, bf16[1024,256]{1,0:T(8,128)(2,1)S(1)} %copy-done.10), custom_call_target="tpu_custom_call" | custom-call | flops 8000000000 | bytes 2000000 | tf_op jit(solution)/shard_map/lookup/pallas_call | solution.py:1331
  37.2 0.0 copy-done
  37.2 0.0 copy-done.1
  37.2 0.0 copy-done.2
  37.2 0.0 copy-done.3
  37.3 0.0 copy-done.4
  37.3 0.0 copy-done.5
  37.3 0.0 copy-done.6
  37.3 0.0 copy-done.7
  37.3 52.4 %dense.1 = (f32[1,512]{1,0:T(1,128)S(1)}, bf16[416,512]{1,0:T(8,128)(2,1)S(1)}, bf16[512,624]{1,0:T(8,128)(2,1)S(1)}, bf16[2,512,624]{2,1,0:T(8,128)(2,1)S(1)}, ...) custom-call(f32[416,512]{1,0:T(8,128)S(1)} %lookup.1.partial, ...), custom_call_target="tpu_custom_call" | custom-call | tf_op jit(solution)/shard_map/dense/pallas_call | solution.py:1359
  89.7 0.0 copy-done.12
  89.7 5.8 %scatter.1.grads = bf16[1024,256]{1,0:T(8,128)(2,1)S(1)} custom-call(s32[2,416,128]{2,1,0:T(8,128)S(1)} %copy-done.12, bf16[416,512]{1,0:T(8,128)(2,1)S(1)} %get-tuple-element.69.grad), custom_call_target="tpu_custom_call" | custom-call | flops 8000000000 | bytes 2000000 | tf_op jit(solution)/shard_map/scatter/pallas_call | solution.py:1425
  95.5 39.0 %reduce.1 = (bf16[4,128,256]{2,1,0:T(8,128)(2,1)S(1)}, bf16[384,640]{1,0:T(8,128)(2,1)S(1)}, bf16[384,640]{1,0:T(8,128)(2,1)S(1)}, bf16[256,640]{1,0:T(8,128)(2,1)S(1)}, f32[8,256]{1,0:T(8,128)S(1)}) custom-call(bf16[1024,256]{1,0:T(8,128)(2,1)S(1)} %scatter.1.grads, bf16[512,624]{1,0:T(8,128)(2,1)S(1)} %get-tuple-element.70.feat, ...), custom_call_target="tpu_custom_call" | custom-call | tf_op jit(solution)/shard_map/reduce/pallas_call | solution.py:1435
  134.6 2.9 %final.1 = (f32[1,512]{1,0:T(1,128)}, f32[13,16]{1,0:T(8,128)}, f32[16,8192]{1,0:T(8,128)}, f32[156,2,624]{2,1,0:T(2,128)}, f32[2,156]{1,0:T(2,128)}, /*index=5*...) custom-call(bf16[4,128,256]{2,1,0:T(8,128)(2,1)S(1)} %get-tuple-elem, ...), custom_call_target="tpu_custom_call" | custom-call | tf_op jit(solution)/shard_map/final/pallas_call | solution.py:1494
  (8 shorter events, 0.0 us)
Async XLA Ops:
  30.8 1.0 copy-start.10
  31.9 1.0 copy-start.11
  32.9 4.3 %copy-start = (bf16[2448,624]{1,0:T(8,128)(2,1)S(1)}, bf16[2448,624]{1,0:T(8,128)(2,1)}, u32[]{:S(2)}) copy-start(bf16[2448,624]{1,0:T(8,128)(2,1)} %get-tuple-element.65.weights) | copy-start | bytes 9165316
  32.9 4.3 %copy-start.1 = (bf16[4,2,100,800]{3,2,1,0:T(8,128)(2,1)S(1)}, bf16[4,2,100,800]{3,2,1,0:T(8,128)(2,1)}, u32[]{:S(2)}) copy-start(bf16[4,2,100,800]{3,2,1,0:T(8,128)(2,1)} %get-tuple-element.67.b_next) | copy-start | bytes 3840004
  32.9 4.3 %copy-start.2 = (bf16[4,2,100,400]{3,2,1,0:T(8,128)(2,1)S(1)}, bf16[4,2,100,400]{3,2,1,0:T(8,128)(2,1)}, u32[]{:S(2)}) copy-start(bf16[4,2,100,400]{3,2,1,0:T(8,128)(2,1)} %get-tuple-element.66.n_next) | copy-start | bytes 1920004
  32.9 4.3 %copy-start.3 = (bf16[512,208]{1,0:T(8,128)(2,1)S(1)}, bf16[512,208]{1,0:T(8,128)(2,1)}, u32[]{:S(2)}) copy-start(bf16[512,208]{1,0:T(8,128)(2,1)} %get-tuple-element.64.numeric) | copy-start | bytes 638980
  32.9 4.3 %copy-start.4 = (f32[512,13]{0,1:T(8,128)S(1)}, f32[512,13]{0,1:T(8,128)}, u32[]{:S(2)}) copy-start(f32[512,13]{0,1:T(8,128)} %param.20) | copy-start | bytes 79876
  32.9 4.3 %copy-start.5 = (f32[50,8,16]{0,2,1:T(8,128)S(1)}, f32[50,8,16]{0,2,1:T(8,128)}, u32[]{:S(2)}) copy-start(f32[50,8,16]{0,2,1:T(8,128)} %param.38) | copy-start | bytes 76804
  32.9 4.3 %copy-start.6 = (f32[16,896]{1,0:T(8,128)S(1)}, f32[16,896]{1,0:T(8,128)}, u32[]{:S(2)}) copy-start(f32[16,896]{1,0:T(8,128)} %get-tuple-element.68.vec) | copy-start | bytes 172036
  32.9 4.3 %copy-start.7 = (f32[800]{0:T(1024)S(1)}, f32[800]{0:T(1024)}, u32[]{:S(2)}) copy-start(f32[800]{0:T(1024)} %right_hbm.1) | copy-start | bytes 9604
  33.0 4.3 %copy-start.8 = (f32[400]{0:T(512)S(1)}, f32[400]{0:T(512)}, u32[]{:S(2)}) copy-start(f32[400]{0:T(512)} %param.36) | copy-start | bytes 4804
  33.0 4.3 %copy-start.9 = (s32[512]{0:T(512)S(1)}, s32[512]{0:T(512)}, u32[]{:S(2)}) copy-start(s32[512]{0:T(512)} %param.23) | copy-start | bytes 6148
  37.3 52.4 %copy-start.12 = (s32[2,416,128]{2,1,0:T(8,128)S(1)}, s32[2,416,128]{2,1,0:T(8,128)}, u32[]{:S(2)}) copy-start(s32[2,416,128]{2,1,0:T(8,128)} %get-tuple-element.62.keys) | copy-start | bytes 1277956
